TPU v7x, 32 devices: a whole 2x2x4 slice. The times are simulated.
32 devices in a mesh: ctx: 8 (over y, x, core), head: 4 (over z).
Axes of the slice: x: 2, y: 2, z: 4, core: 2. Of those that a mesh axis runs over, the one named last changes fastest.
Arguments:
- queries: bfloat16 [4096, 4096], P('ctx', 'head'), may hold values from -150 to 150
- cached_keys: bfloat16 [4096, 2048], P('ctx', 'head'), may hold values from -6 to 6
- values: bfloat16 [4096, 2048], P('ctx', 'head'), may hold values from -6 to 6
- patch_keys: bfloat16 [4096, 2048], P('ctx', 'head'), may hold values from -6 to 6
- out_grad: bfloat16 [4096, 5376], P('ctx', 'head'), may hold values from -6 to 6
- out_weight: bfloat16 [4096, 5376], P('head'), may hold values from -0.09375 to 0.09375
- knocked: int32 [16], P('head'), may hold values 0 or 1
- patch_start: int32 [16], P('head'), may hold values from 0 to 4095
Outputs:
- query_grad: bfloat16 [4096, 4096], P('ctx', 'head')
- key_grad: bfloat16 [4096, 2048], P('ctx', 'head')
- value_grad: bfloat16 [4096, 2048], P('ctx', 'head')
- patch_grad: bfloat16 [4096, 2048], P('ctx', 'head')
- weight_grad: float32 [4096, 5376], P(('head', 'ctx'))
All inputs are finite; a program needn't handle non-finite values. No bound on the sum of `knocked` on one device may be relied on, other than what follows from the above.
Results may differ from a plain program's by a relative error of at most 0.0058.
Values may be sent and summed in bfloat16 or wider, within the bound.
No kernel may reach another device: no remote copies, remote signals or barrier semaphores. Data moves between devices by JAX's collectives and lax.ppermute only.
A program may use at most 128 MiB of HBM per device.

v0:
```python
import functools

import jax
import jax.numpy as jnp
from jax import lax
from jax.experimental import pallas as pl
from jax.experimental.pallas import tpu as pltpu
from jax.sharding import PartitionSpec as P

LOGIT_SCALE = 168.0 ** (-0.5)
EXP2_SCALE = LOGIT_SCALE * 1.4426950408889634
TILE = 256
VMEM_LIMIT = 48 * 1024 * 1024
CHEAP = pl.CostEstimate(flops=1, bytes_accessed=1, transcendentals=0)

NT = (((1,), (1,)), ((), ()))
NN = (((1,), (0,)), ((), ()))


def dot(a, b, dims=NN):
    return lax.dot_general(a, b, dims, preferred_element_type=jnp.float32)


def stack_heads(pair, head_size):
    return jnp.concatenate([pair[:, :head_size], pair[:, head_size:]], axis=0)


def forward_kernel(chip_ref, q_ref, k_ref, v_ref, pk_ref, pv_ref, p_ref, at_ref, keys, values_t):
    tile = pl.program_id(1)
    rows, head_size = k_ref.shape
    blocks = rows // TILE

    @pl.when(tile == 0)
    def _():
        keys[:rows] = pk_ref[...]
        keys[rows:] = k_ref[...]
        values_t[:, :rows] = pv_ref[...].T
        values_t[:, rows:] = v_ref[...].T

    q = stack_heads(q_ref[...], head_size)
    key_id = lax.broadcasted_iota(jnp.int32, (TILE, 2 * TILE), 0)
    query_id = lax.broadcasted_iota(jnp.int32, (TILE, 2 * TILE), 1) & (TILE - 1)
    first = chip_ref[0] == 0
    top = None
    for b in range(blocks + 1):
        start = pl.multiple_of((tile + b) * TILE, TILE)
        s = dot(keys[pl.ds(start, TILE), :], q, NT)
        if b == 0:
            s = jnp.where(key_id > query_id, s, -jnp.inf)
        if b == blocks:
            s = jnp.where(key_id <= query_id, s, -jnp.inf)
        else:
            s = s + jnp.where(jnp.logical_and(first, tile + b < blocks), -jnp.inf, 0.0)
        p_ref[0, 0, b * TILE : (b + 1) * TILE, :] = s
        here = jnp.max(s, axis=0, keepdims=True)
        top = here if top is None else jnp.maximum(top, here)
    total = None
    for b in range(blocks + 1):
        part = pl.ds(b * TILE, TILE)
        e = jnp.exp2((p_ref[0, 0, part, :] - top) * EXP2_SCALE)
        p_ref[0, 0, part, :] = e
        here = jnp.sum(e, axis=0, keepdims=True)
        total = here if total is None else total + here
    inverse = 1.0 / total
    out = None
    for b in range(blocks + 1):
        part = pl.ds(b * TILE, TILE)
        start = pl.multiple_of((tile + b) * TILE, TILE)
        p = p_ref[0, 0, part, :] * inverse
        p_ref[0, 0, part, :] = p
        term = dot(values_t[:, pl.ds(start, TILE)], p.astype(jnp.bfloat16))
        out = term if out is None else out + term
    at_ref[:head_size] = out[:, :TILE].astype(jnp.bfloat16)
    at_ref[head_size:] = out[:, TILE:].astype(jnp.bfloat16)


def forward(chip, packet, before, head_size):
    rows = packet.shape[0]
    groups = packet.shape[1] // (4 * head_size)
    tiles = rows // TILE
    span = rows + TILE
    grid_spec = pltpu.PrefetchScalarGridSpec(
        num_scalar_prefetch=1,
        grid=(groups, tiles),
        in_specs=[
            pl.BlockSpec((TILE, 2 * head_size), lambda g, i, c: (i, g)),
            pl.BlockSpec((rows, head_size), lambda g, i, c: (0, 2 * groups + g)),
            pl.BlockSpec((rows, head_size), lambda g, i, c: (0, 3 * groups + g)),
            pl.BlockSpec((rows, head_size), lambda g, i, c: (0, g)),
            pl.BlockSpec((rows, head_size), lambda g, i, c: (0, groups + g)),
        ],
        out_specs=[
            pl.BlockSpec((1, 1, span, 2 * TILE), lambda g, i, c: (g, i, 0, 0)),
            pl.BlockSpec((2 * head_size, TILE), lambda g, i, c: (g, i)),
        ],
        scratch_shapes=[
            pltpu.VMEM((2 * rows, head_size), jnp.bfloat16),
            pltpu.VMEM((head_size, 2 * rows), jnp.bfloat16),
        ],
    )
    return pl.pallas_call(
        forward_kernel,
        grid_spec=grid_spec,
        out_shape=[
            jax.ShapeDtypeStruct((groups, tiles, span, 2 * TILE), jnp.float32),
            jax.ShapeDtypeStruct((groups * 2 * head_size, rows), jnp.bfloat16),
        ],
        compiler_params=pltpu.CompilerParams(vmem_limit_bytes=VMEM_LIMIT),
        cost_estimate=CHEAP,
        name="attention_forward",
    )(chip, packet, packet, packet, before, before)


def backward_kernel(
    phase, q_ref, k_ref, v_ref, pk_ref, pv_ref, p_ref, do_ref, carry_ref, dq_ref, dprev_ref, keep_ref, keys_t, values, dk, dv, dp
):
    tile = pl.program_id(1)
    rows, head_size = k_ref.shape
    blocks = rows // TILE
    half = rows // 2
    old = rows - phase * half

    @pl.when(tile == 0)
    def _():
        keys_t[:, :old] = pk_ref[rows - old :, :].T
        keys_t[:, old:] = k_ref[: half + rows - old, :].T
        values[:old] = pv_ref[rows - old :, :]
        values[old:] = v_ref[: half + rows - old, :]
        if phase == 0:
            dk[...] = jnp.zeros_like(dk)
            dv[...] = jnp.zeros_like(dv)
        else:
            dk[:rows] = carry_ref[0, 0]
            dv[:rows] = carry_ref[1, 0]
            dk[rows:] = jnp.zeros((half, head_size), jnp.float32)
            dv[rows:] = jnp.zeros((half, head_size), jnp.float32)

    q = stack_heads(q_ref[...], head_size)
    do = jnp.concatenate([do_ref[:head_size], do_ref[head_size:]], axis=1)
    centre = None
    for b in range(blocks + 1):
        start = pl.multiple_of((tile + b) * TILE, TILE)
        part = pl.ds(b * TILE, TILE)
        p = p_ref[0, 0, part, :]
        grad = dot(values[pl.ds(start, TILE), :], do)
        dp[part, :] = grad
        here = jnp.sum(p * grad, axis=0, keepdims=True)
        centre = here if centre is None else centre + here
        dv[pl.ds(start, TILE), :] += dot(p.astype(jnp.bfloat16), do, NT)
    out = None
    for b in range(blocks + 1):
        start = pl.multiple_of((tile + b) * TILE, TILE)
        part = pl.ds(b * TILE, TILE)
        ds = (p_ref[0, 0, part, :] * (dp[part, :] - centre)).astype(jnp.bfloat16)
        dk[pl.ds(start, TILE), :] += dot(ds, q)
        term = dot(keys_t[:, pl.ds(start, TILE)], ds)
        out = term if out is None else out + term
    out = out * LOGIT_SCALE
    dq_ref[:, :head_size] = out[:, :TILE].T.astype(jnp.bfloat16)
    dq_ref[:, head_size:] = out[:, TILE:].T.astype(jnp.bfloat16)

    @pl.when(tile == pl.num_programs(1) - 1)
    def _():
        dprev_ref[0, 0] = (dk[:half] * LOGIT_SCALE).astype(jnp.bfloat16)
        dprev_ref[1, 0] = dv[:half].astype(jnp.bfloat16)
        keep_ref[0, 0] = dk[half:]
        keep_ref[1, 0] = dv[half:]


def backward(phase, members, packet, before, attention, out_grads, carry, head_size):
    rows = packet.shape[0]
    groups = packet.shape[1] // (4 * head_size)
    g0, count = members
    tiles = rows // TILE // 2
    half = rows // 2
    span = rows + TILE
    first = phase * tiles
    if carry is None:
        carry = jnp.zeros((2, 1, 8, head_size), jnp.float32)
        carry_spec = pl.BlockSpec((2, 1, 8, head_size), lambda g, i: (0, 0, 0, 0))
    else:
        carry_spec = pl.BlockSpec((2, 1, rows, head_size), lambda g, i: (0, g0 + g, 0, 0))
    return pl.pallas_call(
        functools.partial(backward_kernel, phase),
        grid=(count, tiles),
        in_specs=[
            pl.BlockSpec((TILE, 2 * head_size), lambda g, i: (first + i, g0 + g)),
            pl.BlockSpec((rows, head_size), lambda g, i: (0, 2 * groups + g0 + g)),
            pl.BlockSpec((rows, head_size), lambda g, i: (0, 3 * groups + g0 + g)),
            pl.BlockSpec((rows, head_size), lambda g, i: (0, g0 + g)),
            pl.BlockSpec((rows, head_size), lambda g, i: (0, groups + g0 + g)),
            pl.BlockSpec((1, 1, span, 2 * TILE), lambda g, i: (g0 + g, first + i, 0, 0)),
            pl.BlockSpec((2 * head_size, TILE), lambda g, i: (g0 + g, i)),
            carry_spec,
        ],
        out_specs=[
            pl.BlockSpec((TILE, 2 * head_size), lambda g, i: (i, g)),
            pl.BlockSpec((2, 1, half, head_size), lambda g, i: (0, g, 0, 0)),
            pl.BlockSpec((2, 1, rows, head_size), lambda g, i: (0, g, 0, 0)),
        ],
        out_shape=[
            jax.ShapeDtypeStruct((half, count * 2 * head_size), jnp.bfloat16),
            jax.ShapeDtypeStruct((2, count, half, head_size), jnp.bfloat16),
            jax.ShapeDtypeStruct((2, count, rows, head_size), jnp.float32),
        ],
        scratch_shapes=[
            pltpu.VMEM((head_size, rows + half), jnp.bfloat16),
            pltpu.VMEM((rows + half, head_size), jnp.bfloat16),
            pltpu.VMEM((rows + half, head_size), jnp.float32),
            pltpu.VMEM((rows + half, head_size), jnp.float32),
            pltpu.VMEM((span, 2 * TILE), jnp.float32),
        ],
        compiler_params=pltpu.CompilerParams(vmem_limit_bytes=VMEM_LIMIT),
        cost_estimate=CHEAP,
        name="attention_backward",
    )(packet, packet, packet, before, before, attention, out_grads, carry)


def grads_kernel(block_ref, weight_ref, *refs):
    total = dot(weight_ref[...], block_ref[0])
    if len(refs) == 2:
        total = total + refs[0][...]
    refs[-1][...] = total.astype(refs[-1].dtype)


def add_grads(block, weight, total, at, dtype):
    parts, cols, tok = block.shape
    width = weight.shape[0]
    tiles = tok // TILE
    return pl.pallas_call(
        grads_kernel,
        grid=(parts * tiles,),
        in_specs=[
            pl.BlockSpec((1, cols, TILE), lambda i: (i // tiles, 0, i % tiles)),
            pl.BlockSpec((width, cols), lambda i: (0, 0)),
        ]
        + ([] if total is None else [pl.BlockSpec((width, TILE), lambda i: (0, at // TILE + i))]),
        out_specs=pl.BlockSpec((width, TILE), lambda i: (0, i)),
        out_shape=jax.ShapeDtypeStruct((width, parts * tok), dtype),
        compiler_params=pltpu.CompilerParams(vmem_limit_bytes=VMEM_LIMIT),
        name="out_grads",
    )(block, weight, *([] if total is None else [total]))


def terms_kernel(count, rows_ref, *refs):
    blocks, outs = refs[: len(refs) - count], refs[len(refs) - count :]
    share = rows_ref.shape[0] // count
    term, at = None, 0
    for block in blocks:
        for part in range(block.shape[0]):
            width = block.shape[2]
            piece = dot(rows_ref[:, at : at + width], block[part], NT)
            term = piece if term is None else term + piece
            at += width
    for s in range(count):
        outs[s][...] = term[s * share : (s + 1) * share].astype(outs[s].dtype)


def make_terms(rows, blocks, count, chunk):
    cols = blocks[0].shape[1]
    share = rows.shape[0] // count
    return pl.pallas_call(
        functools.partial(terms_kernel, count),
        grid=(cols // chunk,),
        in_specs=[pl.BlockSpec(rows.shape, lambda i: (0, 0))]
        + [pl.BlockSpec((block.shape[0], chunk, block.shape[2]), lambda i: (0, i, 0)) for block in blocks],
        out_specs=[pl.BlockSpec((share, chunk), lambda i: (0, i))] * count,
        out_shape=[jax.ShapeDtypeStruct((share, cols), jnp.float32 if s == 0 else jnp.bfloat16) for s in range(count)],
        compiler_params=pltpu.CompilerParams(vmem_limit_bytes=VMEM_LIMIT),
        name="weight_terms",
    )(rows, *blocks)


def shift(shard, by):
    size = lax.axis_size("ctx")
    return lax.ppermute(shard, "ctx", [(i, i + by) for i in range(size) if 0 <= i + by < size])


def swap_cores(shard, only=None):
    size = lax.axis_size("ctx")
    return lax.ppermute(shard, "ctx", [(i, i ^ 1) for i in range(size) if only is None or i % 2 == only])


def gather_chip(block):
    n_ctx, n_head = lax.axis_size("ctx"), lax.axis_size("head")
    groups = [[c * n_head + i for i in range(2 * n_head)] for c in range(0, n_ctx, 2)]
    whole = lax.all_gather(block, ("ctx", "head"), axis=0, axis_index_groups=groups)
    return whole.reshape(2, n_head * block.shape[0], block.shape[1])


def after(values, *others):
    return lax.optimization_barrier((values, *others))[0]


def body(queries, cached_keys, values, patch_keys, out_grad, out_weight, knocked, patch_start):
    tok = queries.shape[0]
    kv_local = knocked.shape[0]
    head_size = cached_keys.shape[1] // kv_local
    cols = out_grad.shape[1]
    out_grad = out_grad.T
    n_head, n_ctx = lax.axis_size("head"), lax.axis_size("ctx")
    chips = n_ctx // 2
    place, z = lax.axis_index("ctx"), lax.axis_index("head")
    core, chip = place % 2, place // 2
    low = core == 0
    half_q, half_kv = queries.shape[1] // 2, cached_keys.shape[1] // 2
    dyn = lax.dynamic_slice_in_dim

    positions = place * tok + jnp.arange(tok, dtype=jnp.int32)
    chosen = (jnp.repeat(knocked, head_size)[None, :] == 1) & (
        positions[:, None] >= jnp.repeat(patch_start, head_size)[None, :]
    )
    patched = jnp.where(chosen, patch_keys, cached_keys)

    def packet_of(which):
        return jnp.concatenate(
            [
                dyn(queries, which * half_q, half_q, 1),
                dyn(patched, which * half_kv, half_kv, 1),
                dyn(values, which * half_kv, half_kv, 1),
            ],
            axis=1,
        )

    mine, other = packet_of(core), swap_cores(packet_of(1 - core))
    packet = jnp.concatenate([jnp.where(low, mine, other), jnp.where(low, other, mine)], axis=0)
    before = shift(packet[:, half_q:], 2)

    cut = 2 * cols // 3
    quarter = tok // 2
    first = gather_chip(out_grad[:cut])
    rest = out_grad[cut:]
    passed = swap_cores(jnp.where(low, rest[:, quarter:], rest[:, :quarter]))
    second = gather_chip(jnp.where(low, rest[:, :quarter], passed))
    third = gather_chip(jnp.where(low, passed, rest[:, quarter:]))

    weight_half = dyn(out_weight, core * half_q, half_q, 0).reshape(half_q, n_head, cols)
    first_weight = weight_half[:, :, :cut].reshape(half_q, n_head * cut)
    rest_weight = weight_half[:, :, cut:].reshape(half_q, n_head * (cols - cut))
    before = after(before, first_weight, rest_weight)

    attention, attended = forward(chip[None].astype(jnp.int32), packet, before, head_size)
    share = out_weight.shape[0] // n_ctx
    parity = attended.reshape(chips // 2, 2, share, 2 * tok)
    kept, given = dyn(parity, core, 1, 1)[:, 0], dyn(parity, 1 - core, 1, 1)[:, 0]
    taken = swap_cores(given)
    by_chip = jnp.concatenate([jnp.where(low, kept, taken), jnp.where(low, taken, kept)], axis=0)
    by_distance = jnp.concatenate([dyn(by_chip, chip ^ s, 1, 0) for s in range(chips)], axis=0)
    by_distance = by_distance.reshape(chips * share, 2 * tok)

    def send_terms(blocks, chunk):
        kept_term, *sent = make_terms(by_distance, blocks, chips, chunk)
        got = [lax.ppermute(x, "ctx", [(i, i ^ (2 * s + 2)) for i in range(n_ctx)]) for s, x in enumerate(sent)]
        return kept_term, sent, got

    first_terms = send_terms([first], 2 * TILE)
    grads = add_grads(first, first_weight, None, 0, jnp.float32)
    grads, _ = lax.optimization_barrier((grads, first_terms[1]))
    all_groups = (0, packet.shape[1] // (4 * head_size))
    grads_low = add_grads(second, rest_weight, grads, 0, jnp.bfloat16)
    query_low, prev_low, carry = backward(0, all_groups, packet, before, attention, grads_low, None, head_size)
    from_low = shift(prev_low, -2)

    third, query_low, first_terms = lax.optimization_barrier((third, query_low, first_terms))
    last_terms = send_terms([second, third], TILE)
    grads_high = add_grads(third, rest_weight, grads, tok, jnp.bfloat16)
    grads_high = after(grads_high, last_terms[1])
    parts = []
    for g in range(all_groups[1]):
        if g == all_groups[1] - 1:
            grads_high, from_low = lax.optimization_barrier((grads_high, from_low))
        parts.append(backward(1, (g, 1), packet, before, attention, grads_high, carry, head_size))
    from_high = jnp.concatenate([shift(part[1], -2) for part in parts], axis=1)
    query_high = jnp.concatenate([part[0] for part in parts], axis=1)
    own = jnp.concatenate([part[2] for part in parts], axis=1)

    sums = [functools.reduce(jnp.add, t[2], t[0]).reshape(share, n_head, -1) for t in (first_terms, last_terms)]
    weight_grad = jnp.concatenate(sums, axis=2).reshape(share, -1)

    query_kept = jnp.where(low, query_low, query_high)
    query_taken = jnp.where(low, swap_cores(query_low, 1), swap_cores(query_high, 0))
    query_grad = jnp.concatenate(
        [jnp.where(low, query_kept, query_taken), jnp.where(low, query_taken, query_kept)], axis=1
    )

    scale = jnp.array([LOGIT_SCALE, 1.0], jnp.float32)[:, None, None, None]
    sums_low = scale * own[:, :, :tok] + from_low
    sums_high = scale * own[:, :, tok:] + from_high
    sums_kept = jnp.where(low, sums_low, sums_high)
    sums_taken = swap_cores(jnp.where(low, sums_high, sums_low).astype(jnp.bfloat16)).astype(jnp.float32)
    sums = jnp.concatenate(
        [jnp.where(low, sums_kept, sums_taken), jnp.where(low, sums_taken, sums_kept)], axis=1
    )
    key_sums, value_sums = [jnp.concatenate([part[h] for h in range(kv_local)], axis=1) for part in (sums[0], sums[1])]
    key_grad = jnp.where(chosen, jnp.float32(0.0), key_sums).astype(jnp.bfloat16)
    patch_grad = jnp.where(chosen, key_sums, jnp.float32(0.0)).astype(jnp.bfloat16)
    value_grad = value_sums.astype(jnp.bfloat16)
    return (query_grad, key_grad, value_grad, patch_grad, weight_grad)


def solution(mesh):
    split = P("ctx", "head")
    return jax.shard_map(
        body,
        mesh=mesh,
        in_specs=(split, split, split, split, split, P("head", None), P("head"), P("head")),
        out_specs=(split, split, split, split, P(("head", "ctx"), None)),
        check_vma=False,
    )
```

profile of v0, /device:TPU:0, one launch (start us, length us, event | category | flops | bytes accessed | tf_op | source)
XLA Modules:
  0.0 215.8 jit_solution(10480032059842038390)
XLA Ops:
  7.2 2.4 %slice.105 = bf16[896,512]{1,0:T(8,128)(2,1)} slice(bf16[1344,512]{1,0:T(8,128)(2,1)} %bitcast.55), slice={[0:896], [0:512]} | slice | bytes 1835008 | tf_op jit(solution)/shard_map/slice | solution.py:331
  14.6 2.3 %collective-permute-done.1 = bf16[512,1024]{1,0:T(8,128)(2,1)S(1)} collective-permute-done((bf16[512,1024]{1,0:T(8,128)(2,1)S(1)}, bf16[512,1024]{1,0:T(8,128)(2,1)S(1)}, u32[]{:S(2)}, u32[]{:S(2)}) %collective-permute-start.1) | collective-permute-done | bytes 1048608 | tf_op jit(solution)/shard_map/ppermute | solution.py:281
  17.9 1.9 broadcast_select_fusion.1
  20.8 4.8 %collective-permute-start.2 = (bf16[1024,512]{1,0:T(8,128)(2,1)}, bf16[1024,512]{1,0:T(8,128)(2,1)S(1)}, u32[]{:S(2)}, u32[]{:S(2)}) collective-permute-start(bf16[1024,512]{1,0:T(8,128)(2,1)} %fusion), channel_id=1, source_target_pairs={{0,8},{4,12},{8,16},{12,20},{16,24},{20,28},{1,9},{5,13},{9,17},{1... | collective-permute-start | bytes 3145736 | tf_op jit(solution)/shard_map/ppermute | solution.py:276
  25.7 5.4 %constant_dynamic-slice_fusion = bf16[512,5376]{1,0:T(8,128)(2,1)} fusion(bf16[1024,5376]{1,0:T(8,128)(2,1)} %param.14, s32[]{:T(128)S(6)} %select_n.142), kind=kLoop, calls=%fused_computation.62 | loop fusion | bytes 11010052 | tf_op jit(solution)/shard_map/dynamic_slice | solution.py:337
  31.1 8.3 %copy.23 = bf16[512,5376]{0,1:T(8,128)(2,1)} copy(bf16[512,5376]{1,0:T(8,128)(2,1)} %constant_dynamic-slice_fusion) | data formatting | bytes 11010048
  39.4 4.2 %slice.103 = bf16[512,4,896]{0,2,1:T(8,128)(2,1)} slice(bf16[512,4,1344]{0,2,1:T(8,128)(2,1)} %bitcast.48), slice={[0:512], [0:4], [0:896]} | slice | bytes 7340032 | tf_op jit(solution)/shard_map/slice | solution.py:338
  43.6 2.8 %slice.104 = bf16[512,4,448]{0,2,1:T(8,128)(2,1)} slice(bf16[512,4,1344]{0,2,1:T(8,128)(2,1)} %bitcast.49), slice={[0:512], [0:4], [896:1344]} | slice | bytes 3670016 | tf_op jit(solution)/shard_map/slice | solution.py:339
  46.4 6.0 %copy.21.weight_ref = bf16[512,3584]{1,0:T(8,128)(2,1)} copy(bf16[512,3584]{0,1:T(8,128)(2,1)} %bitcast.50) | data formatting | bytes 7340032 | tf_op jit(solution)/shard_map/reshape | solution.py:338
  52.6 15.0 %attention_forward.1 = (f32[2,4,1280,512]{3,2,1,0:T(8,128)}, bf16[512,1024]{1,0:T(8,128)(2,1)S(1)}) custom-call(s32[1]{0:T(128)} %bitcast.7.chip_ref, bf16[1024,1024]{1,0:T(8,128)(2,1)S(1)} %pad_maximum_fusion.1.q_ref.k_ref.v_ref, bf16[1024,1024]{1,0:T(8,128)(2,1)S(1)} %pad_maximum_fusion.1.q_ref.k_ref.v_ref, ...), custom_call_target="tpu_custom_call" | custom-call | flops 1 | bytes 1 | tf_op jit(solution)/shard_map/attention_forward/pallas_call | solution.py:101
  67.7 1.9 collective-permute-done.3
  70.2 15.7 %all-gather.11.cloned.1.call-done = bf16[7168,512]{1,0:T(8,128)(2,1)} async-done(((bf16[896,512]{1,0:T(8,128)(2,1)}), bf16[7168,512]{1,0:T(8,128)(2,1)}) %all-gather.11.cloned.1.call-update) | async-done | bytes 7340048 | tf_op jit(solution)/shard_map/all_gather | solution.py:287
  85.9 9.2 %weight_terms.2 = (f32[128,3584]{1,0:T(8,128)S(1)}, bf16[128,3584]{1,0:T(8,128)(2,1)}, bf16[128,3584]{1,0:T(8,128)(2,1)}, bf16[128,3584]{1,0:T(8,128)(2,1)}) custom-call(bf16[512,1024]{1,0:T(8,128)(2,1)S(1)} %bitcast.38, bf16[2,3584,512]{2,1,0:T(8,128)(2,1)} %bitcast.46), custom_call_target="tpu_custom_call" | custom-call | tf_op jit(solution)/shard_map/weight_terms/pallas_call | solution.py:262
  99.9 2.8 %copy.16.weight_ref = bf16[512,1792]{1,0:T(8,128)(2,1)S(1)} copy(bf16[512,1792]{0,1:T(8,128)(2,1)} %bitcast.52) | data formatting | bytes 3670016 | tf_op jit(solution)/shard_map/reshape | solution.py:339
  102.7 2.1 copy-done.5
  104.7 6.6 %out_grads.3.refs_0_ = f32[512,1024]{1,0:T(8,128)S(1)} custom-call(bf16[2,3584,512]{2,1,0:T(8,128)(2,1)} %bitcast.47, bf16[512,3584]{1,0:T(8,128)(2,1)S(1)} %copy-done.5), custom_call_target="tpu_custom_call" | custom-call | tf_op jit(solution)/shard_map/out_grads/pallas_call | solution.py:230
  115.1 2.4 %out_grads.4.do_ref = bf16[512,512]{1,0:T(8,128)(2,1)S(1)} custom-call(bf16[2,1792,256]{2,1,0:T(8,128)(2,1)S(1)} %bitcast.40, bf16[512,1792]{1,0:T(8,128)(2,1)S(1)} %copy.16.weight_ref, f32[512,1024]{1,0:T(8,128)} %copy-done.4), custom_call_target="tpu_custom_call" | custom-call | tf_op jit(solution)/shard_map/out_grads/pallas_call | solution.py:230
  117.5 11.1 %attention_backward.3 = (bf16[512,512]{1,0:T(8,128)(2,1)S(1)}, bf16[2,2,512,128]{3,2,1,0:T(8,128)(2,1)}, f32[2,2,1024,128]{3,2,1,0:T(8,128)S(1)}) custom-call(bf16[1024,1024]{1,0:T(8,128)(2,1)} %copy-done.2, bf16[1024,1024]{1,0:T(8,128)(2,1)} %copy-done.2, bf16[1024,1024]{1,0:T(8,128)(2,1)} %copy-done.2, ...), custom_call_target="tpu_custom_call" | custom-call | flops 1 | bytes 1 | tf_op jit(solution)/shard_map/attention_backward/pallas_call | solution.py:183
  131.5 10.9 %all-gather.7.cloned.1.call-done = bf16[3584,256]{1,0:T(8,128)(2,1)} async-done(((bf16[448,256]{1,0:T(8,128)(2,1)}), bf16[3584,256]{1,0:T(8,128)(2,1)}) %all-gather.7.cloned.1.call-update) | async-done | bytes 1835024 | tf_op jit(solution)/shard_map/all_gather | solution.py:287
  143.9 2.5 %out_grads.5.do_ref = bf16[512,512]{1,0:T(8,128)(2,1)S(1)} custom-call(bf16[2,1792,256]{2,1,0:T(8,128)(2,1)S(1)} %bitcast.43, bf16[512,1792]{1,0:T(8,128)(2,1)S(1)} %copy.16.weight_ref, f32[512,1024]{1,0:T(8,128)} %copy-done.4), custom_call_target="tpu_custom_call" | custom-call | tf_op jit(solution)/shard_map/out_grads/pallas_call | solution.py:230
  146.5 6.9 %weight_terms.3 = (f32[128,1792]{1,0:T(8,128)S(1)}, bf16[128,1792]{1,0:T(8,128)(2,1)}, bf16[128,1792]{1,0:T(8,128)(2,1)}, bf16[128,1792]{1,0:T(8,128)(2,1)}) custom-call(bf16[512,1024]{1,0:T(8,128)(2,1)S(1)} %bitcast.39, bf16[2,1792,256]{2,1,0:T(8,128)(2,1)S(1)} %bitcast.41, bf16[2,1792,256]{2,1,0:T(8,128)(2,1)} %bitcast.42), custom_call_target="tpu_custom_call" | custom-call | tf_op jit(solution)/shard_map/weight_terms/pallas_call | solution.py:262
  153.3 2.4 %collective-permute-start.15 = (bf16[128,1792]{1,0:T(8,128)(2,1)}, bf16[128,1792]{1,0:T(8,128)(2,1)}, u32[]{:S(2)}, u32[]{:S(2)}) collective-permute-start(bf16[128,1792]{1,0:T(8,128)(2,1)} %get-tuple-element.48), channel_id=1, source_target_pairs={{0,24},{4,28},{8,16},{12,20},{16,8},{20,12},{24,0},{28,4},{1,25},{... | collective-permute-start | bytes 1376264 | tf_op jit(solution)/shard_map/ppermute | solution.py:353
  156.8 6.7 %attention_backward.4 = (bf16[512,256]{1,0:T(8,128)(2,1)S(1)}, bf16[2,1,512,128]{3,2,1,0:T(8,128)(2,1)}, f32[2,1,1024,128]{3,2,1,0:T(8,128)S(1)}) custom-call(bf16[1024,1024]{1,0:T(8,128)(2,1)S(1)} %copy-done.3, bf16[1024,1024]{1,0:T(8,128)(2,1)S(1)} %copy-done.3, bf16[1024,1024]{1,0:T(8,128)(2,1)S(1)} %copy-done.3, ...), custom_call_target="tpu_custom_call" | custom-call | flops 1 | bytes 1 | tf_op jit(solution)/shard_map/attention_backward/pallas_call | solution.py:183
  163.6 6.7 %attention_backward.5 = (bf16[512,256]{1,0:T(8,128)(2,1)S(1)}, bf16[2,1,512,128]{3,2,1,0:T(8,128)(2,1)}, f32[2,1,1024,128]{3,2,1,0:T(8,128)S(1)}) custom-call(bf16[1024,1024]{1,0:T(8,128)(2,1)S(1)} %copy-done.3, bf16[1024,1024]{1,0:T(8,128)(2,1)S(1)} %copy-done.3, bf16[1024,1024]{1,0:T(8,128)(2,1)S(1)} %copy-done.3, ...), custom_call_target="tpu_custom_call" | custom-call | flops 1 | bytes 1 | tf_op jit(solution)/shard_map/attention_backward/pallas_call | solution.py:183
  173.9 3.4 %convert_add_fusion = f32[128,3584]{1,0:T(8,128)} fusion(bf16[128,3584]{1,0:T(8,128)(2,1)} %collective-permute-done.6, bf16[128,3584]{1,0:T(8,128)(2,1)} %collective-permute-done.5, f32[128,3584]{1,0:T(8,128)S(1)} %copy-done.13, bf16[128,3584]{1,0:T(8,128)(2,1)} %collective-permute-done.4), kind=kLoop, calls=%fused_computation.4 | loop fusion | flops 2752512 | bytes 6422528 | tf_op jit(solution)/shard_map/add | solution.py:377
  178.8 2.7 %copy.22 = f32[128,3584]{0,1:T(8,128)} copy(f32[128,3584]{1,0:T(8,128)} %convert_add_fusion) | data formatting | bytes 3670016 | tf_op jit(solution)/shard_map/reshape | solution.py:377
  184.6 3.6 %collective-permute-done.10 = bf16[2,1,512,128]{3,2,1,0:T(8,128)(2,1)S(1)} collective-permute-done((bf16[2,1,512,128]{3,2,1,0:T(8,128)(2,1)}, bf16[2,1,512,128]{3,2,1,0:T(8,128)(2,1)S(1)}, u32[]{:S(2)}, u32[]{:S(2)}) %collective-permute-start.10) | collective-permute-done | bytes 262176 | tf_op jit(solution)/shard_map/ppermute | solution.py:276
  188.2 2.1 collective-permute-start.9
  190.3 2.9 %select_convert_fusion.2 = bf16[2,2,512,128]{3,2,1,0:T(8,128)(2,1)} fusion(bf16[2,2,512,128]{3,2,1,0:T(8,128)(2,1)} %collective-permute-done.7, f32[2,2,1024,128]{3,2,1,0:T(8,128)} %constant_dynamic-update-slice_fusion.2, f32[2]{0:T(128)S(1)} %copy-done.26, pred[]{:T(512)S(6)} %eq.20, bf16[2,1,512,128]{3,2,1,0:T(8,128)(2,1)S(1)} %collective-permute-done.11, ...), kind=kLoop, calls=%fused_computation.27 | loop fusion | flops 2359296 | bytes 3670025 | tf_op jit(solution)/shard_map/convert_element_type | solution.py:390
  196.6 2.9 %pad_maximum_fusion = f32[128,4,1344]{0,2,1:T(8,128)} fusion(f32[128,4,448]{0,2,1:T(8,128)} %bitcast.54, f32[128,4,896]{0,2,1:T(8,128)S(1)} %bitcast.53), kind=kLoop, calls=%fused_computation | loop fusion | flops 688128 | bytes 5505024 | tf_op jit(solution)/shard_map/concatenate | solution.py:378
  199.5 3.3 %copy.20 = f32[128,5376]{1,0:T(8,128)} copy(f32[128,5376]{0,1:T(8,128)} %bitcast.51) | data formatting | bytes 5505024
  205.3 1.7 convert_select_fusion.1
  (117 shorter events, 38.1 us)
Async XLA Ops:
  7.2 5.4 %copy-start = (s32[4]{0:T(128)S(1)}, s32[4]{0:T(128)}, u32[]{:S(2)}) copy-start(s32[4]{0:T(128)} %param.16) | copy-start | bytes 52
  7.2 78.7 %all-gather.11.cloned.1.call-start = ((), (), s32[]{:S(2)}) async-start(), calls=%async_computation.2 | async-start | bytes 8257536 | tf_op jit(solution)/shard_map/all_gather | solution.py:287
  7.2 5.1 %copy-start.18 = (bf16[512,1024]{1,0:T(8,128)(2,1)S(1)}, bf16[512,1024]{1,0:T(8,128)(2,1)}, u32[]{:S(2)}) copy-start(bf16[512,1024]{1,0:T(8,128)(2,1)} %param.9) | copy-start | bytes 3145732
  9.6 104.0 %all-gather.9.cloned.1.call-start = ((), (), s32[]{:S(2)}) async-start(), calls=%async_computation.1 | async-start | bytes 2064384 | tf_op jit(solution)/shard_map/all_gather | solution.py:287
  9.7 2.8 %copy-start.27 = (s32[4]{0:T(128)S(1)}, s32[4]{0:T(128)}, u32[]{:S(2)}) copy-start(s32[4]{0:T(128)} %param.15) | copy-start | bytes 52
  9.7 2.9 %copy-start.23 = (bf16[512,512]{1,0:T(8,128)(2,1)S(1)}, bf16[512,512]{1,0:T(8,128)(2,1)}, u32[]{:S(2)}) copy-start(bf16[512,512]{1,0:T(8,128)(2,1)} %param.12) | copy-start | bytes 1572868
  9.7 2.9 %copy-start.24 = (bf16[512,512]{1,0:T(8,128)(2,1)S(1)}, bf16[512,512]{1,0:T(8,128)(2,1)}, u32[]{:S(2)}) copy-start(bf16[512,512]{1,0:T(8,128)(2,1)} %param.10) | copy-start | bytes 1572868
  9.8 1.6 collective-permute-start
  12.3 130.1 %all-gather.7.cloned.1.call-start = ((), (), s32[]{:S(2)}) async-start(), calls=%async_computation | async-start | bytes 2064384 | tf_op jit(solution)/shard_map/all_gather | solution.py:287
  14.2 2.7 %collective-permute-start.1 = (bf16[512,1024]{1,0:T(8,128)(2,1)S(1)}, bf16[512,1024]{1,0:T(8,128)(2,1)S(1)}, u32[]{:S(2)}, u32[]{:S(2)}) collective-permute-start(bf16[512,1024]{1,0:T(8,128)(2,1)S(1)} %pad_maximum_fusion.3), channel_id=1, source_target_pairs={{0,4},{4,0},{8,12},{12,8},{16,20},{20,16},{24,28},{28,24},{1,5},{5... | collective-permute-start | bytes 3145736 | tf_op jit(solution)/shard_map/ppermute | solution.py:281
  20.8 31.7 %collective-permute-start.2 = (bf16[1024,512]{1,0:T(8,128)(2,1)}, bf16[1024,512]{1,0:T(8,128)(2,1)S(1)}, u32[]{:S(2)}, u32[]{:S(2)}) collective-permute-start(bf16[1024,512]{1,0:T(8,128)(2,1)} %fusion), channel_id=1, source_target_pairs={{0,8},{4,12},{8,16},{12,20},{16,24},{20,28},{1,9},{5,13},{9,17},{1... | collective-permute-start | bytes 3145736 | tf_op jit(solution)/shard_map/ppermute | solution.py:276
  52.6 15.0 %copy-start.2 = (bf16[1024,1024]{1,0:T(8,128)(2,1)}, bf16[1024,1024]{1,0:T(8,128)(2,1)S(1)}, u32[]{:S(2)}) copy-start(bf16[1024,1024]{1,0:T(8,128)(2,1)S(1)} %pad_maximum_fusion.1.q_ref.k_ref.v_ref) | copy-start | bytes 6291460
  67.6 2.0 collective-permute-start.3
  70.2 24.9 %copy-start.6 = (bf16[4,128,1024]{2,1,0:T(8,128)(2,1)}, bf16[4,128,1024]{2,1,0:T(8,128)(2,1)S(1)}, u32[]{:S(2)}) copy-start(bf16[4,128,1024]{2,1,0:T(8,128)(2,1)S(1)} %pad_maximum_fusion.4) | copy-start | bytes 3145732
  96.4 46.0 %collective-permute-start.4 = (bf16[128,3584]{1,0:T(8,128)(2,1)}, bf16[128,3584]{1,0:T(8,128)(2,1)}, u32[]{:S(2)}, u32[]{:S(2)}) collective-permute-start(bf16[128,3584]{1,0:T(8,128)(2,1)} %get-tuple-element.38), channel_id=1, source_target_pairs={{0,8},{4,12},{8,0},{12,4},{16,24},{20,28},{24,16},{28,20},{1,9},{5... | collective-permute-start | bytes 2752520 | tf_op jit(solution)/shard_map/ppermute | solution.py:353
  97.9 44.5 %collective-permute-start.5 = (bf16[128,3584]{1,0:T(8,128)(2,1)}, bf16[128,3584]{1,0:T(8,128)(2,1)}, u32[]{:S(2)}, u32[]{:S(2)}) collective-permute-start(bf16[128,3584]{1,0:T(8,128)(2,1)} %get-tuple-element.39), channel_id=1, source_target_pairs={{0,16},{4,20},{8,24},{12,28},{16,0},{20,4},{24,8},{28,12},{1,17},{... | collective-permute-start | bytes 2752520 | tf_op jit(solution)/shard_map/ppermute | solution.py:353
  99.3 43.0 %collective-permute-start.6 = (bf16[128,3584]{1,0:T(8,128)(2,1)}, bf16[128,3584]{1,0:T(8,128)(2,1)}, u32[]{:S(2)}, u32[]{:S(2)}) collective-permute-start(bf16[128,3584]{1,0:T(8,128)(2,1)} %get-tuple-element.40), channel_id=1, source_target_pairs={{0,24},{4,28},{8,16},{12,20},{16,8},{20,12},{24,0},{28,4},{1,25},{... | collective-permute-start | bytes 2752520 | tf_op jit(solution)/shard_map/ppermute | solution.py:353
  130.0 33.5 %collective-permute-start.7 = (bf16[2,2,512,128]{3,2,1,0:T(8,128)(2,1)}, bf16[2,2,512,128]{3,2,1,0:T(8,128)(2,1)}, u32[]{:S(2)}, u32[]{:S(2)}) collective-permute-start(bf16[2,2,512,128]{3,2,1,0:T(8,128)(2,1)} %get-tuple-element.52), channel_id=1, source_target_pairs={{8,0},{12,4},{16,8},{20,12},{24,16},{28,20},{9,1},{13,5},{17,9},{2... | collective-permute-start | bytes 1572872 | tf_op jit(solution)/shard_map/ppermute | solution.py:276
  143.9 2.6 %copy-start.10 = (bf16[3584,256]{1,0:T(8,128)(2,1)S(1)}, bf16[3584,256]{1,0:T(8,128)(2,1)}, u32[]{:S(2)}) copy-start(bf16[3584,256]{1,0:T(8,128)(2,1)} %all-gather.9.cloned.1.call-done) | copy-start | bytes 5505028
  146.4 10.4 %copy-start.3 = (bf16[1024,1024]{1,0:T(8,128)(2,1)S(1)}, bf16[1024,1024]{1,0:T(8,128)(2,1)}, u32[]{:S(2)}) copy-start(bf16[1024,1024]{1,0:T(8,128)(2,1)} %copy-done.2) | copy-start | bytes 6291460
  153.3 39.9 %collective-permute-start.15 = (bf16[128,1792]{1,0:T(8,128)(2,1)}, bf16[128,1792]{1,0:T(8,128)(2,1)}, u32[]{:S(2)}, u32[]{:S(2)}) collective-permute-start(bf16[128,1792]{1,0:T(8,128)(2,1)} %get-tuple-element.48), channel_id=1, source_target_pairs={{0,24},{4,28},{8,16},{12,20},{16,8},{20,12},{24,0},{28,4},{1,25},{... | collective-permute-start | bytes 1376264 | tf_op jit(solution)/shard_map/ppermute | solution.py:353
  155.7 37.5 %collective-permute-start.14 = (bf16[128,1792]{1,0:T(8,128)(2,1)}, bf16[128,1792]{1,0:T(8,128)(2,1)}, u32[]{:S(2)}, u32[]{:S(2)}) collective-permute-start(bf16[128,1792]{1,0:T(8,128)(2,1)} %get-tuple-element.47), channel_id=1, source_target_pairs={{0,16},{4,20},{8,24},{12,28},{16,0},{20,4},{24,8},{28,12},{1,17},{... | collective-permute-start | bytes 1376264 | tf_op jit(solution)/shard_map/ppermute | solution.py:353
  156.2 37.0 %collective-permute-start.13 = (bf16[128,1792]{1,0:T(8,128)(2,1)}, bf16[128,1792]{1,0:T(8,128)(2,1)}, u32[]{:S(2)}, u32[]{:S(2)}) collective-permute-start(bf16[128,1792]{1,0:T(8,128)(2,1)} %get-tuple-element.46), channel_id=1, source_target_pairs={{0,8},{4,12},{8,0},{12,4},{16,24},{20,28},{24,16},{28,20},{1,9},{5... | collective-permute-start | bytes 1376264 | tf_op jit(solution)/shard_map/ppermute | solution.py:353
  170.3 3.6 %copy-start.13 = (f32[128,3584]{1,0:T(8,128)S(1)}, f32[128,3584]{1,0:T(8,128)}, u32[]{:S(2)}) copy-start(f32[128,3584]{1,0:T(8,128)} %copy-done.12) | copy-start | bytes 5505028
  171.3 12.0 %collective-permute-start.11 = (bf16[2,1,512,128]{3,2,1,0:T(8,128)(2,1)}, bf16[2,1,512,128]{3,2,1,0:T(8,128)(2,1)S(1)}, u32[]{:S(2)}, u32[]{:S(2)}) collective-permute-start(bf16[2,1,512,128]{3,2,1,0:T(8,128)(2,1)} %get-tuple-element.59), channel_id=1, source_target_pairs={{8,0},{12,4},{16,8},{20,12},{24,16},{28,20},{9,1},{13,5},{17,9},{2... | collective-permute-start | bytes 786440 | tf_op jit(solution)/shard_map/ppermute | solution.py:276
  172.6 15.6 %collective-permute-start.10 = (bf16[2,1,512,128]{3,2,1,0:T(8,128)(2,1)}, bf16[2,1,512,128]{3,2,1,0:T(8,128)(2,1)S(1)}, u32[]{:S(2)}, u32[]{:S(2)}) collective-permute-start(bf16[2,1,512,128]{3,2,1,0:T(8,128)(2,1)} %get-tuple-element.58), channel_id=1, source_target_pairs={{8,0},{12,4},{16,8},{20,12},{24,16},{28,20},{9,1},{13,5},{17,9},{2... | collective-permute-start | bytes 786440 | tf_op jit(solution)/shard_map/ppermute | solution.py:276
  178.8 11.6 %copy-start.26 = (f32[2]{0:T(128)S(1)}, f32[2]{0:T(128)}, u32[]{:S(2)}) copy-start(f32[2]{0:T(128)} %constant.49.clone) | copy-start | bytes 28
  183.3 9.9 %copy-start.19 = (bf16[2,1,512,128]{3,2,1,0:T(8,128)(2,1)}, bf16[2,1,512,128]{3,2,1,0:T(8,128)(2,1)S(1)}, u32[]{:S(2)}) copy-start(bf16[2,1,512,128]{3,2,1,0:T(8,128)(2,1)S(1)} %collective-permute-done.11) | copy-start | bytes 786436
  183.3 19.5 %collective-permute-start.8 = (bf16[512,512]{1,0:T(8,128)(2,1)S(1)}, bf16[512,512]{1,0:T(8,128)(2,1)}, u32[]{:S(2)}, u32[]{:S(2)}) collective-permute-start(bf16[512,512]{1,0:T(8,128)(2,1)S(1)} %get-tuple-element.44), channel_id=1, source_target_pairs={{4,0},{12,8},{20,16},{28,24},{5,1},{13,9},{21,17},{29,25},{6,2},{1... | collective-permute-start | bytes 1572872 | tf_op jit(solution)/shard_map/ppermute | solution.py:281
  188.2 5.0 %copy-start.21 = (bf16[2,1,512,128]{3,2,1,0:T(8,128)(2,1)}, bf16[2,1,512,128]{3,2,1,0:T(8,128)(2,1)S(1)}, u32[]{:S(2)}) copy-start(bf16[2,1,512,128]{3,2,1,0:T(8,128)(2,1)S(1)} %collective-permute-done.10) | copy-start | bytes 786436
  188.2 14.6 %collective-permute-start.9 = (bf16[512,512]{1,0:T(8,128)(2,1)}, bf16[512,512]{1,0:T(8,128)(2,1)}, u32[]{:S(2)}, u32[]{:S(2)}) collective-permute-start(bf16[512,512]{1,0:T(8,128)(2,1)} %constant_dynamic-update-slice_fusion), channel_id=1, source_target_pairs={{0,4},{8,12},{16,20},{24,28},{1,5},{9,13},{17,21},{25,29},{2,6},{1... | collective-permute-start | bytes 1572872 | tf_op jit(solution)/shard_map/ppermute | solution.py:281
  193.2 12.1 %collective-permute-start.12 = (bf16[2,2,512,128]{3,2,1,0:T(8,128)(2,1)}, bf16[2,2,512,128]{3,2,1,0:T(8,128)(2,1)}, u32[]{:S(2)}, u32[]{:S(2)}) collective-permute-start(bf16[2,2,512,128]{3,2,1,0:T(8,128)(2,1)} %select_convert_fusion.2), channel_id=1, source_target_pairs={{0,4},{4,0},{8,12},{12,8},{16,20},{20,16},{24,28},{28,24},{1,5},{5... | collective-permute-start | bytes 1572872 | tf_op jit(solution)/shard_map/ppermute | solution.py:281
  (15 other events, 27.8 us)
Sparse Core Ops, SparseCore 0:
  9.8 76.0 all-gather.10
  88.0 25.5 all-gather.8
  115.8 26.5 all-gather.6
where the time goes:
time: 218 us; the launch traced here: 216 us
  Pallas kernels  67.1 us (31%)
  local copies, waits for them, and re-layouts  54.8 us (25%)
  waiting for transfers between devices  37.2 us (17%)
  other arithmetic  22 us (10%)
  starting transfers between devices  20.4 us (9%)
  between operations  14.3 us (7%)
    all_gather x3, waiting for transfers between devices, gather_chip(): lax.all_gather(block, ('ctx', 'head'), axis=0, axis_index_groups=groups)  27.5 us
    pallas_call x3, Pallas kernels, backward(): pl.pallas_call(functools.partial(backward_kernel, phase), grid=(count, ti...  24.6 us
    unnamed x60, local copies, waits for them, and re-layouts  24.4 us
    pallas_call x2, Pallas kernels, make_terms(): pl.pallas_call(functools.partial(terms_kernel, count), grid=(cols // chun...  16.1 us
    pallas_call x1, Pallas kernels, forward(): pl.pallas_call(forward_kernel, grid_spec=grid_spec, out_shape=[jax.ShapeD...  15 us
    pallas_call x3, Pallas kernels, add_grads(): pl.pallas_call(grads_kernel, grid=(parts * tiles,), in_specs=[pl.BlockSpe...  11.5 us
    ppermute x4, starting transfers between devices, shift(): lax.ppermute(shard, 'ctx', [(i, i + by) for i in range(size) if 0 <= i +...  8.86 us
    ppermute x6, starting transfers between devices, send_terms(): lax.ppermute(x, 'ctx', [(i, i ^ 2 * s + 2) for i in range(n_ctx)])  6.98 us
  transfers between devices with their start and end apart: 19, of which 8 were waited for; matrix products, arithmetic and copies ran while one was open for 28% of the time, Pallas kernels for 31%

commit v1 on v0

--- a/solution.py
+++ b/solution.py
@@ -10,7 +10,8 @@
 LOGIT_SCALE = 168.0 ** (-0.5)
 EXP2_SCALE = LOGIT_SCALE * 1.4426950408889634
 TILE = 256
-VMEM_LIMIT = 48 * 1024 * 1024
+VMEM_LIMIT = 24 * 1024 * 1024
+ATTENTION_VMEM_LIMIT = 48 * 1024 * 1024
 CHEAP = pl.CostEstimate(flops=1, bytes_accessed=1, transcendentals=0)
 
 NT = (((1,), (1,)), ((), ()))
@@ -105,7 +106,7 @@
             jax.ShapeDtypeStruct((groups, tiles, span, 2 * TILE), jnp.float32),
             jax.ShapeDtypeStruct((groups * 2 * head_size, rows), jnp.bfloat16),
         ],
-        compiler_params=pltpu.CompilerParams(vmem_limit_bytes=VMEM_LIMIT),
+        compiler_params=pltpu.CompilerParams(vmem_limit_bytes=ATTENTION_VMEM_LIMIT),
         cost_estimate=CHEAP,
         name="attention_forward",
     )(chip, packet, packet, packet, before, before)
@@ -190,7 +191,7 @@
             pl.BlockSpec((rows, head_size), lambda g, i: (0, g0 + g)),
             pl.BlockSpec((rows, head_size), lambda g, i: (0, groups + g0 + g)),
             pl.BlockSpec((1, 1, span, 2 * TILE), lambda g, i: (g0 + g, first + i, 0, 0)),
-            pl.BlockSpec((2 * head_size, TILE), lambda g, i: (g0 + g, i)),
+            pl.BlockSpec((2 * head_size, TILE), lambda g, i: (g0 + g, first + i)),
             carry_spec,
         ],
         out_specs=[
@@ -210,65 +211,179 @@
             pltpu.VMEM((rows + half, head_size), jnp.float32),
             pltpu.VMEM((span, 2 * TILE), jnp.float32),
         ],
-        compiler_params=pltpu.CompilerParams(vmem_limit_bytes=VMEM_LIMIT),
+        compiler_params=pltpu.CompilerParams(vmem_limit_bytes=ATTENTION_VMEM_LIMIT),
         cost_estimate=CHEAP,
         name="attention_backward",
     )(packet, packet, packet, before, before, attention, out_grads, carry)
 
 
-def grads_kernel(block_ref, weight_ref, *refs):
-    total = dot(weight_ref[...], block_ref[0])
-    if len(refs) == 2:
-        total = total + refs[0][...]
+def grads_kernel(number, *refs):
+    blocks, weights = refs[:number], refs[number : 2 * number]
+    total = None
+    for block, weight in zip(blocks, weights):
+        term = dot(weight[...], block[0])
+        total = term if total is None else total + term
+    for old in refs[2 * number : -1]:
+        total = total + old[...]
     refs[-1][...] = total.astype(refs[-1].dtype)
 
 
-def add_grads(block, weight, total, at, dtype):
-    parts, cols, tok = block.shape
-    width = weight.shape[0]
+def add_grads(blocks, weights, total, dtype):
+    _, cols, tok = blocks[0].shape
+    width = weights[0].shape[0]
     tiles = tok // TILE
-    return pl.pallas_call(
-        grads_kernel,
-        grid=(parts * tiles,),
-        in_specs=[
-            pl.BlockSpec((1, cols, TILE), lambda i: (i // tiles, 0, i % tiles)),
-            pl.BlockSpec((width, cols), lambda i: (0, 0)),
+    tile_spec = pl.BlockSpec((width, TILE), lambda i: (0, i))
+    number = len(blocks)
+    return pl.pallas_call(
+        functools.partial(grads_kernel, number),
+        grid=(2 * tiles,),
+        in_specs=[pl.BlockSpec((1, cols, TILE), lambda i: (i // tiles, 0, i % tiles))] * number
+        + [pl.BlockSpec((width, cols), lambda i: (0, 0))] * number
+        + ([] if total is None else [tile_spec]),
+        out_specs=tile_spec,
+        out_shape=jax.ShapeDtypeStruct((width, 2 * tok), dtype),
+        compiler_params=pltpu.CompilerParams(vmem_limit_bytes=VMEM_LIMIT),
+        cost_estimate=CHEAP,
+        name="out_grads",
+    )(*blocks, *weights, *([] if total is None else [total]))
+
+
+def terms_kernel(count, rows_ref, block, *outs):
+    _, cols, tok = block.shape
+    share = rows_ref.shape[0] // count
+    for at in range(0, cols, TILE):
+        here = slice(at, min(at + TILE, cols))
+        term = dot(rows_ref[:, :tok], block[0, here, :], NT) + dot(rows_ref[:, tok:], block[1, here, :], NT)
+        for s in range(count):
+            outs[s][:, here] = term[s * share : (s + 1) * share].astype(outs[s].dtype)
+
+
+def make_terms(rows, block, count):
+    cols = block.shape[1]
+    share = rows.shape[0] // count
+    whole = lambda *shape: pl.BlockSpec(shape, lambda i: (0,) * len(shape))
+    shapes = [jax.ShapeDtypeStruct((share, cols), jnp.float32 if s == 0 else jnp.bfloat16) for s in range(count)]
+    return pl.pallas_call(
+        functools.partial(terms_kernel, count),
+        grid=(1,),
+        in_specs=[whole(*rows.shape), whole(*block.shape)],
+        out_specs=[whole(share, cols)] * count,
+        out_shape=shapes,
+        compiler_params=pltpu.CompilerParams(vmem_limit_bytes=VMEM_LIMIT),
+        cost_estimate=CHEAP,
+        name="weight_terms",
+    )(rows, block)
+
+
+def close_kernel(groups, core_ref, from_low_ref, *refs):
+    owns, highs, (keep_ref, send_ref) = refs[:groups], refs[groups : 2 * groups], refs[2 * groups :]
+    half = from_low_ref.shape[2]
+
+    def write(low_ref, high_ref):
+        for part in range(2):
+            scale = LOGIT_SCALE if part == 0 else 1.0
+            for g in range(groups):
+                low = owns[g][part, 0, :half] * scale + from_low_ref[part, g].astype(jnp.float32)
+                high = owns[g][part, 0, half:] * scale + highs[g][part, 0].astype(jnp.float32)
+                low_ref[part, g] = low.astype(jnp.bfloat16)
+                high_ref[part, g] = high.astype(jnp.bfloat16)
+
+    @pl.when(core_ref[0] == 0)
+    def _():
+        write(keep_ref, send_ref)
+
+    @pl.when(core_ref[0] == 1)
+    def _():
+        write(send_ref, keep_ref)
+
+
+def close_sums(core, from_low, owns, highs):
+    whole = lambda x: pl.BlockSpec(x.shape, lambda i, c: (0,) * x.ndim)
+    out = jax.ShapeDtypeStruct(from_low.shape, jnp.bfloat16)
+    return pl.pallas_call(
+        functools.partial(close_kernel, len(owns)),
+        grid_spec=pltpu.PrefetchScalarGridSpec(
+            num_scalar_prefetch=1,
+            grid=(1,),
+            in_specs=[whole(x) for x in (from_low, *owns, *highs)],
+            out_specs=[whole(out), whole(out)],
+        ),
+        out_shape=[out, out],
+        compiler_params=pltpu.CompilerParams(vmem_limit_bytes=VMEM_LIMIT),
+        cost_estimate=CHEAP,
+        name="close_sums",
+    )(core, from_low, *owns, *highs)
+
+
+def place_kernel(where_ref, knocked_ref, start_ref, keep_ref, taken_ref, key_ref, value_ref, patch_ref):
+    groups, tok, head_size = keep_ref.shape[1:]
+    core, row_start = where_ref[0], where_ref[1]
+    positions = row_start + lax.broadcasted_iota(jnp.int32, (tok, head_size), 0)
+    for head in range(2 * groups):
+        own = core == head // groups
+        at = slice(head * head_size, (head + 1) * head_size)
+        both = [
+            jnp.where(own, keep_ref[part, head % groups].astype(jnp.float32), taken_ref[part, head % groups].astype(jnp.float32))
+            for part in range(2)
         ]
-        + ([] if total is None else [pl.BlockSpec((width, TILE), lambda i: (0, at // TILE + i))]),
-        out_specs=pl.BlockSpec((width, TILE), lambda i: (0, i)),
-        out_shape=jax.ShapeDtypeStruct((width, parts * tok), dtype),
+        chosen = jnp.logical_and(knocked_ref[head] == 1, positions >= start_ref[head])
+        key_ref[:, at] = jnp.where(chosen, 0.0, both[0]).astype(jnp.bfloat16)
+        patch_ref[:, at] = jnp.where(chosen, both[0], 0.0).astype(jnp.bfloat16)
+        value_ref[:, at] = both[1].astype(jnp.bfloat16)
+
+
+def place_sums(where, knocked, patch_start, keep, taken):
+    _, groups, tok, head_size = keep.shape
+    whole = pl.BlockSpec(keep.shape, lambda i, *_: (0, 0, 0, 0))
+    shape = (tok, 2 * groups * head_size)
+    return pl.pallas_call(
+        place_kernel,
+        grid_spec=pltpu.PrefetchScalarGridSpec(
+            num_scalar_prefetch=3,
+            grid=(1,),
+            in_specs=[whole, whole],
+            out_specs=[pl.BlockSpec(shape, lambda i, *_: (0, 0))] * 3,
+        ),
+        out_shape=[jax.ShapeDtypeStruct(shape, jnp.bfloat16)] * 3,
         compiler_params=pltpu.CompilerParams(vmem_limit_bytes=VMEM_LIMIT),
-        name="out_grads",
-    )(block, weight, *([] if total is None else [total]))
-
-
-def terms_kernel(count, rows_ref, *refs):
-    blocks, outs = refs[: len(refs) - count], refs[len(refs) - count :]
-    share = rows_ref.shape[0] // count
-    term, at = None, 0
-    for block in blocks:
-        for part in range(block.shape[0]):
-            width = block.shape[2]
-            piece = dot(rows_ref[:, at : at + width], block[part], NT)
-            term = piece if term is None else term + piece
-            at += width
-    for s in range(count):
-        outs[s][...] = term[s * share : (s + 1) * share].astype(outs[s].dtype)
-
-
-def make_terms(rows, blocks, count, chunk):
-    cols = blocks[0].shape[1]
-    share = rows.shape[0] // count
-    return pl.pallas_call(
-        functools.partial(terms_kernel, count),
-        grid=(cols // chunk,),
-        in_specs=[pl.BlockSpec(rows.shape, lambda i: (0, 0))]
-        + [pl.BlockSpec((block.shape[0], chunk, block.shape[2]), lambda i: (0, i, 0)) for block in blocks],
-        out_specs=[pl.BlockSpec((share, chunk), lambda i: (0, i))] * count,
-        out_shape=[jax.ShapeDtypeStruct((share, cols), jnp.float32 if s == 0 else jnp.bfloat16) for s in range(count)],
+        cost_estimate=CHEAP,
+        name="place_sums",
+    )(where, knocked, patch_start, keep, taken)
+
+
+def place_terms_kernel(size, at_ref, *refs):
+    out_ref = refs[-1]
+    cols = out_ref.shape[1] // size
+    each = (len(refs) - 1) // size
+    for n in range(size):
+        group = refs[n * each : (n + 1) * each]
+        for j in range(size):
+
+            @pl.when(at_ref[n] == j)
+            def _():
+                total = group[0][...]
+                for got in group[1:]:
+                    total = total + got[...].astype(jnp.float32)
+                out_ref[:, j * cols : (j + 1) * cols] = total
+
+
+def place_terms(at, groups):
+    flat = [x for group in groups for x in group]
+    share, cols = flat[0].shape
+    shape = (share, len(groups) * cols)
+    return pl.pallas_call(
+        functools.partial(place_terms_kernel, len(groups)),
+        grid_spec=pltpu.PrefetchScalarGridSpec(
+            num_scalar_prefetch=1,
+            grid=(1,),
+            in_specs=[pl.BlockSpec(x.shape, lambda i, c: (0, 0)) for x in flat],
+            out_specs=pl.BlockSpec(shape, lambda i, c: (0, 0)),
+        ),
+        out_shape=jax.ShapeDtypeStruct(shape, jnp.float32),
         compiler_params=pltpu.CompilerParams(vmem_limit_bytes=VMEM_LIMIT),
-        name="weight_terms",
-    )(rows, *blocks)
+        cost_estimate=CHEAP,
+        name="place_terms",
+    )(at, *flat)
 
 
 def shift(shard, by):
@@ -281,11 +396,15 @@
     return lax.ppermute(shard, "ctx", [(i, i ^ 1) for i in range(size) if only is None or i % 2 == only])
 
 
-def gather_chip(block):
-    n_ctx, n_head = lax.axis_size("ctx"), lax.axis_size("head")
-    groups = [[c * n_head + i for i in range(2 * n_head)] for c in range(0, n_ctx, 2)]
-    whole = lax.all_gather(block, ("ctx", "head"), axis=0, axis_index_groups=groups)
-    return whole.reshape(2, n_head * block.shape[0], block.shape[1])
+def turn(shard, by):
+    size = lax.axis_size("head")
+    return lax.ppermute(shard, "head", [(i, (i + by) % size) for i in range(size)])
+
+
+def move(shard, pairs):
+    size, n_ctx = lax.axis_size("head"), lax.axis_size("ctx")
+    places = [((c + a) * size + i, (c + b) * size + j) for c in range(0, n_ctx, 2) for (a, i), (b, j) in pairs]
+    return lax.ppermute(shard, ("ctx", "head"), places)
 
 
 def after(values, *others):
@@ -306,6 +425,16 @@
     half_q, half_kv = queries.shape[1] // 2, cached_keys.shape[1] // 2
     dyn = lax.dynamic_slice_in_dim
 
+    partner = swap_cores(out_grad)
+    own_block = jnp.stack([jnp.where(low, out_grad, partner), jnp.where(low, partner, out_grad)])
+    if n_head == 4:
+        up, down = [((0, i), (0, (i + 1) % 4)) for i in range(4)], [((1, i), (1, (i - 1) % 4)) for i in range(4)]
+        direct = (move(own_block, up + down),)
+        distances, last = [jnp.where(low, 3, 1), jnp.where(low, 1, 3)], 2
+    else:
+        direct = tuple(turn(own_block, s) for s in range(1, n_head - 1))
+        distances, last = [n_head - s for s in range(1, n_head - 1)], 1
+
     positions = place * tok + jnp.arange(tok, dtype=jnp.int32)
     chosen = (jnp.repeat(knocked, head_size)[None, :] == 1) & (
         positions[:, None] >= jnp.repeat(patch_start, head_size)[None, :]
@@ -326,18 +455,12 @@
     packet = jnp.concatenate([jnp.where(low, mine, other), jnp.where(low, other, mine)], axis=0)
     before = shift(packet[:, half_q:], 2)
 
-    cut = 2 * cols // 3
-    quarter = tok // 2
-    first = gather_chip(out_grad[:cut])
-    rest = out_grad[cut:]
-    passed = swap_cores(jnp.where(low, rest[:, quarter:], rest[:, :quarter]))
-    second = gather_chip(jnp.where(low, rest[:, :quarter], passed))
-    third = gather_chip(jnp.where(low, passed, rest[:, quarter:]))
-
-    weight_half = dyn(out_weight, core * half_q, half_q, 0).reshape(half_q, n_head, cols)
-    first_weight = weight_half[:, :, :cut].reshape(half_q, n_head * cut)
-    rest_weight = weight_half[:, :, cut:].reshape(half_q, n_head * (cols - cut))
-    before = after(before, first_weight, rest_weight)
+    order = [0, *distances, last]
+    weight_half = dyn(out_weight, core * half_q, half_q, 0)
+    weights = [dyn(weight_half, ((z + d) % n_head) * cols, cols, 1) for d in order]
+    core_id = core[None].astype(jnp.int32)
+    grads = add_grads([own_block], weights[:1], None, jnp.float32)
+    before = after(before, grads, weights)
 
     attention, attended = forward(chip[None].astype(jnp.int32), packet, before, head_size)
     share = out_weight.shape[0] // n_ctx
@@ -348,53 +471,64 @@
     by_distance = jnp.concatenate([dyn(by_chip, chip ^ s, 1, 0) for s in range(chips)], axis=0)
     by_distance = by_distance.reshape(chips * share, 2 * tok)
 
-    def send_terms(blocks, chunk):
-        kept_term, *sent = make_terms(by_distance, blocks, chips, chunk)
+    def send_terms(block):
+        kept_term, *sent = make_terms(by_distance, block, chips)
         got = [lax.ppermute(x, "ctx", [(i, i ^ (2 * s + 2)) for i in range(n_ctx)]) for s, x in enumerate(sent)]
-        return kept_term, sent, got
-
-    first_terms = send_terms([first], 2 * TILE)
-    grads = add_grads(first, first_weight, None, 0, jnp.float32)
-    grads, _ = lax.optimization_barrier((grads, first_terms[1]))
+        return [kept_term, *got], sent
+
+    terms = []
+
+    def wait(value, *others, on=(), since=slice(None)):
+        value, _, got = lax.optimization_barrier((value, others, [terms[n][since] for n in on]))
+        for n, g in zip(on, got):
+            terms[n][since] = g
+        return value
+
+    term, sent = send_terms(own_block)
+    terms.append(term)
+    direct = wait(direct, sent, on=[0], since=slice(1, 3))
+    if n_head == 4:
+        hops = [((i % 2, i), (i % 2, j)) for i, j in [(0, 1), (1, 0), (2, 3), (3, 2)]]
+        final = move(direct[0], hops)
+        blocks = [direct[0], swap_cores(direct[0])]
+    else:
+        final = turn(own_block, -1)
+        blocks = list(direct)
+    for n, block in enumerate(blocks):
+        block = after(block, sent)
+        term, sent = send_terms(block)
+        terms.append(term)
+    grads = add_grads(blocks, weights[1:-1], grads, jnp.float32)
+
+    final = wait(final, grads, sent, on=[0, 1], since=slice(1, None))
+    final = wait(final, on=[2], since=slice(1, 3))
+    if n_head == 4:
+        final = jnp.where(core == 1 - z % 2, final, swap_cores(final))
+    term, sent = send_terms(final)
+    terms.append(term)
+    final = wait(final, sent, on=[2], since=slice(3, None))
+    grads = add_grads([final], weights[-1:], grads, jnp.bfloat16)
+    grads = wait(grads, on=[3], since=slice(1, None))
     all_groups = (0, packet.shape[1] // (4 * head_size))
-    grads_low = add_grads(second, rest_weight, grads, 0, jnp.bfloat16)
-    query_low, prev_low, carry = backward(0, all_groups, packet, before, attention, grads_low, None, head_size)
+    query_low, prev_low, carry = backward(0, all_groups, packet, before, attention, grads, None, head_size)
     from_low = shift(prev_low, -2)
-
-    third, query_low, first_terms = lax.optimization_barrier((third, query_low, first_terms))
-    last_terms = send_terms([second, third], TILE)
-    grads_high = add_grads(third, rest_weight, grads, tok, jnp.bfloat16)
-    grads_high = after(grads_high, last_terms[1])
     parts = []
     for g in range(all_groups[1]):
-        if g == all_groups[1] - 1:
-            grads_high, from_low = lax.optimization_barrier((grads_high, from_low))
-        parts.append(backward(1, (g, 1), packet, before, attention, grads_high, carry, head_size))
-    from_high = jnp.concatenate([shift(part[1], -2) for part in parts], axis=1)
+        if g > 0 and g == all_groups[1] - 1:
+            grads, from_low = lax.optimization_barrier((grads, from_low))
+        parts.append(backward(1, (g, 1), packet, before, attention, grads, carry, head_size))
     query_high = jnp.concatenate([part[0] for part in parts], axis=1)
-    own = jnp.concatenate([part[2] for part in parts], axis=1)
-
-    sums = [functools.reduce(jnp.add, t[2], t[0]).reshape(share, n_head, -1) for t in (first_terms, last_terms)]
-    weight_grad = jnp.concatenate(sums, axis=2).reshape(share, -1)
+
+    weight_grad = place_terms(jnp.stack([(z + d) % n_head for d in order]).astype(jnp.int32), terms)
 
     query_kept = jnp.where(low, query_low, query_high)
-    query_taken = jnp.where(low, swap_cores(query_low, 1), swap_cores(query_high, 0))
+    query_taken = swap_cores(jnp.where(low, query_high, query_low))
     query_grad = jnp.concatenate(
         [jnp.where(low, query_kept, query_taken), jnp.where(low, query_taken, query_kept)], axis=1
     )
-
-    scale = jnp.array([LOGIT_SCALE, 1.0], jnp.float32)[:, None, None, None]
-    sums_low = scale * own[:, :, :tok] + from_low
-    sums_high = scale * own[:, :, tok:] + from_high
-    sums_kept = jnp.where(low, sums_low, sums_high)
-    sums_taken = swap_cores(jnp.where(low, sums_high, sums_low).astype(jnp.bfloat16)).astype(jnp.float32)
-    sums = jnp.concatenate(
-        [jnp.where(low, sums_kept, sums_taken), jnp.where(low, sums_taken, sums_kept)], axis=1
-    )
-    key_sums, value_sums = [jnp.concatenate([part[h] for h in range(kv_local)], axis=1) for part in (sums[0], sums[1])]
-    key_grad = jnp.where(chosen, jnp.float32(0.0), key_sums).astype(jnp.bfloat16)
-    patch_grad = jnp.where(chosen, key_sums, jnp.float32(0.0)).astype(jnp.bfloat16)
-    value_grad = value_sums.astype(jnp.bfloat16)
+    keep, send = close_sums(core_id, from_low, [part[2] for part in parts], [shift(part[1], -2) for part in parts])
+    where = jnp.stack([core, place * tok]).astype(jnp.int32)
+    key_grad, value_grad, patch_grad = place_sums(where, knocked, patch_start, keep, swap_cores(send))
     return (query_grad, key_grad, value_grad, patch_grad, weight_grad)
 
 

time: 218 us -> 201 us (0.922)
  local copies, waits for them, and re-layouts: 54.8 us -> 23.3 us
  waiting for transfers between devices: 37.2 us -> 65.1 us
  between operations: 14.3 us -> 1.3 us
  starting transfers between devices: 20.4 us -> 31.3 us
  other arithmetic: 22 us -> 11.8 us
    ppermute x6 -> x12, waiting for transfers between devices: 0.02 us -> 30.8 us  [send_terms(): lax.ppermute(x, 'ctx', [(i, i ^ 2 * s + 2) for i in range(n_ctx)])]
    all_gather x3 -> x0, waiting for transfers between devices: 27.5 us -> none  [gather_chip(): lax.all_gather(block, ('ctx', 'head'), axis=0, axis_index_groups=groups)]
    ppermute x4, waiting for transfers between devices: 4.38 us -> 28.4 us  [shift(): lax.ppermute(shard, 'ctx', [(i, i + by) for i in range(size) if 0 <= i +...]
    unnamed x60 -> x77, local copies, waits for them, and re-layouts: 24.4 us -> 12.5 us
    reshape x3 -> x0, local copies, waits for them, and re-layouts: 11.5 us -> none  [the longest x1 5.97 us: body(): first_weight = weight_half[:, :, :cut].reshape(half_q, n_head * cut)]
    slice x3 -> x0, local copies, waits for them, and re-layouts: 9.37 us -> none  [the longest x1 4.18 us: body(): first_weight = weight_half[:, :, :cut].reshape(half_q, n_head * cut)]
    ppermute x6 -> x12, starting transfers between devices: 6.98 us -> 15.8 us  [send_terms(): lax.ppermute(x, 'ctx', [(i, i ^ 2 * s + 2) for i in range(n_ctx)])]
    ppermute x0 -> x2, starting transfers between devices: none -> 5.85 us  [move(): return lax.ppermute(shard, ('ctx', 'head'), places)]
  transfers between devices with their start and end apart: 19 -> 25, of which waited for: 8 -> 12; matrix products, arithmetic and copies ran while one was open for 28% -> 11% of each run, Pallas kernels for 31% -> 24%
where the time goes in v1:
time: 201 us; the launch traced here: 200 us
  Pallas kernels  66.8 us (33%)
  waiting for transfers between devices  65.1 us (32%)
  starting transfers between devices  31.3 us (16%)
  local copies, waits for them, and re-layouts  23.3 us (12%)
  other arithmetic  11.8 us (6%)
    ppermute x12, waiting for transfers between devices, send_terms(): lax.ppermute(x, 'ctx', [(i, i ^ 2 * s + 2) for i in range(n_ctx)])  30.8 us
    ppermute x4, waiting for transfers between devices, shift(): lax.ppermute(shard, 'ctx', [(i, i + by) for i in range(size) if 0 <= i +...  28.4 us
    pallas_call x3, Pallas kernels, backward(): pl.pallas_call(functools.partial(backward_kernel, phase), grid=(count, ti...  22.7 us
    ppermute x12, starting transfers between devices, send_terms(): lax.ppermute(x, 'ctx', [(i, i ^ 2 * s + 2) for i in range(n_ctx)])  15.8 us
    pallas_call x1, Pallas kernels, forward(): pl.pallas_call(forward_kernel, grid_spec=grid_spec, out_shape=[jax.ShapeD...  14.9 us
    pallas_call x3, Pallas kernels, add_grads(): pl.pallas_call(functools.partial(grads_kernel, number), grid=(2 * tiles,)...  13 us
    unnamed x77, local copies, waits for them, and re-layouts  12.5 us
    pallas_call x4, Pallas kernels, make_terms(): pl.pallas_call(functools.partial(terms_kernel, count), grid=(1,), in_spec...  10.9 us
  transfers between devices with their start and end apart: 25, of which 12 were waited for; matrix products, arithmetic and copies ran while one was open for 11% of the time, Pallas kernels for 24%

profile of v1, /device:TPU:0, one launch (start us, length us, event | category | flops | bytes accessed | tf_op | source)
XLA Modules:
  0.0 199.7 jit_solution(5134351754736529622)
XLA Ops:
  8.5 2.9 %collective-permute-start.3 = (bf16[2,1344,512]{2,1,0:T(8,128)(2,1)}, bf16[2,1344,512]{2,1,0:T(8,128)(2,1)}, u32[]{:S(2)}, u32[]{:S(2)}) collective-permute-start(bf16[2,1344,512]{2,1,0:T(8,128)(2,1)} %pad_maximum_fusion.refs_0_.block), channel_id=1, source_target_pairs={{0,1},{1,2},{2,3},{3,0},{4,7},{5,4},{6,5},{7,6},{8,9},{9,10},{10,1... | collective-permute-start | bytes 8257544 | tf_op jit(solution)/shard_map/ppermute | solution.py:407
  15.2 3.4 %collective-permute-start.1 = (bf16[1024,512]{1,0:T(8,128)(2,1)}, bf16[1024,512]{1,0:T(8,128)(2,1)S(1)}, u32[]{:S(2)}, u32[]{:S(2)}) collective-permute-start(bf16[1024,512]{1,0:T(8,128)(2,1)} %fusion), channel_id=1, source_target_pairs={{0,8},{4,12},{8,16},{12,20},{16,24},{20,28},{1,9},{5,13},{9,17},{1... | collective-permute-start | bytes 3145736 | tf_op jit(solution)/shard_map/ppermute | solution.py:391
  18.8 8.4 %fusion.5 = (bf16[512,1344]{1,0:T(8,128)(2,1)}, bf16[512,1344]{1,0:T(8,128)(2,1)}, bf16[512,1344]{1,0:T(8,128)(2,1)S(1)}, bf16[512,1344]{1,0:T(8,128)(2,1)}) fusion(bf16[1024,5376]{1,0:T(8,128)(2,1)} %param.13, s32[]{:T(128)S(6)} %select_n.182, s32[]{:T(128)S(6)} %select_n.196, s32[]{:T(128)S(6)} %select_n.189, s32[]{:T(128)S(6)} %select_n.185, s32[]{:T(128)S(6)} %select_n.193), kind=kLoop, calls=%fused_computation.48 | loop fusion | bytes 11010068 | tf_op jit(solution)/shard_map/dynamic_slice | solution.py:460
  27.4 4.7 %out_grads.3.refs_4_ = f32[512,1024]{1,0:T(8,128)S(1)} custom-call(bf16[2,1344,512]{2,1,0:T(8,128)(2,1)} %pad_maximum_fusion.refs_0_.block, bf16[512,1344]{1,0:T(8,128)(2,1)S(1)} %get-tuple-element.119.refs_1_), custom_call_target="tpu_custom_call" | custom-call | flops 1 | bytes 1 | tf_op jit(solution)/shard_map/out_grads/pallas_call | solution.py:237
  33.4 8.1 %collective-permute-done.1.pk_ref.pv_ref = bf16[1024,512]{1,0:T(8,128)(2,1)S(1)} collective-permute-done((bf16[1024,512]{1,0:T(8,128)(2,1)}, bf16[1024,512]{1,0:T(8,128)(2,1)S(1)}, u32[]{:S(2)}, u32[]{:S(2)}) %collective-permute-start.1) | collective-permute-done | bytes 1048608 | tf_op jit(solution)/shard_map/ppermute | solution.py:391
  41.5 14.9 %attention_forward.1 = (f32[2,4,1280,512]{3,2,1,0:T(8,128)}, bf16[512,1024]{1,0:T(8,128)(2,1)S(1)}) custom-call(s32[1]{0:T(128)} %bitcast.5.chip_ref, bf16[1024,1024]{1,0:T(8,128)(2,1)S(1)} %pad_maximum_fusion.1.q_ref.k_ref.v_ref, bf16[1024,1024]{1,0:T(8,128)(2,1)S(1)} %pad_maximum_fusion.1.q_ref.k_ref.v_ref, ...), custom_call_target="tpu_custom_call" | custom-call | flops 1 | bytes 1 | tf_op jit(solution)/shard_map/attention_forward/pallas_call | solution.py:102
  59.8 3.6 %weight_terms.4 = (f32[128,1344]{1,0:T(8,128)S(1)}, bf16[128,1344]{1,0:T(8,128)(2,1)S(1)}, bf16[128,1344]{1,0:T(8,128)(2,1)S(1)}, bf16[128,1344]{1,0:T(8,128)(2,1)S(1)}) custom-call(bf16[512,1024]{1,0:T(8,128)(2,1)S(1)} %bitcast.25, bf16[2,1344,512]{2,1,0:T(8,128)(2,1)} %pad_maximum_fusion.refs_0_.block), custom_call_target="tpu_custom_call" | custom-call | flops 1 | bytes 1 | tf_op jit(solution)/shard_map/weight_terms/pallas_call | solution.py:266
  63.4 2.6 %collective-permute-start.5 = (bf16[128,1344]{1,0:T(8,128)(2,1)S(1)}, bf16[128,1344]{1,0:T(8,128)(2,1)S(1)}, u32[]{:S(2)}, u32[]{:S(2)}) collective-permute-start(bf16[128,1344]{1,0:T(8,128)(2,1)S(1)} %get-tuple-element.64), channel_id=1, source_target_pairs={{0,8},{4,12},{8,0},{12,4},{16,24},{20,28},{24,16},{28,20},{1,9},{5... | collective-permute-start | bytes 1032200 | tf_op jit(solution)/shard_map/ppermute | solution.py:476
  67.5 7.4 %collective-permute-done.5.refs_1_ = bf16[128,1344]{1,0:T(8,128)(2,1)S(1)} collective-permute-done((bf16[128,1344]{1,0:T(8,128)(2,1)S(1)}, bf16[128,1344]{1,0:T(8,128)(2,1)S(1)}, u32[]{:S(2)}, u32[]{:S(2)}) %collective-permute-start.5) | collective-permute-done | bytes 344096 | tf_op jit(solution)/shard_map/ppermute | solution.py:476
  77.1 2.9 %collective-permute-start.7 = (bf16[2,1344,512]{2,1,0:T(8,128)(2,1)}, bf16[2,1344,512]{2,1,0:T(8,128)(2,1)}, u32[]{:S(2)}, u32[]{:S(2)}) collective-permute-start(bf16[2,1344,512]{2,1,0:T(8,128)(2,1)} %collective-permute-done.3.refs_0_.block), channel_id=1, source_target_pairs={{0,1},{5,4},{2,3},{7,6},{8,9},{13,12},{10,11},{15,14},{16,17},{21,... | collective-permute-start | bytes 8257544 | tf_op jit(solution)/shard_map/ppermute | solution.py:407
  80.0 2.4 %collective-permute-start.9 = (bf16[128,1344]{1,0:T(8,128)(2,1)S(1)}, bf16[128,1344]{1,0:T(8,128)(2,1)S(1)}, u32[]{:S(2)}, u32[]{:S(2)}) collective-permute-start(bf16[128,1344]{1,0:T(8,128)(2,1)S(1)} %get-tuple-element.66), channel_id=1, source_target_pairs={{0,24},{4,28},{8,16},{12,20},{16,8},{20,12},{24,0},{28,4},{1,25},{... | collective-permute-start | bytes 1032200 | tf_op jit(solution)/shard_map/ppermute | solution.py:476
  82.4 3.7 %weight_terms.5 = (f32[128,1344]{1,0:T(8,128)S(1)}, bf16[128,1344]{1,0:T(8,128)(2,1)S(1)}, bf16[128,1344]{1,0:T(8,128)(2,1)S(1)}, bf16[128,1344]{1,0:T(8,128)(2,1)S(1)}) custom-call(bf16[512,1024]{1,0:T(8,128)(2,1)S(1)} %bitcast.26, bf16[2,1344,512]{2,1,0:T(8,128)(2,1)} %collective-permute-done.3.refs_0_.block), custom_call_target="tpu_custom_call" | custom-call | flops 1 | bytes 1 | tf_op jit(solution)/shard_map/weight_terms/pallas_call | solution.py:266
  87.3 2.4 %collective-permute-start.12 = (bf16[128,1344]{1,0:T(8,128)(2,1)S(1)}, bf16[128,1344]{1,0:T(8,128)(2,1)S(1)}, u32[]{:S(2)}, u32[]{:S(2)}) collective-permute-start(bf16[128,1344]{1,0:T(8,128)(2,1)S(1)} %get-tuple-element.71), channel_id=1, source_target_pairs={{0,24},{4,28},{8,16},{12,20},{16,8},{20,12},{24,0},{28,4},{1,25},{... | collective-permute-start | bytes 1032200 | tf_op jit(solution)/shard_map/ppermute | solution.py:476
  89.7 1.8 weight_terms.6
  94.9 5.6 %collective-permute-done.10.refs_5_ = bf16[128,1344]{1,0:T(8,128)(2,1)S(1)} collective-permute-done((bf16[128,1344]{1,0:T(8,128)(2,1)S(1)}, bf16[128,1344]{1,0:T(8,128)(2,1)S(1)}, u32[]{:S(2)}, u32[]{:S(2)}) %collective-permute-start.10) | collective-permute-done | bytes 344096 | tf_op jit(solution)/shard_map/ppermute | solution.py:476
  101.3 5.4 %out_grads.4.refs_2_ = f32[512,1024]{1,0:T(8,128)S(1)} custom-call(bf16[2,1344,512]{2,1,0:T(8,128)(2,1)} %collective-permute-done.3.refs_0_.block, bf16[2,1344,512]{2,1,0:T(8,128)(2,1)S(1)} %collective-permute-done.8.refs_1_.block, bf16[512,1344]{1,0:T(8,128)(2,1)S(1)} %copy-done.7, bf16[512,1344]{1,0:T(8,128)(2,1)S(1)} %copy-done.8, f32[512,1024]{1,0:T(8,128)S(1)} %copy-done.4), custom_call_target="tpu_custom_call" | custom-call | flops 1 | bytes 1 | tf_op jit(solution)/shard_map/out_grads/pallas_call | solution.py:237
  109.6 4.5 %collective-permute-done.13.refs_9_ = bf16[128,1344]{1,0:T(8,128)(2,1)S(1)} collective-permute-done((bf16[128,1344]{1,0:T(8,128)(2,1)S(1)}, bf16[128,1344]{1,0:T(8,128)(2,1)S(1)}, u32[]{:S(2)}, u32[]{:S(2)}) %collective-permute-start.13) | collective-permute-done | bytes 344096 | tf_op jit(solution)/shard_map/ppermute | solution.py:476
  116.6 4.3 %collective-permute-done.15 = bf16[2,1344,512]{2,1,0:T(8,128)(2,1)} collective-permute-done((bf16[2,1344,512]{2,1,0:T(8,128)(2,1)}, bf16[2,1344,512]{2,1,0:T(8,128)(2,1)}, u32[]{:S(2)}, u32[]{:S(2)}) %collective-permute-start.15) | collective-permute-done | bytes 2752544 | tf_op jit(solution)/shard_map/ppermute | solution.py:396
  121.0 2.1 %broadcast_select_fusion.block.refs_0_ = bf16[2,1344,512]{2,1,0:T(8,128)(2,1)S(1)} fusion(bf16[2,1344,512]{2,1,0:T(8,128)(2,1)} %collective-permute-done.7, bf16[2,1344,512]{2,1,0:T(8,128)(2,1)} %collective-permute-done.15, pred[]{:T(512)S(6)} %eq.36), kind=kLoop, calls=%fused_computation.1 | loop fusion | flops 1376256 | bytes 8257537 | tf_op jit(solution)/shard_map/jit(_where)/select_n | solution.py:506
  123.1 1.8 weight_terms.7
  126.6 1.8 collective-permute-start.19
  128.5 2.9 %out_grads.5.do_ref = bf16[512,1024]{1,0:T(8,128)(2,1)S(1)} custom-call(bf16[2,1344,512]{2,1,0:T(8,128)(2,1)S(1)} %broadcast_select_fusion.block.refs_0_, bf16[512,1344]{1,0:T(8,128)(2,1)S(1)} %copy-done.9, f32[512,1024]{1,0:T(8,128)S(1)} %copy-done.6), custom_call_target="tpu_custom_call" | custom-call | flops 1 | bytes 1 | tf_op jit(solution)/shard_map/out_grads/pallas_call | solution.py:237
  131.4 4.9 %collective-permute-done.17.refs_13_ = bf16[128,1344]{1,0:T(8,128)(2,1)S(1)} collective-permute-done((bf16[128,1344]{1,0:T(8,128)(2,1)S(1)}, bf16[128,1344]{1,0:T(8,128)(2,1)S(1)}, u32[]{:S(2)}, u32[]{:S(2)}) %collective-permute-start.17) | collective-permute-done | bytes 344096 | tf_op jit(solution)/shard_map/ppermute | solution.py:476
  136.2 7.6 %collective-permute-done.18.refs_14_ = bf16[128,1344]{1,0:T(8,128)(2,1)S(1)} collective-permute-done((bf16[128,1344]{1,0:T(8,128)(2,1)S(1)}, bf16[128,1344]{1,0:T(8,128)(2,1)S(1)}, u32[]{:S(2)}, u32[]{:S(2)}) %collective-permute-start.18) | collective-permute-done | bytes 344096 | tf_op jit(solution)/shard_map/ppermute | solution.py:476
  143.9 10.7 %attention_backward.3 = (bf16[512,512]{1,0:T(8,128)(2,1)S(1)}, bf16[2,2,512,128]{3,2,1,0:T(8,128)(2,1)S(1)}, f32[2,2,1024,128]{3,2,1,0:T(8,128)S(1)}) custom-call(bf16[1024,1024]{1,0:T(8,128)(2,1)} %copy-done, bf16[1024,1024]{1,0:T(8,128)(2,1)} %copy-done, bf16[1024,1024]{1,0:T(8,128)(2,1)} %copy-done, ...), custom_call_target="tpu_custom_call" | custom-call | flops 1 | bytes 1 | tf_op jit(solution)/shard_map/attention_backward/pallas_call | solution.py:184
  157.4 6.1 %attention_backward.4 = (bf16[512,256]{1,0:T(8,128)(2,1)S(1)}, bf16[2,1,512,128]{3,2,1,0:T(8,128)(2,1)S(1)}, f32[2,1,1024,128]{3,2,1,0:T(8,128)S(1)}) custom-call(bf16[1024,1024]{1,0:T(8,128)(2,1)S(1)} %copy-done.1, bf16[1024,1024]{1,0:T(8,128)(2,1)S(1)} %copy-done.1, bf16[1024,1024]{1,0:T(8,128)(2,1)S(1)} %copy-done.1, ...), custom_call_target="tpu_custom_call" | custom-call | flops 1 | bytes 1 | tf_op jit(solution)/shard_map/attention_backward/pallas_call | solution.py:184
  163.5 6.8 %collective-permute-done.20.from_low_ref = bf16[2,2,512,128]{3,2,1,0:T(8,128)(2,1)S(1)} collective-permute-done((bf16[2,2,512,128]{3,2,1,0:T(8,128)(2,1)S(1)}, bf16[2,2,512,128]{3,2,1,0:T(8,128)(2,1)S(1)}, u32[]{:S(2)}, u32[]{:S(2)}) %collective-permute-start.20) | collective-permute-done | bytes 524320 | tf_op jit(solution)/shard_map/ppermute | solution.py:391
  170.3 6.0 %attention_backward.5 = (bf16[512,256]{1,0:T(8,128)(2,1)S(1)}, bf16[2,1,512,128]{3,2,1,0:T(8,128)(2,1)S(1)}, f32[2,1,1024,128]{3,2,1,0:T(8,128)S(1)}) custom-call(bf16[1024,1024]{1,0:T(8,128)(2,1)S(1)} %copy-done.1, bf16[1024,1024]{1,0:T(8,128)(2,1)S(1)} %copy-done.1, bf16[1024,1024]{1,0:T(8,128)(2,1)S(1)} %copy-done.1, ...), custom_call_target="tpu_custom_call" | custom-call | flops 1 | bytes 1 | tf_op jit(solution)/shard_map/attention_backward/pallas_call | solution.py:184
  179.5 8.3 %collective-permute-done.22.refs_2_ = bf16[2,1,512,128]{3,2,1,0:T(8,128)(2,1)S(1)} collective-permute-done((bf16[2,1,512,128]{3,2,1,0:T(8,128)(2,1)S(1)}, bf16[2,1,512,128]{3,2,1,0:T(8,128)(2,1)S(1)}, u32[]{:S(2)}, u32[]{:S(2)}) %collective-permute-start.22) | collective-permute-done | bytes 262176 | tf_op jit(solution)/shard_map/ppermute | solution.py:391
  187.9 5.1 %collective-permute-done.23.refs_3_ = bf16[2,1,512,128]{3,2,1,0:T(8,128)(2,1)S(1)} collective-permute-done((bf16[2,1,512,128]{3,2,1,0:T(8,128)(2,1)S(1)}, bf16[2,1,512,128]{3,2,1,0:T(8,128)(2,1)S(1)}, u32[]{:S(2)}, u32[]{:S(2)}) %collective-permute-start.23) | collective-permute-done | bytes 262176 | tf_op jit(solution)/shard_map/ppermute | solution.py:391
  193.4 3.0 %place_terms.1 = f32[128,5376]{1,0:T(8,128)} custom-call(s32[4]{0:T(128)S(1)} %pad_add_fusion.1.at_ref, f32[128,1344]{1,0:T(8,128)S(1)} %get-tuple-element.101.refs_0_, bf16[128,1344]{1,0:T(8,128)(2,1)S(1)} %copy-done.13, bf16[128,1344]{1,0:T(8,128)(2,1)S(1)} %copy-done.15, bf16[128,1344]{1,0:T(8,128)(2,1)S(1)} %copy-done.17, ...), custom_call_target="tpu_custom_call" | custom-call | flops 1 | bytes 1 | tf_op jit(solution)/shard_map/place_terms/pallas_call | solution.py:374
  197.7 2.0 %place_sums.1 = (bf16[512,512]{1,0:T(8,128)(2,1)}, bf16[512,512]{1,0:T(8,128)(2,1)}, bf16[512,512]{1,0:T(8,128)(2,1)}) custom-call(s32[2]{0:T(128)S(1)} %pad_add_fusion.where_ref, s32[4]{0:T(128)S(1)} %copy-done.29, s32[4]{0:T(128)S(1)} %copy-done.28, bf16[2,2,512,128]{3,2,1,0:T(8,128)(2,1)S(1)} %get-tuple-element.96.keep_ref, ...), custom_call_target="tpu_custom_call" | custom-call | flops 1 | bytes 1 | tf_op jit(solution)/shard_map/place_sums/pallas_call | solution.py:339
  (135 shorter events, 40.1 us)
Async XLA Ops:
  0.7 4.5 %collective-permute-start.2 = (bf16[1344,512]{1,0:T(8,128)(2,1)}, bf16[1344,512]{1,0:T(8,128)(2,1)}, u32[]{:S(2)}, u32[]{:S(2)}) collective-permute-start(bf16[1344,512]{1,0:T(8,128)(2,1)} %bitcast.31), channel_id=1, source_target_pairs={{0,4},{4,0},{8,12},{12,8},{16,20},{20,16},{24,28},{28,24},{1,5},{5... | collective-permute-start | bytes 4128776 | tf_op jit(solution)/shard_map/ppermute | solution.py:396
  5.0 6.4 %collective-permute-start = (bf16[512,1024]{1,0:T(8,128)(2,1)}, bf16[512,1024]{1,0:T(8,128)(2,1)S(1)}, u32[]{:S(2)}, u32[]{:S(2)}) collective-permute-start(bf16[512,1024]{1,0:T(8,128)(2,1)} %pad_maximum_fusion.3), channel_id=1, source_target_pairs={{0,4},{4,0},{8,12},{12,8},{16,20},{20,16},{24,28},{28,24},{1,5},{5... | collective-permute-start | bytes 3145736 | tf_op jit(solution)/shard_map/ppermute | solution.py:396
  8.5 68.6 %collective-permute-start.3 = (bf16[2,1344,512]{2,1,0:T(8,128)(2,1)}, bf16[2,1344,512]{2,1,0:T(8,128)(2,1)}, u32[]{:S(2)}, u32[]{:S(2)}) collective-permute-start(bf16[2,1344,512]{2,1,0:T(8,128)(2,1)} %pad_maximum_fusion.refs_0_.block), channel_id=1, source_target_pairs={{0,1},{1,2},{2,3},{3,0},{4,7},{5,4},{6,5},{7,6},{8,9},{9,10},{10,1... | collective-permute-start | bytes 8257544 | tf_op jit(solution)/shard_map/ppermute | solution.py:407
  15.2 26.3 %collective-permute-start.1 = (bf16[1024,512]{1,0:T(8,128)(2,1)}, bf16[1024,512]{1,0:T(8,128)(2,1)S(1)}, u32[]{:S(2)}, u32[]{:S(2)}) collective-permute-start(bf16[1024,512]{1,0:T(8,128)(2,1)} %fusion), channel_id=1, source_target_pairs={{0,8},{4,12},{8,16},{12,20},{16,24},{20,28},{1,9},{5,13},{9,17},{1... | collective-permute-start | bytes 3145736 | tf_op jit(solution)/shard_map/ppermute | solution.py:391
  56.5 2.7 %collective-permute-start.4 = (bf16[2,128,1024]{2,1,0:T(8,128)(2,1)S(1)}, bf16[2,128,1024]{2,1,0:T(8,128)(2,1)S(1)}, u32[]{:S(2)}, u32[]{:S(2)}) collective-permute-start(bf16[2,128,1024]{2,1,0:T(8,128)(2,1)S(1)} %dynamic-slice_bitcast_fusion), channel_id=1, source_target_pairs={{0,4},{4,0},{8,12},{12,8},{16,20},{20,16},{24,28},{28,24},{1,5},{5... | collective-permute-start | bytes 1572872 | tf_op jit(solution)/shard_map/ppermute | solution.py:396
  63.4 11.5 %collective-permute-start.5 = (bf16[128,1344]{1,0:T(8,128)(2,1)S(1)}, bf16[128,1344]{1,0:T(8,128)(2,1)S(1)}, u32[]{:S(2)}, u32[]{:S(2)}) collective-permute-start(bf16[128,1344]{1,0:T(8,128)(2,1)S(1)} %get-tuple-element.64), channel_id=1, source_target_pairs={{0,8},{4,12},{8,0},{12,4},{16,24},{20,28},{24,16},{28,20},{1,9},{5... | collective-permute-start | bytes 1032200 | tf_op jit(solution)/shard_map/ppermute | solution.py:476
  66.0 10.4 %collective-permute-start.6 = (bf16[128,1344]{1,0:T(8,128)(2,1)S(1)}, bf16[128,1344]{1,0:T(8,128)(2,1)S(1)}, u32[]{:S(2)}, u32[]{:S(2)}) collective-permute-start(bf16[128,1344]{1,0:T(8,128)(2,1)S(1)} %get-tuple-element.65), channel_id=1, source_target_pairs={{0,16},{4,20},{8,24},{12,28},{16,0},{20,4},{24,8},{28,12},{1,17},{... | collective-permute-start | bytes 1032200 | tf_op jit(solution)/shard_map/ppermute | solution.py:476
  77.1 10.2 %collective-permute-start.8 = (bf16[2,1344,512]{2,1,0:T(8,128)(2,1)}, bf16[2,1344,512]{2,1,0:T(8,128)(2,1)S(1)}, u32[]{:S(2)}, u32[]{:S(2)}) collective-permute-start(bf16[2,1344,512]{2,1,0:T(8,128)(2,1)} %collective-permute-done.3.refs_0_.block), channel_id=1, source_target_pairs={{0,4},{4,0},{8,12},{12,8},{16,20},{20,16},{24,28},{28,24},{1,5},{5... | collective-permute-start | bytes 8257544 | tf_op jit(solution)/shard_map/ppermute | solution.py:396
  77.1 32.5 %collective-permute-start.7 = (bf16[2,1344,512]{2,1,0:T(8,128)(2,1)}, bf16[2,1344,512]{2,1,0:T(8,128)(2,1)}, u32[]{:S(2)}, u32[]{:S(2)}) collective-permute-start(bf16[2,1344,512]{2,1,0:T(8,128)(2,1)} %collective-permute-done.3.refs_0_.block), channel_id=1, source_target_pairs={{0,1},{5,4},{2,3},{7,6},{8,9},{13,12},{10,11},{15,14},{16,17},{21,... | collective-permute-start | bytes 8257544 | tf_op jit(solution)/shard_map/ppermute | solution.py:407
  80.0 13.1 %collective-permute-start.9 = (bf16[128,1344]{1,0:T(8,128)(2,1)S(1)}, bf16[128,1344]{1,0:T(8,128)(2,1)S(1)}, u32[]{:S(2)}, u32[]{:S(2)}) collective-permute-start(bf16[128,1344]{1,0:T(8,128)(2,1)S(1)} %get-tuple-element.66), channel_id=1, source_target_pairs={{0,24},{4,28},{8,16},{12,20},{16,8},{20,12},{24,0},{28,4},{1,25},{... | collective-permute-start | bytes 1032200 | tf_op jit(solution)/shard_map/ppermute | solution.py:476
  82.4 18.9 %copy-start.8 = (bf16[512,1344]{1,0:T(8,128)(2,1)S(1)}, bf16[512,1344]{1,0:T(8,128)(2,1)}, u32[]{:S(2)}) copy-start(bf16[512,1344]{1,0:T(8,128)(2,1)} %get-tuple-element.120.refs_3_) | copy-start | bytes 4128772
  86.1 14.4 %collective-permute-start.10 = (bf16[128,1344]{1,0:T(8,128)(2,1)S(1)}, bf16[128,1344]{1,0:T(8,128)(2,1)S(1)}, u32[]{:S(2)}, u32[]{:S(2)}) collective-permute-start(bf16[128,1344]{1,0:T(8,128)(2,1)S(1)} %get-tuple-element.69), channel_id=1, source_target_pairs={{0,8},{4,12},{8,0},{12,4},{16,24},{20,28},{24,16},{28,20},{1,9},{5... | collective-permute-start | bytes 1032200 | tf_op jit(solution)/shard_map/ppermute | solution.py:476
  87.2 20.8 %collective-permute-start.11 = (bf16[128,1344]{1,0:T(8,128)(2,1)S(1)}, bf16[128,1344]{1,0:T(8,128)(2,1)S(1)}, u32[]{:S(2)}, u32[]{:S(2)}) collective-permute-start(bf16[128,1344]{1,0:T(8,128)(2,1)S(1)} %get-tuple-element.70), channel_id=1, source_target_pairs={{0,16},{4,20},{8,24},{12,28},{16,0},{20,4},{24,8},{28,12},{1,17},{... | collective-permute-start | bytes 1032200 | tf_op jit(solution)/shard_map/ppermute | solution.py:476
  87.3 21.5 %collective-permute-start.12 = (bf16[128,1344]{1,0:T(8,128)(2,1)S(1)}, bf16[128,1344]{1,0:T(8,128)(2,1)S(1)}, u32[]{:S(2)}, u32[]{:S(2)}) collective-permute-start(bf16[128,1344]{1,0:T(8,128)(2,1)S(1)} %get-tuple-element.71), channel_id=1, source_target_pairs={{0,24},{4,28},{8,16},{12,20},{16,8},{20,12},{24,0},{28,4},{1,25},{... | collective-permute-start | bytes 1032200 | tf_op jit(solution)/shard_map/ppermute | solution.py:476
  93.9 20.2 %collective-permute-start.13 = (bf16[128,1344]{1,0:T(8,128)(2,1)S(1)}, bf16[128,1344]{1,0:T(8,128)(2,1)S(1)}, u32[]{:S(2)}, u32[]{:S(2)}) collective-permute-start(bf16[128,1344]{1,0:T(8,128)(2,1)S(1)} %get-tuple-element.73), channel_id=1, source_target_pairs={{0,8},{4,12},{8,0},{12,4},{16,24},{20,28},{24,16},{28,20},{1,9},{5... | collective-permute-start | bytes 1032200 | tf_op jit(solution)/shard_map/ppermute | solution.py:476
  101.2 13.6 %collective-permute-start.14 = (bf16[128,1344]{1,0:T(8,128)(2,1)S(1)}, bf16[128,1344]{1,0:T(8,128)(2,1)S(1)}, u32[]{:S(2)}, u32[]{:S(2)}) collective-permute-start(bf16[128,1344]{1,0:T(8,128)(2,1)S(1)} %get-tuple-element.74), channel_id=1, source_target_pairs={{0,16},{4,20},{8,24},{12,28},{16,0},{20,4},{24,8},{28,12},{1,17},{... | collective-permute-start | bytes 1032200 | tf_op jit(solution)/shard_map/ppermute | solution.py:476
  115.5 5.4 %collective-permute-start.15 = (bf16[2,1344,512]{2,1,0:T(8,128)(2,1)}, bf16[2,1344,512]{2,1,0:T(8,128)(2,1)}, u32[]{:S(2)}, u32[]{:S(2)}) collective-permute-start(bf16[2,1344,512]{2,1,0:T(8,128)(2,1)} %collective-permute-done.7), channel_id=1, source_target_pairs={{0,4},{4,0},{8,12},{12,8},{16,20},{20,16},{24,28},{28,24},{1,5},{5... | collective-permute-start | bytes 8257544 | tf_op jit(solution)/shard_map/ppermute | solution.py:396
  115.5 12.9 %collective-permute-start.16 = (bf16[128,1344]{1,0:T(8,128)(2,1)}, bf16[128,1344]{1,0:T(8,128)(2,1)S(1)}, u32[]{:S(2)}, u32[]{:S(2)}) collective-permute-start(bf16[128,1344]{1,0:T(8,128)(2,1)} %copy-done.30), channel_id=1, source_target_pairs={{0,24},{4,28},{8,16},{12,20},{16,8},{20,12},{24,0},{28,4},{1,25},{... | collective-permute-start | bytes 1032200 | tf_op jit(solution)/shard_map/ppermute | solution.py:476
  124.9 11.3 %collective-permute-start.17 = (bf16[128,1344]{1,0:T(8,128)(2,1)S(1)}, bf16[128,1344]{1,0:T(8,128)(2,1)S(1)}, u32[]{:S(2)}, u32[]{:S(2)}) collective-permute-start(bf16[128,1344]{1,0:T(8,128)(2,1)S(1)} %get-tuple-element.80), channel_id=1, source_target_pairs={{0,8},{4,12},{8,0},{12,4},{16,24},{20,28},{24,16},{28,20},{1,9},{5... | collective-permute-start | bytes 1032200 | tf_op jit(solution)/shard_map/ppermute | solution.py:476
  126.0 17.9 %collective-permute-start.18 = (bf16[128,1344]{1,0:T(8,128)(2,1)S(1)}, bf16[128,1344]{1,0:T(8,128)(2,1)S(1)}, u32[]{:S(2)}, u32[]{:S(2)}) collective-permute-start(bf16[128,1344]{1,0:T(8,128)(2,1)S(1)} %get-tuple-element.81), channel_id=1, source_target_pairs={{0,16},{4,20},{8,24},{12,28},{16,0},{20,4},{24,8},{28,12},{1,17},{... | collective-permute-start | bytes 1032200 | tf_op jit(solution)/shard_map/ppermute | solution.py:476
  126.6 17.2 %collective-permute-start.19 = (bf16[128,1344]{1,0:T(8,128)(2,1)S(1)}, bf16[128,1344]{1,0:T(8,128)(2,1)S(1)}, u32[]{:S(2)}, u32[]{:S(2)}) collective-permute-start(bf16[128,1344]{1,0:T(8,128)(2,1)S(1)} %get-tuple-element.82), channel_id=1, source_target_pairs={{0,24},{4,28},{8,16},{12,20},{16,8},{20,12},{24,0},{28,4},{1,25},{... | collective-permute-start | bytes 1032200 | tf_op jit(solution)/shard_map/ppermute | solution.py:476
  155.9 14.4 %collective-permute-start.20 = (bf16[2,2,512,128]{3,2,1,0:T(8,128)(2,1)S(1)}, bf16[2,2,512,128]{3,2,1,0:T(8,128)(2,1)S(1)}, u32[]{:S(2)}, u32[]{:S(2)}) collective-permute-start(bf16[2,2,512,128]{3,2,1,0:T(8,128)(2,1)S(1)} %get-tuple-element.88), channel_id=1, source_target_pairs={{8,0},{12,4},{16,8},{20,12},{24,16},{28,20},{9,1},{13,5},{17,9},{2... | collective-permute-start | bytes 1572872 | tf_op jit(solution)/shard_map/ppermute | solution.py:391
  176.4 17.0 %copy-start.11 = (f32[128,1344]{1,0:T(8,128)S(1)}, f32[128,1344]{1,0:T(8,128)}, u32[]{:S(2)}) copy-start(f32[128,1344]{1,0:T(8,128)} %copy-done.10) | copy-start | bytes 2064388
  176.4 17.0 %copy-start.13 = (bf16[128,1344]{1,0:T(8,128)(2,1)S(1)}, bf16[128,1344]{1,0:T(8,128)(2,1)}, u32[]{:S(2)}) copy-start(bf16[128,1344]{1,0:T(8,128)(2,1)} %copy-done.12) | copy-start | bytes 1032196
  176.4 17.0 %copy-start.15 = (bf16[128,1344]{1,0:T(8,128)(2,1)S(1)}, bf16[128,1344]{1,0:T(8,128)(2,1)}, u32[]{:S(2)}) copy-start(bf16[128,1344]{1,0:T(8,128)(2,1)} %copy-done.14) | copy-start | bytes 1032196
  176.4 17.0 %copy-start.17 = (bf16[128,1344]{1,0:T(8,128)(2,1)S(1)}, bf16[128,1344]{1,0:T(8,128)(2,1)}, u32[]{:S(2)}) copy-start(bf16[128,1344]{1,0:T(8,128)(2,1)} %copy-done.16) | copy-start | bytes 1032196
  176.4 17.0 %copy-start.19 = (bf16[128,1344]{1,0:T(8,128)(2,1)S(1)}, bf16[128,1344]{1,0:T(8,128)(2,1)}, u32[]{:S(2)}) copy-start(bf16[128,1344]{1,0:T(8,128)(2,1)} %copy-done.18) | copy-start | bytes 1032196
  176.4 17.0 %copy-start.21 = (bf16[128,1344]{1,0:T(8,128)(2,1)S(1)}, bf16[128,1344]{1,0:T(8,128)(2,1)}, u32[]{:S(2)}) copy-start(bf16[128,1344]{1,0:T(8,128)(2,1)} %copy-done.20) | copy-start | bytes 1032196
  176.5 19.9 %collective-permute-start.21 = (bf16[512,512]{1,0:T(8,128)(2,1)S(1)}, bf16[512,512]{1,0:T(8,128)(2,1)S(1)}, u32[]{:S(2)}, u32[]{:S(2)}) collective-permute-start(bf16[512,512]{1,0:T(8,128)(2,1)S(1)} %broadcast_select_fusion.5), channel_id=1, source_target_pairs={{0,4},{4,0},{8,12},{12,8},{16,20},{20,16},{24,28},{28,24},{1,5},{5... | collective-permute-start | bytes 1572872 | tf_op jit(solution)/shard_map/ppermute | solution.py:396
  176.6 11.3 %collective-permute-start.22 = (bf16[2,1,512,128]{3,2,1,0:T(8,128)(2,1)S(1)}, bf16[2,1,512,128]{3,2,1,0:T(8,128)(2,1)S(1)}, u32[]{:S(2)}, u32[]{:S(2)}) collective-permute-start(bf16[2,1,512,128]{3,2,1,0:T(8,128)(2,1)S(1)} %get-tuple-element.94), channel_id=1, source_target_pairs={{8,0},{12,4},{16,8},{20,12},{24,16},{28,20},{9,1},{13,5},{17,9},{2... | collective-permute-start | bytes 786440 | tf_op jit(solution)/shard_map/ppermute | solution.py:391
  178.2 14.8 %collective-permute-start.23 = (bf16[2,1,512,128]{3,2,1,0:T(8,128)(2,1)S(1)}, bf16[2,1,512,128]{3,2,1,0:T(8,128)(2,1)S(1)}, u32[]{:S(2)}, u32[]{:S(2)}) collective-permute-start(bf16[2,1,512,128]{3,2,1,0:T(8,128)(2,1)S(1)} %get-tuple-element.95), channel_id=1, source_target_pairs={{8,0},{12,4},{16,8},{20,12},{24,16},{28,20},{9,1},{13,5},{17,9},{2... | collective-permute-start | bytes 786440 | tf_op jit(solution)/shard_map/ppermute | solution.py:391
  193.2 4.4 %collective-permute-start.24 = (bf16[2,2,512,128]{3,2,1,0:T(8,128)(2,1)S(1)}, bf16[2,2,512,128]{3,2,1,0:T(8,128)(2,1)S(1)}, u32[]{:S(2)}, u32[]{:S(2)}) collective-permute-start(bf16[2,2,512,128]{3,2,1,0:T(8,128)(2,1)S(1)} %get-tuple-element.97), channel_id=1, source_target_pairs={{0,4},{4,0},{8,12},{12,8},{16,20},{20,16},{24,28},{28,24},{1,5},{5... | collective-permute-start | bytes 1572872 | tf_op jit(solution)/shard_map/ppermute | solution.py:396
  (31 other events, 155.9 us)

commit v2 on v1

--- a/solution.py
+++ b/solution.py
@@ -248,31 +248,52 @@
     )(*blocks, *weights, *([] if total is None else [total]))
 
 
-def terms_kernel(count, rows_ref, block, *outs):
-    _, cols, tok = block.shape
-    share = rows_ref.shape[0] // count
-    for at in range(0, cols, TILE):
-        here = slice(at, min(at + TILE, cols))
-        term = dot(rows_ref[:, :tok], block[0, here, :], NT) + dot(rows_ref[:, tok:], block[1, here, :], NT)
-        for s in range(count):
-            outs[s][:, here] = term[s * share : (s + 1) * share].astype(outs[s].dtype)
-
-
-def make_terms(rows, block, count):
-    cols = block.shape[1]
-    share = rows.shape[0] // count
-    whole = lambda *shape: pl.BlockSpec(shape, lambda i: (0,) * len(shape))
-    shapes = [jax.ShapeDtypeStruct((share, cols), jnp.float32 if s == 0 else jnp.bfloat16) for s in range(count)]
-    return pl.pallas_call(
-        functools.partial(terms_kernel, count),
+def terms_kernel(orders, count, rows_ref, *refs):
+    number = len(orders)
+    blocks, waiting = refs[:number], refs[number : number + 3 * count]
+    outs, passed = refs[number + 3 * count : number + 3 * count + 3 * number], refs[number + 3 * count + 3 * number :]
+    for n in range(count):
+        keep, near, got = waiting[3 * n : 3 * n + 3]
+        cols = keep.shape[1]
+        passed[2 * n][...] = keep[...] + got[:, :cols].astype(jnp.float32)
+        passed[2 * n + 1][...] = (near[...] + got[:, cols:].astype(jnp.float32)).astype(jnp.bfloat16)
+    for n, (block, first) in enumerate(zip(blocks, orders)):
+        _, cols, tok = block.shape
+        share = rows_ref.shape[0] // 4
+        keep, near, send = outs[3 * n : 3 * n + 3]
+        for at in range(0, cols, TILE):
+            end = min(at + TILE, cols)
+            term = dot(rows_ref[:, :tok], block[0, at:end, :], NT) + dot(rows_ref[:, tok:], block[1, at:end, :], NT)
+            parts = [term[s * share : (s + 1) * share] for s in range(4)]
+            keep[:, at:end] = parts[0]
+            near[:, at:end] = parts[3 - first]
+            send[:, at:end] = parts[first].astype(jnp.bfloat16)
+            send[:, cols + at : cols + end] = parts[3].astype(jnp.bfloat16)
+
+
+def make_terms(rows, blocks, orders, waiting):
+    share = rows.shape[0] // 4
+    flat = [x for group in waiting for x in group]
+    whole = lambda x: pl.BlockSpec(x.shape, lambda i: (0,) * len(x.shape))
+    shapes = []
+    for block in blocks:
+        cols = block.shape[1]
+        shapes += [jax.ShapeDtypeStruct((share, cols), jnp.float32)] * 2
+        shapes.append(jax.ShapeDtypeStruct((share, 2 * cols), jnp.bfloat16))
+    for keep, _, _ in waiting:
+        shapes += [jax.ShapeDtypeStruct(keep.shape, jnp.float32), jax.ShapeDtypeStruct(keep.shape, jnp.bfloat16)]
+    out = pl.pallas_call(
+        functools.partial(terms_kernel, orders, len(waiting)),
         grid=(1,),
-        in_specs=[whole(*rows.shape), whole(*block.shape)],
-        out_specs=[whole(share, cols)] * count,
+        in_specs=[whole(x) for x in (rows, *blocks, *flat)],
+        out_specs=[whole(x) for x in shapes],
         out_shape=shapes,
         compiler_params=pltpu.CompilerParams(vmem_limit_bytes=VMEM_LIMIT),
         cost_estimate=CHEAP,
         name="weight_terms",
-    )(rows, block)
+    )(rows, *blocks, *flat)
+    cut = 3 * len(blocks)
+    return [list(out[n : n + 3]) for n in range(0, cut, 3)], [list(out[n : n + 2]) for n in range(cut, len(out), 2)]
 
 
 def close_kernel(groups, core_ref, from_low_ref, *refs):
@@ -351,35 +372,30 @@
     )(where, knocked, patch_start, keep, taken)
 
 
-def place_terms_kernel(size, at_ref, *refs):
+def place_terms_kernel(at_ref, *refs):
     out_ref = refs[-1]
-    cols = out_ref.shape[1] // size
-    each = (len(refs) - 1) // size
+    size = (len(refs) - 1) // 2
+    cols = refs[0].shape[1]
     for n in range(size):
-        group = refs[n * each : (n + 1) * each]
         for j in range(size):
 
             @pl.when(at_ref[n] == j)
             def _():
-                total = group[0][...]
-                for got in group[1:]:
-                    total = total + got[...].astype(jnp.float32)
-                out_ref[:, j * cols : (j + 1) * cols] = total
-
-
-def place_terms(at, groups):
-    flat = [x for group in groups for x in group]
+                out_ref[:, j * cols : (j + 1) * cols] = refs[2 * n][...] + refs[2 * n + 1][...].astype(jnp.float32)
+
+
+def place_terms(at, terms):
+    flat = [x for term in terms for x in term]
     share, cols = flat[0].shape
-    shape = (share, len(groups) * cols)
     return pl.pallas_call(
-        functools.partial(place_terms_kernel, len(groups)),
+        place_terms_kernel,
         grid_spec=pltpu.PrefetchScalarGridSpec(
             num_scalar_prefetch=1,
             grid=(1,),
             in_specs=[pl.BlockSpec(x.shape, lambda i, c: (0, 0)) for x in flat],
-            out_specs=pl.BlockSpec(shape, lambda i, c: (0, 0)),
+            out_specs=pl.BlockSpec((share, cols * len(terms)), lambda i, c: (0, 0)),
         ),
-        out_shape=jax.ShapeDtypeStruct(shape, jnp.float32),
+        out_shape=jax.ShapeDtypeStruct((share, cols * len(terms)), jnp.float32),
         compiler_params=pltpu.CompilerParams(vmem_limit_bytes=VMEM_LIMIT),
         cost_estimate=CHEAP,
         name="place_terms",
@@ -425,15 +441,16 @@
     half_q, half_kv = queries.shape[1] // 2, cached_keys.shape[1] // 2
     dyn = lax.dynamic_slice_in_dim
 
+    fast = n_head == 4 and chips == 4
     partner = swap_cores(out_grad)
     own_block = jnp.stack([jnp.where(low, out_grad, partner), jnp.where(low, partner, out_grad)])
-    if n_head == 4:
+    if fast:
         up, down = [((0, i), (0, (i + 1) % 4)) for i in range(4)], [((1, i), (1, (i - 1) % 4)) for i in range(4)]
-        direct = (move(own_block, up + down),)
-        distances, last = [jnp.where(low, 3, 1), jnp.where(low, 1, 3)], 2
+        direct = move(own_block, up + down)
+        order = [0, jnp.where(low, 3, 1), jnp.where(low, 1, 3), 2]
     else:
-        direct = tuple(turn(own_block, s) for s in range(1, n_head - 1))
-        distances, last = [n_head - s for s in range(1, n_head - 1)], 1
+        direct = [turn(own_block, s) for s in range(1, n_head)]
+        order = [(n_head - s) % n_head for s in range(n_head)]
 
     positions = place * tok + jnp.arange(tok, dtype=jnp.int32)
     chosen = (jnp.repeat(knocked, head_size)[None, :] == 1) & (
@@ -455,7 +472,6 @@
     packet = jnp.concatenate([jnp.where(low, mine, other), jnp.where(low, other, mine)], axis=0)
     before = shift(packet[:, half_q:], 2)
 
-    order = [0, *distances, last]
     weight_half = dyn(out_weight, core * half_q, half_q, 0)
     weights = [dyn(weight_half, ((z + d) % n_head) * cols, cols, 1) for d in order]
     core_id = core[None].astype(jnp.int32)
@@ -463,72 +479,77 @@
     before = after(before, grads, weights)
 
     attention, attended = forward(chip[None].astype(jnp.int32), packet, before, head_size)
-    share = out_weight.shape[0] // n_ctx
-    parity = attended.reshape(chips // 2, 2, share, 2 * tok)
-    kept, given = dyn(parity, core, 1, 1)[:, 0], dyn(parity, 1 - core, 1, 1)[:, 0]
-    taken = swap_cores(given)
-    by_chip = jnp.concatenate([jnp.where(low, kept, taken), jnp.where(low, taken, kept)], axis=0)
-    by_distance = jnp.concatenate([dyn(by_chip, chip ^ s, 1, 0) for s in range(chips)], axis=0)
-    by_distance = by_distance.reshape(chips * share, 2 * tok)
-
-    def send_terms(block):
-        kept_term, *sent = make_terms(by_distance, block, chips)
-        got = [lax.ppermute(x, "ctx", [(i, i ^ (2 * s + 2)) for i in range(n_ctx)]) for s, x in enumerate(sent)]
-        return [kept_term, *got], sent
-
-    terms = []
-
-    def wait(value, *others, on=(), since=slice(None)):
-        value, _, got = lax.optimization_barrier((value, others, [terms[n][since] for n in on]))
-        for n, g in zip(on, got):
-            terms[n][since] = g
-        return value
-
-    term, sent = send_terms(own_block)
-    terms.append(term)
-    direct = wait(direct, sent, on=[0], since=slice(1, 3))
-    if n_head == 4:
-        hops = [((i % 2, i), (i % 2, j)) for i, j in [(0, 1), (1, 0), (2, 3), (3, 2)]]
-        final = move(direct[0], hops)
-        blocks = [direct[0], swap_cores(direct[0])]
+    if fast:
+        share = out_weight.shape[0] // n_ctx
+        parity = attended.reshape(chips // 2, 2, share, 2 * tok)
+        kept, given = dyn(parity, core, 1, 1)[:, 0], dyn(parity, 1 - core, 1, 1)[:, 0]
+        taken = swap_cores(given)
+        by_chip = jnp.concatenate([jnp.where(low, kept, taken), jnp.where(low, taken, kept)], axis=0)
+        by_distance = jnp.concatenate([dyn(by_chip, chip ^ s, 1, 0) for s in range(chips)], axis=0)
+        by_distance = by_distance.reshape(chips * share, 2 * tok)
+
+        def exchange(shard, distance):
+            return lax.ppermute(shard, "ctx", [(i, i ^ (2 * distance)) for i in range(n_ctx)])
+
+        direct = after(direct, by_distance)
+        final = move(direct, [((i % 2, i), (i % 2, j)) for i, j in [(0, 1), (1, 0), (2, 3), (3, 2)]])
+        blocks = [direct, swap_cores(direct)]
+        (own_terms, up_terms, down_terms), _ = make_terms(by_distance, [own_block, *blocks], (1, 1, 2), [])
+        own_got, up_got, down_got = exchange(own_terms[2], 1), exchange(up_terms[2], 1), exchange(down_terms[2], 2)
+        grads = add_grads(blocks, weights[1:3], grads, jnp.float32)
+
+        final, own_got, down_got, grads = lax.optimization_barrier((final, own_got, down_got, grads))
+        final = jnp.where(core == 1 - z % 2, final, swap_cores(final))
+        (last_terms,), (own_sum, down_sum) = make_terms(
+            by_distance, [final], (2,), [(*own_terms[:2], own_got), (*down_terms[:2], down_got)]
+        )
+        last_got = exchange(last_terms[2], 2)
+        own_sum[1], down_sum[1] = exchange(own_sum[1], 2), exchange(down_sum[1], 1)
+        final, _, up_got = lax.optimization_barrier((final, last_terms[2], up_got))
+        grads = add_grads([final], weights[3:], grads, jnp.bfloat16)
     else:
-        final = turn(own_block, -1)
-        blocks = list(direct)
-    for n, block in enumerate(blocks):
-        block = after(block, sent)
-        term, sent = send_terms(block)
-        terms.append(term)
-    grads = add_grads(blocks, weights[1:-1], grads, jnp.float32)
-
-    final = wait(final, grads, sent, on=[0, 1], since=slice(1, None))
-    final = wait(final, on=[2], since=slice(1, 3))
-    if n_head == 4:
-        final = jnp.where(core == 1 - z % 2, final, swap_cores(final))
-    term, sent = send_terms(final)
-    terms.append(term)
-    final = wait(final, sent, on=[2], since=slice(3, None))
-    grads = add_grads([final], weights[-1:], grads, jnp.bfloat16)
-    grads = wait(grads, on=[3], since=slice(1, None))
+        blocks = [own_block, *direct]
+        grads = add_grads(blocks[1:], weights[1:], grads, jnp.float32).astype(jnp.bfloat16)
+        term = jnp.stack([sum(dot(attended[:, i * tok : (i + 1) * tok], x[i], NT) for i in (0, 1)) for x in blocks])
+        term = jnp.concatenate([dyn(term, (z - j) % n_head, 1, 0)[0] for j in range(n_head)], axis=1)
+        term = jnp.concatenate([jnp.where(low, term, 0.0), jnp.where(low, 0.0, term)], axis=0)
+        weight_grad = lax.psum_scatter(term, "ctx", scatter_dimension=0, tiled=True)
     all_groups = (0, packet.shape[1] // (4 * head_size))
     query_low, prev_low, carry = backward(0, all_groups, packet, before, attention, grads, None, head_size)
+    if fast:
+        sent = (own_sum[1], down_sum[1])
+        query_low, prev_low, carry, last_got, sent = lax.optimization_barrier(
+            (query_low, prev_low, carry, last_got, sent)
+        )
+        own_sum[1], down_sum[1] = sent
+        waiting = [(*up_terms[:2], up_got), (*last_terms[:2], last_got)]
+        _, (up_sum, last_sum) = make_terms(by_distance, [], (), waiting)
+        prev_low = after(prev_low, last_sum[1])
+        up_sum[1], last_sum[1] = exchange(up_sum[1], 2), exchange(last_sum[1], 1)
     from_low = shift(prev_low, -2)
-    parts = []
+    parts, from_high = [], []
     for g in range(all_groups[1]):
-        if g > 0 and g == all_groups[1] - 1:
-            grads, from_low = lax.optimization_barrier((grads, from_low))
-        parts.append(backward(1, (g, 1), packet, before, attention, grads, carry, head_size))
+        part = backward(1, (g, 1), packet, before, attention, grads, carry, head_size)
+        if g > 0:
+            part, from_low, from_high = lax.optimization_barrier((part, from_low, from_high))
+        parts.append(part)
+        from_high.append(shift(part[1], -2))
     query_high = jnp.concatenate([part[0] for part in parts], axis=1)
 
-    weight_grad = place_terms(jnp.stack([(z + d) % n_head for d in order]).astype(jnp.int32), terms)
+    if fast:
+        at = jnp.stack([(z + d) % n_head for d in order]).astype(jnp.int32)
+        weight_grad = place_terms(at, [own_sum, up_sum, down_sum, last_sum])
 
     query_kept = jnp.where(low, query_low, query_high)
     query_taken = swap_cores(jnp.where(low, query_high, query_low))
     query_grad = jnp.concatenate(
         [jnp.where(low, query_kept, query_taken), jnp.where(low, query_taken, query_kept)], axis=1
     )
-    keep, send = close_sums(core_id, from_low, [part[2] for part in parts], [shift(part[1], -2) for part in parts])
-    where = jnp.stack([core, place * tok]).astype(jnp.int32)
-    key_grad, value_grad, patch_grad = place_sums(where, knocked, patch_start, keep, swap_cores(send))
+    from_high = after(from_high, weight_grad)
+    keep, send = close_sums(core_id, from_low, [part[2] for part in parts], from_high)
+    rows_at = jnp.stack([core, place * tok]).astype(jnp.int32)
+    taken = after(swap_cores(send), query_grad)
+    key_grad, value_grad, patch_grad = place_sums(rows_at, knocked, patch_start, keep, taken)
     return (query_grad, key_grad, value_grad, patch_grad, weight_grad)
 
 

time: 201 us -> 191 us (0.950)
  local copies, waits for them, and re-layouts: 23.3 us -> 16.3 us
  starting transfers between devices: 31.3 us -> 28.7 us
    ppermute x2, waiting for transfers between devices: 0.01 us -> 22.9 us  [move(): return lax.ppermute(shard, ('ctx', 'head'), places)]
    ppermute x12 -> x8, waiting for transfers between devices: 30.8 us -> 16.9 us  [exchange(): lax.ppermute(shard, 'ctx', [(i, i ^ 2 * distance) for i in range(n_ctx)])]
    ppermute x4, waiting for transfers between devices: 28.4 us -> 16.2 us  [shift(): lax.ppermute(shard, 'ctx', [(i, i + by) for i in range(size) if 0 <= i +...]
    unnamed x77 -> x85, local copies, waits for them, and re-layouts: 12.5 us -> 5.52 us
    ppermute x12 -> x8, starting transfers between devices: 15.8 us -> 10.7 us  [exchange(): lax.ppermute(shard, 'ctx', [(i, i ^ 2 * distance) for i in range(n_ctx)])]
    ppermute x7, starting transfers between devices: 1.94 us -> 4.39 us  [swap_cores(): lax.ppermute(shard, 'ctx', [(i, i ^ 1) for i in range(size) if only is No...]
    ppermute x7, waiting for transfers between devices: 5.88 us -> 7.92 us  [swap_cores(): lax.ppermute(shard, 'ctx', [(i, i ^ 1) for i in range(size) if only is No...]
    pallas_call x5 -> x4, Pallas kernels: 13.9 us -> 14.6 us  [the longest x3 11.8 us: make_terms(): pl.pallas_call(functools.partial(terms_kernel, orders, len(waiting)), gri...]
  transfers between devices with their start and end apart: 25 -> 21, of which waited for: 12 -> 14; matrix products, arithmetic and copies ran while one was open for 11% -> 12% of each run, Pallas kernels for 24% -> 34%
where the time goes in v2:
time: 191 us; the launch traced here: 190 us
  Pallas kernels  67.9 us (36%)
  waiting for transfers between devices  63.9 us (33%)
  starting transfers between devices  28.7 us (15%)
  local copies, waits for them, and re-layouts  16.3 us (9%)
  other arithmetic  11.9 us (6%)
    pallas_call x3, Pallas kernels, backward(): pl.pallas_call(functools.partial(backward_kernel, phase), grid=(count, ti...  23.2 us
    ppermute x2, waiting for transfers between devices, move(): return lax.ppermute(shard, ('ctx', 'head'), places)  22.9 us
    ppermute x8, waiting for transfers between devices, exchange(): lax.ppermute(shard, 'ctx', [(i, i ^ 2 * distance) for i in range(n_ctx)])  16.9 us
    ppermute x4, waiting for transfers between devices, shift(): lax.ppermute(shard, 'ctx', [(i, i + by) for i in range(size) if 0 <= i +...  16.2 us
    pallas_call x1, Pallas kernels, forward(): pl.pallas_call(forward_kernel, grid_spec=grid_spec, out_shape=[jax.ShapeD...  15 us
    pallas_call x3, Pallas kernels, add_grads(): pl.pallas_call(functools.partial(grads_kernel, number), grid=(2 * tiles,)...  12.9 us
    pallas_call x3, Pallas kernels, make_terms(): pl.pallas_call(functools.partial(terms_kernel, orders, len(waiting)), gri...  11.8 us
    ppermute x8, starting transfers between devices, exchange(): lax.ppermute(shard, 'ctx', [(i, i ^ 2 * distance) for i in range(n_ctx)])  10.7 us
  transfers between devices with their start and end apart: 21, of which 14 were waited for; matrix products, arithmetic and copies ran while one was open for 12% of the time, Pallas kernels for 34%

profile of v2, /device:TPU:0, one launch (start us, length us, event | category | flops | bytes accessed | tf_op | source)
XLA Modules:
  0.0 190.0 jit_solution(11340832316741825069)
XLA Ops:
  6.1 1.8 pad_maximum_fusion.refs_0_
  7.8 2.7 %collective-permute-start.3 = (bf16[2,1344,512]{2,1,0:T(8,128)(2,1)}, bf16[2,1344,512]{2,1,0:T(8,128)(2,1)}, u32[]{:S(2)}, u32[]{:S(2)}) collective-permute-start(bf16[2,1344,512]{2,1,0:T(8,128)(2,1)} %pad_maximum_fusion.refs_0_), channel_id=1, source_target_pairs={{0,1},{1,2},{2,3},{3,0},{4,7},{5,4},{6,5},{7,6},{8,9},{9,10},{10,1... | collective-permute-start | bytes 8257544 | tf_op jit(solution)/shard_map/ppermute | solution.py:423
  10.6 1.7 broadcast_select_fusion.2
  13.4 3.4 %collective-permute-start.1 = (bf16[1024,512]{1,0:T(8,128)(2,1)}, bf16[1024,512]{1,0:T(8,128)(2,1)S(1)}, u32[]{:S(2)}, u32[]{:S(2)}) collective-permute-start(bf16[1024,512]{1,0:T(8,128)(2,1)} %fusion), channel_id=1, source_target_pairs={{0,8},{4,12},{8,16},{12,20},{16,24},{20,28},{1,9},{5,13},{9,17},{1... | collective-permute-start | bytes 3145736 | tf_op jit(solution)/shard_map/ppermute | solution.py:407
  17.0 8.4 %fusion.5 = (bf16[512,1344]{1,0:T(8,128)(2,1)}, bf16[512,1344]{1,0:T(8,128)(2,1)}, bf16[512,1344]{1,0:T(8,128)(2,1)S(1)}, bf16[512,1344]{1,0:T(8,128)(2,1)}) fusion(bf16[1024,5376]{1,0:T(8,128)(2,1)} %param.13, s32[]{:T(128)S(6)} %select_n.182, s32[]{:T(128)S(6)} %select_n.196, s32[]{:T(128)S(6)} %select_n.189, s32[]{:T(128)S(6)} %select_n.185, s32[]{:T(128)S(6)} %select_n.193), kind=kLoop, calls=%fused_computation.48 | loop fusion | bytes 11010068 | tf_op jit(solution)/shard_map/dynamic_slice | solution.py:476
  25.6 4.7 %out_grads.3.refs_4_ = f32[512,1024]{1,0:T(8,128)S(1)} custom-call(bf16[2,1344,512]{2,1,0:T(8,128)(2,1)} %pad_maximum_fusion.refs_0_, bf16[512,1344]{1,0:T(8,128)(2,1)S(1)} %get-tuple-element.125.refs_1_), custom_call_target="tpu_custom_call" | custom-call | flops 1 | bytes 1 | tf_op jit(solution)/shard_map/out_grads/pallas_call | solution.py:237
  31.6 7.9 %collective-permute-done.1.pk_ref.pv_ref = bf16[1024,512]{1,0:T(8,128)(2,1)S(1)} collective-permute-done((bf16[1024,512]{1,0:T(8,128)(2,1)}, bf16[1024,512]{1,0:T(8,128)(2,1)S(1)}, u32[]{:S(2)}, u32[]{:S(2)}) %collective-permute-start.1) | collective-permute-done | bytes 1048608 | tf_op jit(solution)/shard_map/ppermute | solution.py:407
  39.5 15.0 %attention_forward.1 = (f32[2,4,1280,512]{3,2,1,0:T(8,128)}, bf16[512,1024]{1,0:T(8,128)(2,1)S(1)}) custom-call(s32[1]{0:T(128)} %bitcast.5.chip_ref, bf16[1024,1024]{1,0:T(8,128)(2,1)S(1)} %pad_maximum_fusion.1.q_ref.k_ref.v_ref, bf16[1024,1024]{1,0:T(8,128)(2,1)S(1)} %pad_maximum_fusion.1.q_ref.k_ref.v_ref, ...), custom_call_target="tpu_custom_call" | custom-call | flops 1 | bytes 1 | tf_op jit(solution)/shard_map/attention_forward/pallas_call | solution.py:102
  55.9 1.7 collective-permute-done.4
  59.2 14.1 %collective-permute-done.3.refs_1_.refs_0_ = bf16[2,1344,512]{2,1,0:T(8,128)(2,1)} collective-permute-done((bf16[2,1344,512]{2,1,0:T(8,128)(2,1)}, bf16[2,1344,512]{2,1,0:T(8,128)(2,1)}, u32[]{:S(2)}, u32[]{:S(2)}) %collective-permute-start.3) | collective-permute-done | bytes 2752544 | tf_op jit(solution)/shard_map/ppermute | solution.py:423
  73.3 3.2 %collective-permute-start.5 = (bf16[2,1344,512]{2,1,0:T(8,128)(2,1)}, bf16[2,1344,512]{2,1,0:T(8,128)(2,1)}, u32[]{:S(2)}, u32[]{:S(2)}) collective-permute-start(bf16[2,1344,512]{2,1,0:T(8,128)(2,1)} %collective-permute-done.3.refs_1_.refs_0_), channel_id=1, source_target_pairs={{0,1},{5,4},{2,3},{7,6},{8,9},{13,12},{10,11},{15,14},{16,17},{21,... | collective-permute-start | bytes 8257544 | tf_op jit(solution)/shard_map/ppermute | solution.py:423
  76.5 2.1 %collective-permute-done.6.refs_2_.refs_1_ = bf16[2,1344,512]{2,1,0:T(8,128)(2,1)S(1)} collective-permute-done((bf16[2,1344,512]{2,1,0:T(8,128)(2,1)}, bf16[2,1344,512]{2,1,0:T(8,128)(2,1)S(1)}, u32[]{:S(2)}, u32[]{:S(2)}) %collective-permute-start.6) | collective-permute-done | bytes 2752544 | tf_op jit(solution)/shard_map/ppermute | solution.py:412
  78.6 8.4 %weight_terms.3 = (f32[128,1344]{1,0:T(8,128)S(1)}, f32[128,1344]{1,0:T(8,128)S(1)}, bf16[128,2688]{1,0:T(8,128)(2,1)S(1)}, f32[128,1344]{1,0:T(8,128)S(1)}, f32...) custom-call(bf16[512,1024]{1,0:T(8,128)(2,1)S(1)} %bitcast.25, ...), custom_call_target="tpu_custom_call" | custom-call | flops 1 | bytes 1 | tf_op jit(solution)/shard_map/weight_terms/pallas_call | solution.py:285
  90.1 5.4 %out_grads.4.refs_2_ = f32[512,1024]{1,0:T(8,128)S(1)} custom-call(bf16[2,1344,512]{2,1,0:T(8,128)(2,1)} %collective-permute-done.3.refs_1_.refs_0_, bf16[2,1344,512]{2,1,0:T(8,128)(2,1)S(1)} %collective-permute-done.6.refs_2_.refs_1_, bf16[512,1344]{1,0:T(8,128)(2,1)S(1)} %copy-done.7, bf16[512,1344]{1,0:T(8,128)(2,1)S(1)} %copy-done.8, ...), custom_call_target="tpu_custom_call" | custom-call | flops 1 | bytes 1 | tf_op jit(solution)/shard_map/out_grads/pallas_call | solution.py:237
  96.9 8.8 %collective-permute-done.5 = bf16[2,1344,512]{2,1,0:T(8,128)(2,1)} collective-permute-done((bf16[2,1344,512]{2,1,0:T(8,128)(2,1)}, bf16[2,1344,512]{2,1,0:T(8,128)(2,1)}, u32[]{:S(2)}, u32[]{:S(2)}) %collective-permute-start.5) | collective-permute-done | bytes 2752544 | tf_op jit(solution)/shard_map/ppermute | solution.py:423
  107.5 2.2 %collective-permute-start.9 = (bf16[2,1344,512]{2,1,0:T(8,128)(2,1)}, bf16[2,1344,512]{2,1,0:T(8,128)(2,1)}, u32[]{:S(2)}, u32[]{:S(2)}) collective-permute-start(bf16[2,1344,512]{2,1,0:T(8,128)(2,1)} %collective-permute-done.5), channel_id=1, source_target_pairs={{0,4},{4,0},{8,12},{12,8},{16,20},{20,16},{24,28},{28,24},{1,5},{5... | collective-permute-start | bytes 8257544 | tf_op jit(solution)/shard_map/ppermute | solution.py:412
  111.3 3.5 %collective-permute-done.9 = bf16[2,1344,512]{2,1,0:T(8,128)(2,1)} collective-permute-done((bf16[2,1344,512]{2,1,0:T(8,128)(2,1)}, bf16[2,1344,512]{2,1,0:T(8,128)(2,1)}, u32[]{:S(2)}, u32[]{:S(2)}) %collective-permute-start.9) | collective-permute-done | bytes 2752544 | tf_op jit(solution)/shard_map/ppermute | solution.py:412
  114.7 2.1 %broadcast_select_fusion.refs_0_ = bf16[2,1344,512]{2,1,0:T(8,128)(2,1)S(1)} fusion(bf16[2,1344,512]{2,1,0:T(8,128)(2,1)} %collective-permute-done.5, bf16[2,1344,512]{2,1,0:T(8,128)(2,1)} %collective-permute-done.9, pred[]{:T(512)S(6)} %eq.36), kind=kLoop, calls=%fused_computation.1 | loop fusion | flops 1376256 | bytes 8257537 | tf_op jit(solution)/shard_map/jit(_where)/select_n | solution.py:502
  116.9 3.0 %weight_terms.4 = (f32[128,1344]{1,0:T(8,128)S(1)}, f32[128,1344]{1,0:T(8,128)S(1)}, bf16[128,2688]{1,0:T(8,128)(2,1)}, f32[128,1344]{1,0:T(8,128)S(1)}, bf16[12...) custom-call(bf16[512,1024]{1,0:T(8,128)(2,1)S(1)} %bitcast.26, ...), custom_call_target="tpu_custom_call" | custom-call | flops 1 | bytes 1 | tf_op jit(solution)/shard_map/weight_terms/pallas_call | solution.py:285
  123.4 4.9 %collective-permute-done.10.refs_2_ = bf16[128,2688]{1,0:T(8,128)(2,1)S(1)} collective-permute-done((bf16[128,2688]{1,0:T(8,128)(2,1)}, bf16[128,2688]{1,0:T(8,128)(2,1)S(1)}, u32[]{:S(2)}, u32[]{:S(2)}) %collective-permute-start.10) | collective-permute-done | bytes 688160 | tf_op jit(solution)/shard_map/ppermute | solution.py:492
  128.3 2.9 %out_grads.5.do_ref = bf16[512,1024]{1,0:T(8,128)(2,1)S(1)} custom-call(bf16[2,1344,512]{2,1,0:T(8,128)(2,1)S(1)} %broadcast_select_fusion.refs_0_, bf16[512,1344]{1,0:T(8,128)(2,1)S(1)} %copy-done.9, f32[512,1024]{1,0:T(8,128)S(1)} %copy-done.6), custom_call_target="tpu_custom_call" | custom-call | flops 1 | bytes 1 | tf_op jit(solution)/shard_map/out_grads/pallas_call | solution.py:237
  131.2 11.2 %attention_backward.3 = (bf16[512,512]{1,0:T(8,128)(2,1)S(1)}, bf16[2,2,512,128]{3,2,1,0:T(8,128)(2,1)}, f32[2,2,1024,128]{3,2,1,0:T(8,128)S(1)}) custom-call(bf16[1024,1024]{1,0:T(8,128)(2,1)} %copy-done, bf16[1024,1024]{1,0:T(8,128)(2,1)} %copy-done, bf16[1024,1024]{1,0:T(8,128)(2,1)} %copy-done, ...), custom_call_target="tpu_custom_call" | custom-call | flops 1 | bytes 1 | tf_op jit(solution)/shard_map/attention_backward/pallas_call | solution.py:184
  142.4 3.1 %collective-permute-done.12.refs_1_ = bf16[128,1344]{1,0:T(8,128)(2,1)S(1)} collective-permute-done((bf16[128,1344]{1,0:T(8,128)(2,1)}, bf16[128,1344]{1,0:T(8,128)(2,1)S(1)}, u32[]{:S(2)}, u32[]{:S(2)}) %collective-permute-start.12) | collective-permute-done | bytes 344096 | tf_op jit(solution)/shard_map/ppermute | solution.py:492
  146.7 1.6 collective-permute-start.14
  148.4 6.0 %attention_backward.4 = (bf16[512,256]{1,0:T(8,128)(2,1)S(1)}, bf16[2,1,512,128]{3,2,1,0:T(8,128)(2,1)S(1)}, f32[2,1,1024,128]{3,2,1,0:T(8,128)S(1)}) custom-call(bf16[1024,1024]{1,0:T(8,128)(2,1)S(1)} %copy-done.1, bf16[1024,1024]{1,0:T(8,128)(2,1)S(1)} %copy-done.1, bf16[1024,1024]{1,0:T(8,128)(2,1)S(1)} %copy-done.1, ...), custom_call_target="tpu_custom_call" | custom-call | flops 1 | bytes 1 | tf_op jit(solution)/shard_map/attention_backward/pallas_call | solution.py:184
  155.7 6.0 %attention_backward.5 = (bf16[512,256]{1,0:T(8,128)(2,1)S(1)}, bf16[2,1,512,128]{3,2,1,0:T(8,128)(2,1)S(1)}, f32[2,1,1024,128]{3,2,1,0:T(8,128)S(1)}) custom-call(bf16[1024,1024]{1,0:T(8,128)(2,1)S(1)} %copy-done.1, bf16[1024,1024]{1,0:T(8,128)(2,1)S(1)} %copy-done.1, bf16[1024,1024]{1,0:T(8,128)(2,1)S(1)} %copy-done.1, ...), custom_call_target="tpu_custom_call" | custom-call | flops 1 | bytes 1 | tf_op jit(solution)/shard_map/attention_backward/pallas_call | solution.py:184
  161.8 6.2 %collective-permute-done.15.refs_2_ = bf16[2,1,512,128]{3,2,1,0:T(8,128)(2,1)S(1)} collective-permute-done((bf16[2,1,512,128]{3,2,1,0:T(8,128)(2,1)S(1)}, bf16[2,1,512,128]{3,2,1,0:T(8,128)(2,1)S(1)}, u32[]{:S(2)}, u32[]{:S(2)}) %collective-permute-start.15) | collective-permute-done | bytes 262176 | tf_op jit(solution)/shard_map/ppermute | solution.py:407
  172.1 6.9 %collective-permute-done.18.refs_3_ = bf16[128,1344]{1,0:T(8,128)(2,1)S(1)} collective-permute-done((bf16[128,1344]{1,0:T(8,128)(2,1)S(1)}, bf16[128,1344]{1,0:T(8,128)(2,1)S(1)}, u32[]{:S(2)}, u32[]{:S(2)}) %collective-permute-start.18) | collective-permute-done | bytes 344096 | tf_op jit(solution)/shard_map/ppermute | solution.py:492
  179.0 2.0 %collective-permute-done.19.refs_7_ = bf16[128,1344]{1,0:T(8,128)(2,1)S(1)} collective-permute-done((bf16[128,1344]{1,0:T(8,128)(2,1)S(1)}, bf16[128,1344]{1,0:T(8,128)(2,1)S(1)}, u32[]{:S(2)}, u32[]{:S(2)}) %collective-permute-start.19) | collective-permute-done | bytes 344096 | tf_op jit(solution)/shard_map/ppermute | solution.py:492
  181.0 2.8 %place_terms.1 = f32[128,5376]{1,0:T(8,128)} custom-call(s32[4]{0:T(128)S(1)} %pad_add_fusion.1.at_ref, f32[128,1344]{1,0:T(8,128)S(1)} %get-tuple-element.108.refs_0_, bf16[128,1344]{1,0:T(8,128)(2,1)S(1)} %collective-permute-done.12.refs_1_, f32[128,1344]{1,0:T(8,128)S(1)} %get-tuple-element.110.refs_2_, ...), custom_call_target="tpu_custom_call" | custom-call | flops 1 | bytes 1 | tf_op jit(solution)/shard_map/place_terms/pallas_call | solution.py:390
  183.8 2.0 %collective-permute-done.17.refs_3_ = bf16[2,1,512,128]{3,2,1,0:T(8,128)(2,1)S(1)} collective-permute-done((bf16[2,1,512,128]{3,2,1,0:T(8,128)(2,1)S(1)}, bf16[2,1,512,128]{3,2,1,0:T(8,128)(2,1)S(1)}, u32[]{:S(2)}, u32[]{:S(2)}) %collective-permute-start.17) | collective-permute-done | bytes 262176 | tf_op jit(solution)/shard_map/ppermute | solution.py:407
  188.0 2.0 %place_sums.1 = (bf16[512,512]{1,0:T(8,128)(2,1)}, bf16[512,512]{1,0:T(8,128)(2,1)}, bf16[512,512]{1,0:T(8,128)(2,1)}) custom-call(s32[2]{0:T(128)S(1)} %pad_add_fusion.where_ref, s32[4]{0:T(128)S(1)} %copy-done.35, s32[4]{0:T(128)S(1)} %copy-done.34, bf16[2,2,512,128]{3,2,1,0:T(8,128)(2,1)S(1)} %get-tuple-element.117.keep_ref, ...), custom_call_target="tpu_custom_call" | custom-call | flops 1 | bytes 1 | tf_op jit(solution)/shard_map/place_sums/pallas_call | solution.py:360
  (134 shorter events, 30.9 us)
Async XLA Ops:
  0.7 3.6 %collective-permute-start.2 = (bf16[1344,512]{1,0:T(8,128)(2,1)}, bf16[1344,512]{1,0:T(8,128)(2,1)}, u32[]{:S(2)}, u32[]{:S(2)}) collective-permute-start(bf16[1344,512]{1,0:T(8,128)(2,1)} %bitcast.30), channel_id=1, source_target_pairs={{0,4},{4,0},{8,12},{12,8},{16,20},{20,16},{24,28},{28,24},{1,5},{5... | collective-permute-start | bytes 4128776 | tf_op jit(solution)/shard_map/ppermute | solution.py:412
  4.0 6.6 %collective-permute-start = (bf16[512,1024]{1,0:T(8,128)(2,1)S(1)}, bf16[512,1024]{1,0:T(8,128)(2,1)}, u32[]{:S(2)}, u32[]{:S(2)}) collective-permute-start(bf16[512,1024]{1,0:T(8,128)(2,1)S(1)} %pad_maximum_fusion.3), channel_id=1, source_target_pairs={{0,4},{4,0},{8,12},{12,8},{16,20},{20,16},{24,28},{28,24},{1,5},{5... | collective-permute-start | bytes 3145736 | tf_op jit(solution)/shard_map/ppermute | solution.py:412
  7.8 65.4 %collective-permute-start.3 = (bf16[2,1344,512]{2,1,0:T(8,128)(2,1)}, bf16[2,1344,512]{2,1,0:T(8,128)(2,1)}, u32[]{:S(2)}, u32[]{:S(2)}) collective-permute-start(bf16[2,1344,512]{2,1,0:T(8,128)(2,1)} %pad_maximum_fusion.refs_0_), channel_id=1, source_target_pairs={{0,1},{1,2},{2,3},{3,0},{4,7},{5,4},{6,5},{7,6},{8,9},{9,10},{10,1... | collective-permute-start | bytes 8257544 | tf_op jit(solution)/shard_map/ppermute | solution.py:423
  13.4 26.1 %collective-permute-start.1 = (bf16[1024,512]{1,0:T(8,128)(2,1)}, bf16[1024,512]{1,0:T(8,128)(2,1)S(1)}, u32[]{:S(2)}, u32[]{:S(2)}) collective-permute-start(bf16[1024,512]{1,0:T(8,128)(2,1)} %fusion), channel_id=1, source_target_pairs={{0,8},{4,12},{8,16},{12,20},{16,24},{20,28},{1,9},{5,13},{9,17},{1... | collective-permute-start | bytes 3145736 | tf_op jit(solution)/shard_map/ppermute | solution.py:407
  25.6 13.9 %copy-start = (bf16[1024,1024]{1,0:T(8,128)(2,1)}, bf16[1024,1024]{1,0:T(8,128)(2,1)S(1)}, u32[]{:S(2)}) copy-start(bf16[1024,1024]{1,0:T(8,128)(2,1)S(1)} %pad_maximum_fusion.1.q_ref.k_ref.v_ref) | copy-start | bytes 6291460
  54.5 3.0 %collective-permute-start.4 = (bf16[2,128,1024]{2,1,0:T(8,128)(2,1)S(1)}, bf16[2,128,1024]{2,1,0:T(8,128)(2,1)}, u32[]{:S(2)}, u32[]{:S(2)}) collective-permute-start(bf16[2,128,1024]{2,1,0:T(8,128)(2,1)S(1)} %dynamic-slice_bitcast_fusion), channel_id=1, source_target_pairs={{0,4},{4,0},{8,12},{12,8},{16,20},{20,16},{24,28},{28,24},{1,5},{5... | collective-permute-start | bytes 1572872 | tf_op jit(solution)/shard_map/ppermute | solution.py:412
  73.3 16.9 %copy-start.4 = (f32[512,1024]{1,0:T(8,128)S(1)}, f32[512,1024]{1,0:T(8,128)}, u32[]{:S(2)}) copy-start(f32[512,1024]{1,0:T(8,128)} %copy-done.3) | copy-start | bytes 6291460
  73.3 16.9 %copy-start.7 = (bf16[512,1344]{1,0:T(8,128)(2,1)S(1)}, bf16[512,1344]{1,0:T(8,128)(2,1)}, u32[]{:S(2)}) copy-start(bf16[512,1344]{1,0:T(8,128)(2,1)} %get-tuple-element.124.refs_2_) | copy-start | bytes 4128772
  73.3 16.9 %copy-start.8 = (bf16[512,1344]{1,0:T(8,128)(2,1)S(1)}, bf16[512,1344]{1,0:T(8,128)(2,1)}, u32[]{:S(2)}) copy-start(bf16[512,1344]{1,0:T(8,128)(2,1)} %get-tuple-element.126.refs_3_) | copy-start | bytes 4128772
  73.3 5.3 %collective-permute-start.6 = (bf16[2,1344,512]{2,1,0:T(8,128)(2,1)}, bf16[2,1344,512]{2,1,0:T(8,128)(2,1)S(1)}, u32[]{:S(2)}, u32[]{:S(2)}) collective-permute-start(bf16[2,1344,512]{2,1,0:T(8,128)(2,1)} %collective-permute-done.3.refs_1_.refs_0_), channel_id=1, source_target_pairs={{0,4},{4,0},{8,12},{12,8},{16,20},{20,16},{24,28},{28,24},{1,5},{5... | collective-permute-start | bytes 8257544 | tf_op jit(solution)/shard_map/ppermute | solution.py:412
  73.3 32.4 %collective-permute-start.5 = (bf16[2,1344,512]{2,1,0:T(8,128)(2,1)}, bf16[2,1344,512]{2,1,0:T(8,128)(2,1)}, u32[]{:S(2)}, u32[]{:S(2)}) collective-permute-start(bf16[2,1344,512]{2,1,0:T(8,128)(2,1)} %collective-permute-done.3.refs_1_.refs_0_), channel_id=1, source_target_pairs={{0,1},{5,4},{2,3},{7,6},{8,9},{13,12},{10,11},{15,14},{16,17},{21,... | collective-permute-start | bytes 8257544 | tf_op jit(solution)/shard_map/ppermute | solution.py:423
  87.0 18.7 %collective-permute-start.7 = (bf16[128,2688]{1,0:T(8,128)(2,1)S(1)}, bf16[128,2688]{1,0:T(8,128)(2,1)S(1)}, u32[]{:S(2)}, u32[]{:S(2)}) collective-permute-start(bf16[128,2688]{1,0:T(8,128)(2,1)S(1)} %get-tuple-element.68), channel_id=1, source_target_pairs={{0,8},{4,12},{8,0},{12,4},{16,24},{20,28},{24,16},{28,20},{1,9},{5... | collective-permute-start | bytes 2064392 | tf_op jit(solution)/shard_map/ppermute | solution.py:492
  88.6 18.0 %collective-permute-start.8 = (bf16[128,2688]{1,0:T(8,128)(2,1)S(1)}, bf16[128,2688]{1,0:T(8,128)(2,1)S(1)}, u32[]{:S(2)}, u32[]{:S(2)}) collective-permute-start(bf16[128,2688]{1,0:T(8,128)(2,1)S(1)} %get-tuple-element.69), channel_id=1, source_target_pairs={{0,16},{4,20},{8,24},{12,28},{16,0},{20,4},{24,8},{28,12},{1,17},{... | collective-permute-start | bytes 2064392 | tf_op jit(solution)/shard_map/ppermute | solution.py:492
  107.5 7.2 %collective-permute-start.9 = (bf16[2,1344,512]{2,1,0:T(8,128)(2,1)}, bf16[2,1344,512]{2,1,0:T(8,128)(2,1)}, u32[]{:S(2)}, u32[]{:S(2)}) collective-permute-start(bf16[2,1344,512]{2,1,0:T(8,128)(2,1)} %collective-permute-done.5), channel_id=1, source_target_pairs={{0,4},{4,0},{8,12},{12,8},{16,20},{20,16},{24,28},{28,24},{1,5},{5... | collective-permute-start | bytes 8257544 | tf_op jit(solution)/shard_map/ppermute | solution.py:412
  109.7 18.6 %collective-permute-start.10 = (bf16[128,2688]{1,0:T(8,128)(2,1)}, bf16[128,2688]{1,0:T(8,128)(2,1)S(1)}, u32[]{:S(2)}, u32[]{:S(2)}) collective-permute-start(bf16[128,2688]{1,0:T(8,128)(2,1)} %get-tuple-element.78), channel_id=1, source_target_pairs={{0,8},{4,12},{8,0},{12,4},{16,24},{20,28},{24,16},{28,20},{1,9},{5... | collective-permute-start | bytes 2064392 | tf_op jit(solution)/shard_map/ppermute | solution.py:492
  116.9 11.4 %copy-start.6 = (f32[512,1024]{1,0:T(8,128)S(1)}, f32[512,1024]{1,0:T(8,128)}, u32[]{:S(2)}) copy-start(f32[512,1024]{1,0:T(8,128)} %copy-done.5) | copy-start | bytes 6291460
  119.9 26.4 %collective-permute-start.11 = (bf16[128,2688]{1,0:T(8,128)(2,1)}, bf16[128,2688]{1,0:T(8,128)(2,1)S(1)}, u32[]{:S(2)}, u32[]{:S(2)}) collective-permute-start(bf16[128,2688]{1,0:T(8,128)(2,1)} %get-tuple-element.77), channel_id=1, source_target_pairs={{0,16},{4,20},{8,24},{12,28},{16,0},{20,4},{24,8},{28,12},{1,17},{... | collective-permute-start | bytes 2064392 | tf_op jit(solution)/shard_map/ppermute | solution.py:492
  121.4 24.1 %collective-permute-start.12 = (bf16[128,1344]{1,0:T(8,128)(2,1)}, bf16[128,1344]{1,0:T(8,128)(2,1)S(1)}, u32[]{:S(2)}, u32[]{:S(2)}) collective-permute-start(bf16[128,1344]{1,0:T(8,128)(2,1)} %get-tuple-element.84), channel_id=1, source_target_pairs={{0,16},{4,20},{8,24},{12,28},{16,0},{20,4},{24,8},{28,12},{1,17},{... | collective-permute-start | bytes 1032200 | tf_op jit(solution)/shard_map/ppermute | solution.py:492
  121.9 23.6 %collective-permute-start.13 = (bf16[128,1344]{1,0:T(8,128)(2,1)}, bf16[128,1344]{1,0:T(8,128)(2,1)S(1)}, u32[]{:S(2)}, u32[]{:S(2)}) collective-permute-start(bf16[128,1344]{1,0:T(8,128)(2,1)} %get-tuple-element.85), channel_id=1, source_target_pairs={{0,8},{4,12},{8,0},{12,4},{16,24},{20,28},{24,16},{28,20},{1,9},{5... | collective-permute-start | bytes 1032200 | tf_op jit(solution)/shard_map/ppermute | solution.py:492
  131.2 15.1 %copy-start.11 = (f32[128,1344]{1,0:T(8,128)S(1)}, f32[128,1344]{1,0:T(8,128)}, u32[]{:S(2)}) copy-start(f32[128,1344]{1,0:T(8,128)} %copy-done.10) | copy-start | bytes 2064388
  131.2 15.1 %copy-start.13 = (f32[128,1344]{1,0:T(8,128)S(1)}, f32[128,1344]{1,0:T(8,128)}, u32[]{:S(2)}) copy-start(f32[128,1344]{1,0:T(8,128)} %copy-done.12) | copy-start | bytes 2064388
  131.2 15.1 %copy-start.15 = (f32[128,1344]{1,0:T(8,128)S(1)}, f32[128,1344]{1,0:T(8,128)}, u32[]{:S(2)}) copy-start(f32[128,1344]{1,0:T(8,128)} %copy-done.14) | copy-start | bytes 2064388
  131.2 15.1 %copy-start.17 = (f32[128,1344]{1,0:T(8,128)S(1)}, f32[128,1344]{1,0:T(8,128)}, u32[]{:S(2)}) copy-start(f32[128,1344]{1,0:T(8,128)} %copy-done.16) | copy-start | bytes 2064388
  131.2 15.1 %copy-start.27 = (bf16[128,2688]{1,0:T(8,128)(2,1)S(1)}, bf16[128,2688]{1,0:T(8,128)(2,1)}, u32[]{:S(2)}) copy-start(bf16[128,2688]{1,0:T(8,128)(2,1)} %copy-done.26) | copy-start | bytes 2064388
  146.7 21.2 %collective-permute-start.14 = (bf16[2,2,512,128]{3,2,1,0:T(8,128)(2,1)}, bf16[2,2,512,128]{3,2,1,0:T(8,128)(2,1)S(1)}, u32[]{:S(2)}, u32[]{:S(2)}) collective-permute-start(bf16[2,2,512,128]{3,2,1,0:T(8,128)(2,1)} %get-tuple-element.100), channel_id=1, source_target_pairs={{8,0},{12,4},{16,8},{20,12},{24,16},{28,20},{9,1},{13,5},{17,9},{2... | collective-permute-start | bytes 1572872 | tf_op jit(solution)/shard_map/ppermute | solution.py:407
  154.4 13.6 %collective-permute-start.15 = (bf16[2,1,512,128]{3,2,1,0:T(8,128)(2,1)S(1)}, bf16[2,1,512,128]{3,2,1,0:T(8,128)(2,1)S(1)}, u32[]{:S(2)}, u32[]{:S(2)}) collective-permute-start(bf16[2,1,512,128]{3,2,1,0:T(8,128)(2,1)S(1)} %get-tuple-element.101), channel_id=1, source_target_pairs={{8,0},{12,4},{16,8},{20,12},{24,16},{28,20},{9,1},{13,5},{17,9},{2... | collective-permute-start | bytes 786440 | tf_op jit(solution)/shard_map/ppermute | solution.py:407
  161.7 19.3 %copy-start.33 = (bf16[128,1344]{1,0:T(8,128)(2,1)S(1)}, bf16[128,1344]{1,0:T(8,128)(2,1)}, u32[]{:S(2)}) copy-start(bf16[128,1344]{1,0:T(8,128)(2,1)} %copy-done.32) | copy-start | bytes 1032196
  168.1 18.2 %collective-permute-start.16 = (bf16[512,512]{1,0:T(8,128)(2,1)S(1)}, bf16[512,512]{1,0:T(8,128)(2,1)S(1)}, u32[]{:S(2)}, u32[]{:S(2)}) collective-permute-start(bf16[512,512]{1,0:T(8,128)(2,1)S(1)} %broadcast_select_fusion.5), channel_id=1, source_target_pairs={{0,4},{4,0},{8,12},{12,8},{16,20},{20,16},{24,28},{28,24},{1,5},{5... | collective-permute-start | bytes 1572872 | tf_op jit(solution)/shard_map/ppermute | solution.py:412
  168.2 10.8 %collective-permute-start.18 = (bf16[128,1344]{1,0:T(8,128)(2,1)S(1)}, bf16[128,1344]{1,0:T(8,128)(2,1)S(1)}, u32[]{:S(2)}, u32[]{:S(2)}) collective-permute-start(bf16[128,1344]{1,0:T(8,128)(2,1)S(1)} %get-tuple-element.111), channel_id=1, source_target_pairs={{0,16},{4,20},{8,24},{12,28},{16,0},{20,4},{24,8},{28,12},{1,17},{... | collective-permute-start | bytes 1032200 | tf_op jit(solution)/shard_map/ppermute | solution.py:492
  169.7 11.3 %collective-permute-start.19 = (bf16[128,1344]{1,0:T(8,128)(2,1)S(1)}, bf16[128,1344]{1,0:T(8,128)(2,1)S(1)}, u32[]{:S(2)}, u32[]{:S(2)}) collective-permute-start(bf16[128,1344]{1,0:T(8,128)(2,1)S(1)} %get-tuple-element.99), channel_id=1, source_target_pairs={{0,8},{4,12},{8,0},{12,4},{16,24},{20,28},{24,16},{28,20},{1,9},{5... | collective-permute-start | bytes 1032200 | tf_op jit(solution)/shard_map/ppermute | solution.py:492
  170.7 15.2 %collective-permute-start.17 = (bf16[2,1,512,128]{3,2,1,0:T(8,128)(2,1)S(1)}, bf16[2,1,512,128]{3,2,1,0:T(8,128)(2,1)S(1)}, u32[]{:S(2)}, u32[]{:S(2)}) collective-permute-start(bf16[2,1,512,128]{3,2,1,0:T(8,128)(2,1)S(1)} %get-tuple-element.107), channel_id=1, source_target_pairs={{8,0},{12,4},{16,8},{20,12},{24,16},{28,20},{9,1},{13,5},{17,9},{2... | collective-permute-start | bytes 786440 | tf_op jit(solution)/shard_map/ppermute | solution.py:407
  186.1 2.0 %collective-permute-start.20 = (bf16[2,2,512,128]{3,2,1,0:T(8,128)(2,1)S(1)}, bf16[2,2,512,128]{3,2,1,0:T(8,128)(2,1)S(1)}, u32[]{:S(2)}, u32[]{:S(2)}) collective-permute-start(bf16[2,2,512,128]{3,2,1,0:T(8,128)(2,1)S(1)} %get-tuple-element.118), channel_id=1, source_target_pairs={{0,4},{4,0},{8,12},{12,8},{16,20},{20,16},{24,28},{28,24},{1,5},{5... | collective-permute-start | bytes 1572872 | tf_op jit(solution)/shard_map/ppermute | solution.py:412
  (31 other events, 163.2 us)

commit v3 on v2

--- a/solution.py
+++ b/solution.py
@@ -217,39 +217,42 @@
     )(packet, packet, packet, before, before, attention, out_grads, carry)
 
 
-def grads_kernel(number, *refs):
+def grads_kernel(number, halves, *refs):
     blocks, weights = refs[:number], refs[number : 2 * number]
     total = None
-    for block, weight in zip(blocks, weights):
-        term = dot(weight[...], block[0])
+    others = refs[2 * number : 3 * number] if halves else [None] * number
+    for block, other, weight in zip(blocks, others, weights):
+        term = dot(weight[...], block[0] if other is None else block[0] + other[0])
         total = term if total is None else total + term
-    for old in refs[2 * number : -1]:
+    for old in refs[(3 if halves else 2) * number : -1]:
         total = total + old[...]
     refs[-1][...] = total.astype(refs[-1].dtype)
 
 
-def add_grads(blocks, weights, total, dtype):
+def add_grads(blocks, weights, total, dtype, others=()):
     _, cols, tok = blocks[0].shape
     width = weights[0].shape[0]
     tiles = tok // TILE
     tile_spec = pl.BlockSpec((width, TILE), lambda i: (0, i))
     number = len(blocks)
     return pl.pallas_call(
-        functools.partial(grads_kernel, number),
+        functools.partial(grads_kernel, number, len(others) > 0),
         grid=(2 * tiles,),
         in_specs=[pl.BlockSpec((1, cols, TILE), lambda i: (i // tiles, 0, i % tiles))] * number
         + [pl.BlockSpec((width, cols), lambda i: (0, 0))] * number
+        + [pl.BlockSpec((1, cols, TILE), lambda i: (i // tiles, 0, i % tiles))] * len(others)
         + ([] if total is None else [tile_spec]),
         out_specs=tile_spec,
         out_shape=jax.ShapeDtypeStruct((width, 2 * tok), dtype),
         compiler_params=pltpu.CompilerParams(vmem_limit_bytes=VMEM_LIMIT),
         cost_estimate=CHEAP,
         name="out_grads",
-    )(*blocks, *weights, *([] if total is None else [total]))
-
-
-def terms_kernel(orders, count, rows_ref, *refs):
+    )(*blocks, *weights, *others, *([] if total is None else [total]))
+
+
+def terms_kernel(orders, count, halves, rows_ref, *refs):
     number = len(orders)
+    others, refs = (refs[:number], refs[number:]) if halves else ([None] * number, refs)
     blocks, waiting = refs[:number], refs[number : number + 3 * count]
     outs, passed = refs[number + 3 * count : number + 3 * count + 3 * number], refs[number + 3 * count + 3 * number :]
     for n in range(count):
@@ -257,13 +260,14 @@
         cols = keep.shape[1]
         passed[2 * n][...] = keep[...] + got[:, :cols].astype(jnp.float32)
         passed[2 * n + 1][...] = (near[...] + got[:, cols:].astype(jnp.float32)).astype(jnp.bfloat16)
-    for n, (block, first) in enumerate(zip(blocks, orders)):
+    for n, (block, other, first) in enumerate(zip(blocks, others, orders)):
         _, cols, tok = block.shape
         share = rows_ref.shape[0] // 4
         keep, near, send = outs[3 * n : 3 * n + 3]
         for at in range(0, cols, TILE):
             end = min(at + TILE, cols)
-            term = dot(rows_ref[:, :tok], block[0, at:end, :], NT) + dot(rows_ref[:, tok:], block[1, at:end, :], NT)
+            pair = [block[i, at:end, :] if other is None else block[i, at:end, :] + other[i, at:end, :] for i in (0, 1)]
+            term = dot(rows_ref[:, :tok], pair[0], NT) + dot(rows_ref[:, tok:], pair[1], NT)
             parts = [term[s * share : (s + 1) * share] for s in range(4)]
             keep[:, at:end] = parts[0]
             near[:, at:end] = parts[3 - first]
@@ -271,7 +275,7 @@
             send[:, cols + at : cols + end] = parts[3].astype(jnp.bfloat16)
 
 
-def make_terms(rows, blocks, orders, waiting):
+def make_terms(rows, blocks, orders, waiting, others=()):
     share = rows.shape[0] // 4
     flat = [x for group in waiting for x in group]
     whole = lambda x: pl.BlockSpec(x.shape, lambda i: (0,) * len(x.shape))
@@ -283,15 +287,15 @@
     for keep, _, _ in waiting:
         shapes += [jax.ShapeDtypeStruct(keep.shape, jnp.float32), jax.ShapeDtypeStruct(keep.shape, jnp.bfloat16)]
     out = pl.pallas_call(
-        functools.partial(terms_kernel, orders, len(waiting)),
+        functools.partial(terms_kernel, orders, len(waiting), len(others) > 0),
         grid=(1,),
-        in_specs=[whole(x) for x in (rows, *blocks, *flat)],
+        in_specs=[whole(x) for x in (rows, *others, *blocks, *flat)],
         out_specs=[whole(x) for x in shapes],
         out_shape=shapes,
         compiler_params=pltpu.CompilerParams(vmem_limit_bytes=VMEM_LIMIT),
         cost_estimate=CHEAP,
         name="weight_terms",
-    )(rows, *blocks, *flat)
+    )(rows, *others, *blocks, *flat)
     cut = 3 * len(blocks)
     return [list(out[n : n + 3]) for n in range(0, cut, 3)], [list(out[n : n + 2]) for n in range(cut, len(out), 2)]
 
@@ -499,14 +503,14 @@
         grads = add_grads(blocks, weights[1:3], grads, jnp.float32)
 
         final, own_got, down_got, grads = lax.optimization_barrier((final, own_got, down_got, grads))
-        final = jnp.where(core == 1 - z % 2, final, swap_cores(final))
+        there = swap_cores(final)
         (last_terms,), (own_sum, down_sum) = make_terms(
-            by_distance, [final], (2,), [(*own_terms[:2], own_got), (*down_terms[:2], down_got)]
+            by_distance, [final], (2,), [(*own_terms[:2], own_got), (*down_terms[:2], down_got)], [there]
         )
         last_got = exchange(last_terms[2], 2)
         own_sum[1], down_sum[1] = exchange(own_sum[1], 2), exchange(down_sum[1], 1)
-        final, _, up_got = lax.optimization_barrier((final, last_terms[2], up_got))
-        grads = add_grads([final], weights[3:], grads, jnp.bfloat16)
+        final, there, _, up_got = lax.optimization_barrier((final, there, last_terms[2], up_got))
+        grads = add_grads([final], weights[3:], grads, jnp.bfloat16, [there])
     else:
         blocks = [own_block, *direct]
         grads = add_grads(blocks[1:], weights[1:], grads, jnp.float32).astype(jnp.bfloat16)

time: 191 us -> 186 us (0.974)
  waiting for transfers between devices: 63.9 us -> 66 us
    select_n x1 -> x0, other arithmetic: 2.06 us -> none  [body(): final = jnp.where(core == 1 - z % 2, final, swap_cores(final))]
    unnamed x85 -> x43, local copies, waits for them, and re-layouts: 5.52 us -> 3.84 us
  transfers between devices with their start and end apart: 21 -> 21, of which waited for: 14 -> 12; matrix products, arithmetic and copies ran while one was open for 12% -> 12% of each run, Pallas kernels for 34% -> 34%
where the time goes in v3:
time: 186 us
  Pallas kernels  66.4 us (36%)
  waiting for transfers between devices  66 us (35%)
  starting transfers between devices  27 us (15%)
  local copies, waits for them, and re-layouts  14.6 us (8%)
  other arithmetic  10.8 us (6%)
    ppermute x2, waiting for transfers between devices, move(): return lax.ppermute(shard, ('ctx', 'head'), places)  24.8 us
    pallas_call x3, Pallas kernels, backward(): pl.pallas_call(functools.partial(backward_kernel, phase), grid=(count, ti...  23.1 us
    ppermute x8, waiting for transfers between devices, exchange(): lax.ppermute(shard, 'ctx', [(i, i ^ 2 * distance) for i in range(n_ctx)])  16.8 us
    ppermute x4, waiting for transfers between devices, shift(): lax.ppermute(shard, 'ctx', [(i, i + by) for i in range(size) if 0 <= i +...  15.6 us
    pallas_call x1, Pallas kernels, forward(): pl.pallas_call(forward_kernel, grid_spec=grid_spec, out_shape=[jax.ShapeD...  15 us
    pallas_call x3, Pallas kernels, add_grads(): pl.pallas_call(functools.partial(grads_kernel, number, len(others) > 0),...  13.1 us
    ppermute x8, starting transfers between devices, exchange(): lax.ppermute(shard, 'ctx', [(i, i ^ 2 * distance) for i in range(n_ctx)])  10.7 us
    pallas_call x3, Pallas kernels, make_terms(): pl.pallas_call(functools.partial(terms_kernel, orders, len(waiting), len(...  10.2 us
  transfers between devices with their start and end apart: 21, of which 12 were waited for; matrix products, arithmetic and copies ran while one was open for 12% of the time, Pallas kernels for 34%

profile of v3, /device:TPU:0, one launch (start us, length us, event | category | flops | bytes accessed | tf_op | source)
XLA Modules:
  0.0 186.0 jit_solution(293430851218054076)
XLA Ops:
  6.6 1.8 pad_maximum_fusion.refs_0_
  8.4 3.0 %collective-permute-start.3 = (bf16[2,1344,512]{2,1,0:T(8,128)(2,1)}, bf16[2,1344,512]{2,1,0:T(8,128)(2,1)}, u32[]{:S(2)}, u32[]{:S(2)}) collective-permute-start(bf16[2,1344,512]{2,1,0:T(8,128)(2,1)} %pad_maximum_fusion.refs_0_), channel_id=1, source_target_pairs={{0,1},{1,2},{2,3},{3,0},{4,7},{5,4},{6,5},{7,6},{8,9},{9,10},{10,1... | collective-permute-start | bytes 8257544 | tf_op jit(solution)/shard_map/ppermute | solution.py:427
  11.3 1.7 broadcast_select_fusion.1
  14.2 3.4 %collective-permute-start.1 = (bf16[1024,512]{1,0:T(8,128)(2,1)}, bf16[1024,512]{1,0:T(8,128)(2,1)S(1)}, u32[]{:S(2)}, u32[]{:S(2)}) collective-permute-start(bf16[1024,512]{1,0:T(8,128)(2,1)} %fusion), channel_id=1, source_target_pairs={{0,8},{4,12},{8,16},{12,20},{16,24},{20,28},{1,9},{5,13},{9,17},{1... | collective-permute-start | bytes 3145736 | tf_op jit(solution)/shard_map/ppermute | solution.py:411
  17.7 8.5 %fusion.5 = (bf16[512,1344]{1,0:T(8,128)(2,1)}, bf16[512,1344]{1,0:T(8,128)(2,1)}, bf16[512,1344]{1,0:T(8,128)(2,1)S(1)}, bf16[512,1344]{1,0:T(8,128)(2,1)}) fusion(bf16[1024,5376]{1,0:T(8,128)(2,1)} %param.13, s32[]{:T(128)S(6)} %select_n.170, s32[]{:T(128)S(6)} %select_n.184, s32[]{:T(128)S(6)} %select_n.177, s32[]{:T(128)S(6)} %select_n.173, s32[]{:T(128)S(6)} %select_n.181), kind=kLoop, calls=%fused_computation.47 | loop fusion | bytes 11010068 | tf_op jit(solution)/shard_map/dynamic_slice | solution.py:480
  26.4 4.7 %out_grads.3.refs_4_ = f32[512,1024]{1,0:T(8,128)S(1)} custom-call(bf16[2,1344,512]{2,1,0:T(8,128)(2,1)} %pad_maximum_fusion.refs_0_, bf16[512,1344]{1,0:T(8,128)(2,1)S(1)} %get-tuple-element.127.refs_1_), custom_call_target="tpu_custom_call" | custom-call | flops 1 | bytes 1 | tf_op jit(solution)/shard_map/out_grads/pallas_call | solution.py:238
  32.4 8.2 %collective-permute-done.1.pk_ref.pv_ref = bf16[1024,512]{1,0:T(8,128)(2,1)S(1)} collective-permute-done((bf16[1024,512]{1,0:T(8,128)(2,1)}, bf16[1024,512]{1,0:T(8,128)(2,1)S(1)}, u32[]{:S(2)}, u32[]{:S(2)}) %collective-permute-start.1) | collective-permute-done | bytes 1048608 | tf_op jit(solution)/shard_map/ppermute | solution.py:411
  40.5 15.0 %attention_forward.1 = (f32[2,4,1280,512]{3,2,1,0:T(8,128)}, bf16[512,1024]{1,0:T(8,128)(2,1)S(1)}) custom-call(s32[1]{0:T(128)} %bitcast.5.chip_ref, bf16[1024,1024]{1,0:T(8,128)(2,1)S(1)} %pad_maximum_fusion.1.q_ref.k_ref.v_ref, bf16[1024,1024]{1,0:T(8,128)(2,1)S(1)} %pad_maximum_fusion.1.q_ref.k_ref.v_ref, ...), custom_call_target="tpu_custom_call" | custom-call | flops 1 | bytes 1 | tf_op jit(solution)/shard_map/attention_forward/pallas_call | solution.py:102
  56.6 1.7 collective-permute-done.4
  59.9 13.9 %collective-permute-done.3.refs_1_.refs_0_ = bf16[2,1344,512]{2,1,0:T(8,128)(2,1)} collective-permute-done((bf16[2,1344,512]{2,1,0:T(8,128)(2,1)}, bf16[2,1344,512]{2,1,0:T(8,128)(2,1)}, u32[]{:S(2)}, u32[]{:S(2)}) %collective-permute-start.3) | collective-permute-done | bytes 2752544 | tf_op jit(solution)/shard_map/ppermute | solution.py:427
  73.8 1.9 %collective-permute-start.5 = (bf16[2,1344,512]{2,1,0:T(8,128)(2,1)}, bf16[2,1344,512]{2,1,0:T(8,128)(2,1)S(1)}, u32[]{:S(2)}, u32[]{:S(2)}) collective-permute-start(bf16[2,1344,512]{2,1,0:T(8,128)(2,1)} %collective-permute-done.3.refs_1_.refs_0_), channel_id=1, source_target_pairs={{0,1},{5,4},{2,3},{7,6},{8,9},{13,12},{10,11},{15,14},{16,17},{21,... | collective-permute-start | bytes 8257544 | tf_op jit(solution)/shard_map/ppermute | solution.py:427
  75.7 3.4 %collective-permute-done.6.refs_2_.refs_1_ = bf16[2,1344,512]{2,1,0:T(8,128)(2,1)S(1)} collective-permute-done((bf16[2,1344,512]{2,1,0:T(8,128)(2,1)}, bf16[2,1344,512]{2,1,0:T(8,128)(2,1)S(1)}, u32[]{:S(2)}, u32[]{:S(2)}) %collective-permute-start.6) | collective-permute-done | bytes 2752544 | tf_op jit(solution)/shard_map/ppermute | solution.py:416
  79.1 7.8 %weight_terms.3 = (f32[128,1344]{1,0:T(8,128)S(1)}, f32[128,1344]{1,0:T(8,128)S(1)}, bf16[128,2688]{1,0:T(8,128)(2,1)S(1)}, f32[128,1344]{1,0:T(8,128)S(1)}, f32...) custom-call(bf16[512,1024]{1,0:T(8,128)(2,1)S(1)} %bitcast.25, ...), custom_call_target="tpu_custom_call" | custom-call | flops 1 | bytes 1 | tf_op jit(solution)/shard_map/weight_terms/pallas_call | solution.py:289
  86.9 1.6 collective-permute-start.7
  90.0 5.4 %out_grads.4.refs_3_ = f32[512,1024]{1,0:T(8,128)S(1)} custom-call(bf16[2,1344,512]{2,1,0:T(8,128)(2,1)} %collective-permute-done.3.refs_1_.refs_0_, bf16[2,1344,512]{2,1,0:T(8,128)(2,1)S(1)} %collective-permute-done.6.refs_2_.refs_1_, bf16[512,1344]{1,0:T(8,128)(2,1)S(1)} %copy-done.6, bf16[512,1344]{1,0:T(8,128)(2,1)S(1)} %copy-done.7, ...), custom_call_target="tpu_custom_call" | custom-call | flops 1 | bytes 1 | tf_op jit(solution)/shard_map/out_grads/pallas_call | solution.py:238
  95.4 10.9 %collective-permute-done.5.refs_1_.refs_0_ = bf16[2,1344,512]{2,1,0:T(8,128)(2,1)S(1)} collective-permute-done((bf16[2,1344,512]{2,1,0:T(8,128)(2,1)}, bf16[2,1344,512]{2,1,0:T(8,128)(2,1)S(1)}, u32[]{:S(2)}, u32[]{:S(2)}) %collective-permute-start.5) | collective-permute-done | bytes 2752544 | tf_op jit(solution)/shard_map/ppermute | solution.py:427
  106.3 2.1 %collective-permute-start.9 = (bf16[2,1344,512]{2,1,0:T(8,128)(2,1)S(1)}, bf16[2,1344,512]{2,1,0:T(8,128)(2,1)S(1)}, u32[]{:S(2)}, u32[]{:S(2)}) collective-permute-start(bf16[2,1344,512]{2,1,0:T(8,128)(2,1)S(1)} %collective-permute-done.5.refs_1_.refs_0_), channel_id=1, source_target_pairs={{0,4},{4,0},{8,12},{12,8},{16,20},{20,16},{24,28},{28,24},{1,5},{5... | collective-permute-start | bytes 8257544 | tf_op jit(solution)/shard_map/ppermute | solution.py:416
  109.8 3.2 %collective-permute-done.9.refs_0_.refs_2_ = bf16[2,1344,512]{2,1,0:T(8,128)(2,1)S(1)} collective-permute-done((bf16[2,1344,512]{2,1,0:T(8,128)(2,1)S(1)}, bf16[2,1344,512]{2,1,0:T(8,128)(2,1)S(1)}, u32[]{:S(2)}, u32[]{:S(2)}) %collective-permute-start.9) | collective-permute-done | bytes 2752544 | tf_op jit(solution)/shard_map/ppermute | solution.py:416
  113.0 2.1 %weight_terms.4 = (f32[128,1344]{1,0:T(8,128)S(1)}, f32[128,1344]{1,0:T(8,128)S(1)}, bf16[128,2688]{1,0:T(8,128)(2,1)S(1)}, f32[128,1344]{1,0:T(8,128)S(1)}, bf1...) custom-call(bf16[512,1024]{1,0:T(8,128)(2,1)S(1)} %bitcast.26, ...), custom_call_target="tpu_custom_call" | custom-call | flops 1 | bytes 1 | tf_op jit(solution)/shard_map/weight_terms/pallas_call | solution.py:289
  115.1 1.6 collective-permute-start.11
  118.7 7.9 %collective-permute-done.10.refs_2_ = bf16[128,2688]{1,0:T(8,128)(2,1)S(1)} collective-permute-done((bf16[128,2688]{1,0:T(8,128)(2,1)S(1)}, bf16[128,2688]{1,0:T(8,128)(2,1)S(1)}, u32[]{:S(2)}, u32[]{:S(2)}) %collective-permute-start.10) | collective-permute-done | bytes 688160 | tf_op jit(solution)/shard_map/ppermute | solution.py:496
  126.6 3.0 %out_grads.5.do_ref = bf16[512,1024]{1,0:T(8,128)(2,1)S(1)} custom-call(bf16[2,1344,512]{2,1,0:T(8,128)(2,1)S(1)} %collective-permute-done.5.refs_1_.refs_0_, bf16[512,1344]{1,0:T(8,128)(2,1)S(1)} %copy-done.5, bf16[2,1344,512]{2,1,0:T(8,128)(2,1)S(1)} %collective-permute-done.9.refs_0_.refs_2_, f32[512,1024]{1,0:T(8,128)S(1)} %out_grads.4.refs_3_), custom_call_target="tpu_custom_call" | custom-call | flops 1 | bytes 1 | tf_op jit(solution)/shard_map/out_grads/pallas_call | solution.py:238
  129.7 11.1 %attention_backward.3 = (bf16[512,512]{1,0:T(8,128)(2,1)S(1)}, bf16[2,2,512,128]{3,2,1,0:T(8,128)(2,1)}, f32[2,2,1024,128]{3,2,1,0:T(8,128)S(1)}) custom-call(bf16[1024,1024]{1,0:T(8,128)(2,1)} %copy-done, bf16[1024,1024]{1,0:T(8,128)(2,1)} %copy-done, bf16[1024,1024]{1,0:T(8,128)(2,1)} %copy-done, ...), custom_call_target="tpu_custom_call" | custom-call | flops 1 | bytes 1 | tf_op jit(solution)/shard_map/attention_backward/pallas_call | solution.py:184
  145.2 6.0 %attention_backward.4 = (bf16[512,256]{1,0:T(8,128)(2,1)S(1)}, bf16[2,1,512,128]{3,2,1,0:T(8,128)(2,1)S(1)}, f32[2,1,1024,128]{3,2,1,0:T(8,128)S(1)}) custom-call(bf16[1024,1024]{1,0:T(8,128)(2,1)S(1)} %copy-done.1, bf16[1024,1024]{1,0:T(8,128)(2,1)S(1)} %copy-done.1, bf16[1024,1024]{1,0:T(8,128)(2,1)S(1)} %copy-done.1, ...), custom_call_target="tpu_custom_call" | custom-call | flops 1 | bytes 1 | tf_op jit(solution)/shard_map/attention_backward/pallas_call | solution.py:184
  152.5 6.0 %attention_backward.5 = (bf16[512,256]{1,0:T(8,128)(2,1)S(1)}, bf16[2,1,512,128]{3,2,1,0:T(8,128)(2,1)S(1)}, f32[2,1,1024,128]{3,2,1,0:T(8,128)S(1)}) custom-call(bf16[1024,1024]{1,0:T(8,128)(2,1)S(1)} %copy-done.1, bf16[1024,1024]{1,0:T(8,128)(2,1)S(1)} %copy-done.1, bf16[1024,1024]{1,0:T(8,128)(2,1)S(1)} %copy-done.1, ...), custom_call_target="tpu_custom_call" | custom-call | flops 1 | bytes 1 | tf_op jit(solution)/shard_map/attention_backward/pallas_call | solution.py:184
  158.6 5.4 %collective-permute-done.15.refs_2_ = bf16[2,1,512,128]{3,2,1,0:T(8,128)(2,1)S(1)} collective-permute-done((bf16[2,1,512,128]{3,2,1,0:T(8,128)(2,1)S(1)}, bf16[2,1,512,128]{3,2,1,0:T(8,128)(2,1)S(1)}, u32[]{:S(2)}, u32[]{:S(2)}) %collective-permute-start.15) | collective-permute-done | bytes 262176 | tf_op jit(solution)/shard_map/ppermute | solution.py:411
  164.1 1.6 collective-permute-start.18
  168.0 6.9 %collective-permute-done.18.refs_3_ = bf16[128,1344]{1,0:T(8,128)(2,1)S(1)} collective-permute-done((bf16[128,1344]{1,0:T(8,128)(2,1)S(1)}, bf16[128,1344]{1,0:T(8,128)(2,1)S(1)}, u32[]{:S(2)}, u32[]{:S(2)}) %collective-permute-start.18) | collective-permute-done | bytes 344096 | tf_op jit(solution)/shard_map/ppermute | solution.py:496
  174.9 2.0 %collective-permute-done.19.refs_7_ = bf16[128,1344]{1,0:T(8,128)(2,1)S(1)} collective-permute-done((bf16[128,1344]{1,0:T(8,128)(2,1)S(1)}, bf16[128,1344]{1,0:T(8,128)(2,1)S(1)}, u32[]{:S(2)}, u32[]{:S(2)}) %collective-permute-start.19) | collective-permute-done | bytes 344096 | tf_op jit(solution)/shard_map/ppermute | solution.py:496
  177.0 2.8 %place_terms.1 = f32[128,5376]{1,0:T(8,128)} custom-call(s32[4]{0:T(128)S(1)} %pad_add_fusion.1.at_ref, f32[128,1344]{1,0:T(8,128)S(1)} %get-tuple-element.110.refs_0_, bf16[128,1344]{1,0:T(8,128)(2,1)S(1)} %collective-permute-done.12.refs_1_, f32[128,1344]{1,0:T(8,128)S(1)} %get-tuple-element.112.refs_2_, ...), custom_call_target="tpu_custom_call" | custom-call | flops 1 | bytes 1 | tf_op jit(solution)/shard_map/place_terms/pallas_call | solution.py:394
  179.8 2.0 %collective-permute-done.17.refs_3_ = bf16[2,1,512,128]{3,2,1,0:T(8,128)(2,1)S(1)} collective-permute-done((bf16[2,1,512,128]{3,2,1,0:T(8,128)(2,1)S(1)}, bf16[2,1,512,128]{3,2,1,0:T(8,128)(2,1)S(1)}, u32[]{:S(2)}, u32[]{:S(2)}) %collective-permute-start.17) | collective-permute-done | bytes 262176 | tf_op jit(solution)/shard_map/ppermute | solution.py:411
  184.0 2.0 %place_sums.1 = (bf16[512,512]{1,0:T(8,128)(2,1)}, bf16[512,512]{1,0:T(8,128)(2,1)}, bf16[512,512]{1,0:T(8,128)(2,1)}) custom-call(s32[2]{0:T(128)S(1)} %pad_add_fusion.where_ref, s32[4]{0:T(128)S(1)} %copy-done.11, s32[4]{0:T(128)S(1)} %copy-done.10, bf16[2,2,512,128]{3,2,1,0:T(8,128)(2,1)S(1)} %get-tuple-element.119.keep_ref, ...), custom_call_target="tpu_custom_call" | custom-call | flops 1 | bytes 1 | tf_op jit(solution)/shard_map/place_sums/pallas_call | solution.py:364
  (91 shorter events, 26.5 us)
Async XLA Ops:
  0.7 2.0 %copy-start.18 = (bf16[512,512]{1,0:T(8,128)(2,1)S(1)}, bf16[512,512]{1,0:T(8,128)(2,1)}, u32[]{:S(2)}) copy-start(bf16[512,512]{1,0:T(8,128)(2,1)} %param.11) | copy-start | bytes 1572868
  0.7 4.4 %collective-permute-start.2 = (bf16[1344,512]{1,0:T(8,128)(2,1)}, bf16[1344,512]{1,0:T(8,128)(2,1)}, u32[]{:S(2)}, u32[]{:S(2)}) collective-permute-start(bf16[1344,512]{1,0:T(8,128)(2,1)} %bitcast.30), channel_id=1, source_target_pairs={{0,4},{4,0},{8,12},{12,8},{16,20},{20,16},{24,28},{28,24},{1,5},{5... | collective-permute-start | bytes 4128776 | tf_op jit(solution)/shard_map/ppermute | solution.py:416
  4.9 6.4 %collective-permute-start = (bf16[512,1024]{1,0:T(8,128)(2,1)}, bf16[512,1024]{1,0:T(8,128)(2,1)}, u32[]{:S(2)}, u32[]{:S(2)}) collective-permute-start(bf16[512,1024]{1,0:T(8,128)(2,1)} %pad_maximum_fusion.3), channel_id=1, source_target_pairs={{0,4},{4,0},{8,12},{12,8},{16,20},{20,16},{24,28},{28,24},{1,5},{5... | collective-permute-start | bytes 3145736 | tf_op jit(solution)/shard_map/ppermute | solution.py:416
  6.6 4.8 %copy-start.17 = (bf16[512,256]{1,0:T(8,128)(2,1)S(1)}, bf16[512,256]{1,0:T(8,128)(2,1)}, u32[]{:S(2)}) copy-start(bf16[512,256]{1,0:T(8,128)(2,1)} %get-tuple-element.148) | copy-start | bytes 786436
  8.4 65.4 %collective-permute-start.3 = (bf16[2,1344,512]{2,1,0:T(8,128)(2,1)}, bf16[2,1344,512]{2,1,0:T(8,128)(2,1)}, u32[]{:S(2)}, u32[]{:S(2)}) collective-permute-start(bf16[2,1344,512]{2,1,0:T(8,128)(2,1)} %pad_maximum_fusion.refs_0_), channel_id=1, source_target_pairs={{0,1},{1,2},{2,3},{3,0},{4,7},{5,4},{6,5},{7,6},{8,9},{9,10},{10,1... | collective-permute-start | bytes 8257544 | tf_op jit(solution)/shard_map/ppermute | solution.py:427
  14.2 26.4 %collective-permute-start.1 = (bf16[1024,512]{1,0:T(8,128)(2,1)}, bf16[1024,512]{1,0:T(8,128)(2,1)S(1)}, u32[]{:S(2)}, u32[]{:S(2)}) collective-permute-start(bf16[1024,512]{1,0:T(8,128)(2,1)} %fusion), channel_id=1, source_target_pairs={{0,8},{4,12},{8,16},{12,20},{16,24},{20,28},{1,9},{5,13},{9,17},{1... | collective-permute-start | bytes 3145736 | tf_op jit(solution)/shard_map/ppermute | solution.py:411
  26.4 14.2 %copy-start = (bf16[1024,1024]{1,0:T(8,128)(2,1)}, bf16[1024,1024]{1,0:T(8,128)(2,1)S(1)}, u32[]{:S(2)}) copy-start(bf16[1024,1024]{1,0:T(8,128)(2,1)S(1)} %pad_maximum_fusion.1.q_ref.k_ref.v_ref) | copy-start | bytes 6291460
  55.5 2.7 %collective-permute-start.4 = (bf16[2,128,1024]{2,1,0:T(8,128)(2,1)S(1)}, bf16[2,128,1024]{2,1,0:T(8,128)(2,1)}, u32[]{:S(2)}, u32[]{:S(2)}) collective-permute-start(bf16[2,128,1024]{2,1,0:T(8,128)(2,1)S(1)} %dynamic-slice_bitcast_fusion), channel_id=1, source_target_pairs={{0,4},{4,0},{8,12},{12,8},{16,20},{20,16},{24,28},{28,24},{1,5},{5... | collective-permute-start | bytes 1572872 | tf_op jit(solution)/shard_map/ppermute | solution.py:416
  73.8 16.2 %copy-start.4 = (f32[512,1024]{1,0:T(8,128)S(1)}, f32[512,1024]{1,0:T(8,128)}, u32[]{:S(2)}) copy-start(f32[512,1024]{1,0:T(8,128)} %copy-done.3) | copy-start | bytes 6291460
  73.8 16.2 %copy-start.6 = (bf16[512,1344]{1,0:T(8,128)(2,1)S(1)}, bf16[512,1344]{1,0:T(8,128)(2,1)}, u32[]{:S(2)}) copy-start(bf16[512,1344]{1,0:T(8,128)(2,1)} %get-tuple-element.126.refs_2_) | copy-start | bytes 4128772
  73.8 16.2 %copy-start.7 = (bf16[512,1344]{1,0:T(8,128)(2,1)S(1)}, bf16[512,1344]{1,0:T(8,128)(2,1)}, u32[]{:S(2)}) copy-start(bf16[512,1344]{1,0:T(8,128)(2,1)} %get-tuple-element.128.refs_3_) | copy-start | bytes 4128772
  73.8 5.3 %collective-permute-start.6 = (bf16[2,1344,512]{2,1,0:T(8,128)(2,1)}, bf16[2,1344,512]{2,1,0:T(8,128)(2,1)S(1)}, u32[]{:S(2)}, u32[]{:S(2)}) collective-permute-start(bf16[2,1344,512]{2,1,0:T(8,128)(2,1)} %collective-permute-done.3.refs_1_.refs_0_), channel_id=1, source_target_pairs={{0,4},{4,0},{8,12},{12,8},{16,20},{20,16},{24,28},{28,24},{1,5},{5... | collective-permute-start | bytes 8257544 | tf_op jit(solution)/shard_map/ppermute | solution.py:416
  73.8 32.4 %collective-permute-start.5 = (bf16[2,1344,512]{2,1,0:T(8,128)(2,1)}, bf16[2,1344,512]{2,1,0:T(8,128)(2,1)S(1)}, u32[]{:S(2)}, u32[]{:S(2)}) collective-permute-start(bf16[2,1344,512]{2,1,0:T(8,128)(2,1)} %collective-permute-done.3.refs_1_.refs_0_), channel_id=1, source_target_pairs={{0,1},{5,4},{2,3},{7,6},{8,9},{13,12},{10,11},{15,14},{16,17},{21,... | collective-permute-start | bytes 8257544 | tf_op jit(solution)/shard_map/ppermute | solution.py:427
  86.9 19.4 %collective-permute-start.7 = (bf16[128,2688]{1,0:T(8,128)(2,1)S(1)}, bf16[128,2688]{1,0:T(8,128)(2,1)S(1)}, u32[]{:S(2)}, u32[]{:S(2)}) collective-permute-start(bf16[128,2688]{1,0:T(8,128)(2,1)S(1)} %get-tuple-element.69), channel_id=1, source_target_pairs={{0,8},{4,12},{8,0},{12,4},{16,24},{20,28},{24,16},{28,20},{1,9},{5... | collective-permute-start | bytes 2064392 | tf_op jit(solution)/shard_map/ppermute | solution.py:496
  88.4 17.8 %collective-permute-start.8 = (bf16[128,2688]{1,0:T(8,128)(2,1)S(1)}, bf16[128,2688]{1,0:T(8,128)(2,1)S(1)}, u32[]{:S(2)}, u32[]{:S(2)}) collective-permute-start(bf16[128,2688]{1,0:T(8,128)(2,1)S(1)} %get-tuple-element.70), channel_id=1, source_target_pairs={{0,16},{4,20},{8,24},{12,28},{16,0},{20,4},{24,8},{28,12},{1,17},{... | collective-permute-start | bytes 2064392 | tf_op jit(solution)/shard_map/ppermute | solution.py:496
  106.3 6.8 %collective-permute-start.9 = (bf16[2,1344,512]{2,1,0:T(8,128)(2,1)S(1)}, bf16[2,1344,512]{2,1,0:T(8,128)(2,1)S(1)}, u32[]{:S(2)}, u32[]{:S(2)}) collective-permute-start(bf16[2,1344,512]{2,1,0:T(8,128)(2,1)S(1)} %collective-permute-done.5.refs_1_.refs_0_), channel_id=1, source_target_pairs={{0,4},{4,0},{8,12},{12,8},{16,20},{20,16},{24,28},{28,24},{1,5},{5... | collective-permute-start | bytes 8257544 | tf_op jit(solution)/shard_map/ppermute | solution.py:416
  108.3 18.3 %collective-permute-start.10 = (bf16[128,2688]{1,0:T(8,128)(2,1)S(1)}, bf16[128,2688]{1,0:T(8,128)(2,1)S(1)}, u32[]{:S(2)}, u32[]{:S(2)}) collective-permute-start(bf16[128,2688]{1,0:T(8,128)(2,1)S(1)} %get-tuple-element.79), channel_id=1, source_target_pairs={{0,8},{4,12},{8,0},{12,4},{16,24},{20,28},{24,16},{28,20},{1,9},{5... | collective-permute-start | bytes 2064392 | tf_op jit(solution)/shard_map/ppermute | solution.py:496
  113.0 13.6 %copy-start.5 = (bf16[512,1344]{1,0:T(8,128)(2,1)S(1)}, bf16[512,1344]{1,0:T(8,128)(2,1)}, u32[]{:S(2)}) copy-start(bf16[512,1344]{1,0:T(8,128)(2,1)} %get-tuple-element.125.refs_1_) | copy-start | bytes 4128772
  115.1 25.6 %collective-permute-start.11 = (bf16[128,2688]{1,0:T(8,128)(2,1)S(1)}, bf16[128,2688]{1,0:T(8,128)(2,1)S(1)}, u32[]{:S(2)}, u32[]{:S(2)}) collective-permute-start(bf16[128,2688]{1,0:T(8,128)(2,1)S(1)} %get-tuple-element.78), channel_id=1, source_target_pairs={{0,16},{4,20},{8,24},{12,28},{16,0},{20,4},{24,8},{28,12},{1,17},{... | collective-permute-start | bytes 2064392 | tf_op jit(solution)/shard_map/ppermute | solution.py:496
  116.7 24.0 %collective-permute-start.12 = (bf16[128,1344]{1,0:T(8,128)(2,1)S(1)}, bf16[128,1344]{1,0:T(8,128)(2,1)S(1)}, u32[]{:S(2)}, u32[]{:S(2)}) collective-permute-start(bf16[128,1344]{1,0:T(8,128)(2,1)S(1)} %get-tuple-element.86), channel_id=1, source_target_pairs={{0,16},{4,20},{8,24},{12,28},{16,0},{20,4},{24,8},{28,12},{1,17},{... | collective-permute-start | bytes 1032200 | tf_op jit(solution)/shard_map/ppermute | solution.py:496
  117.2 23.5 %collective-permute-start.13 = (bf16[128,1344]{1,0:T(8,128)(2,1)S(1)}, bf16[128,1344]{1,0:T(8,128)(2,1)S(1)}, u32[]{:S(2)}, u32[]{:S(2)}) collective-permute-start(bf16[128,1344]{1,0:T(8,128)(2,1)S(1)} %get-tuple-element.87), channel_id=1, source_target_pairs={{0,8},{4,12},{8,0},{12,4},{16,24},{20,28},{24,16},{28,20},{1,9},{5... | collective-permute-start | bytes 1032200 | tf_op jit(solution)/shard_map/ppermute | solution.py:496
  140.8 4.4 %copy-start.1 = (bf16[1024,1024]{1,0:T(8,128)(2,1)S(1)}, bf16[1024,1024]{1,0:T(8,128)(2,1)}, u32[]{:S(2)}) copy-start(bf16[1024,1024]{1,0:T(8,128)(2,1)} %copy-done) | copy-start | bytes 6291460
  143.6 20.3 %collective-permute-start.14 = (bf16[2,2,512,128]{3,2,1,0:T(8,128)(2,1)}, bf16[2,2,512,128]{3,2,1,0:T(8,128)(2,1)S(1)}, u32[]{:S(2)}, u32[]{:S(2)}) collective-permute-start(bf16[2,2,512,128]{3,2,1,0:T(8,128)(2,1)} %get-tuple-element.102), channel_id=1, source_target_pairs={{8,0},{12,4},{16,8},{20,12},{24,16},{28,20},{9,1},{13,5},{17,9},{2... | collective-permute-start | bytes 1572872 | tf_op jit(solution)/shard_map/ppermute | solution.py:411
  151.2 12.8 %collective-permute-start.15 = (bf16[2,1,512,128]{3,2,1,0:T(8,128)(2,1)S(1)}, bf16[2,1,512,128]{3,2,1,0:T(8,128)(2,1)S(1)}, u32[]{:S(2)}, u32[]{:S(2)}) collective-permute-start(bf16[2,1,512,128]{3,2,1,0:T(8,128)(2,1)S(1)} %get-tuple-element.103), channel_id=1, source_target_pairs={{8,0},{12,4},{16,8},{20,12},{24,16},{28,20},{9,1},{13,5},{17,9},{2... | collective-permute-start | bytes 786440 | tf_op jit(solution)/shard_map/ppermute | solution.py:411
  158.5 5.6 %copy-start.15 = (bf16[128,1344]{1,0:T(8,128)(2,1)S(1)}, bf16[128,1344]{1,0:T(8,128)(2,1)}, u32[]{:S(2)}) copy-start(bf16[128,1344]{1,0:T(8,128)(2,1)} %copy-done.14) | copy-start | bytes 1032196
  158.5 7.2 %copy-start.13 = (bf16[128,1344]{1,0:T(8,128)(2,1)S(1)}, bf16[128,1344]{1,0:T(8,128)(2,1)}, u32[]{:S(2)}) copy-start(bf16[128,1344]{1,0:T(8,128)(2,1)} %copy-done.12) | copy-start | bytes 1032196
  158.5 18.5 %copy-start.9 = (bf16[128,1344]{1,0:T(8,128)(2,1)S(1)}, bf16[128,1344]{1,0:T(8,128)(2,1)}, u32[]{:S(2)}) copy-start(bf16[128,1344]{1,0:T(8,128)(2,1)} %copy-done.8) | copy-start | bytes 1032196
  164.0 18.1 %collective-permute-start.16 = (bf16[512,512]{1,0:T(8,128)(2,1)S(1)}, bf16[512,512]{1,0:T(8,128)(2,1)S(1)}, u32[]{:S(2)}, u32[]{:S(2)}) collective-permute-start(bf16[512,512]{1,0:T(8,128)(2,1)S(1)} %broadcast_select_fusion.4), channel_id=1, source_target_pairs={{0,4},{4,0},{8,12},{12,8},{16,20},{20,16},{24,28},{28,24},{1,5},{5... | collective-permute-start | bytes 1572872 | tf_op jit(solution)/shard_map/ppermute | solution.py:416
  164.1 10.8 %collective-permute-start.18 = (bf16[128,1344]{1,0:T(8,128)(2,1)S(1)}, bf16[128,1344]{1,0:T(8,128)(2,1)S(1)}, u32[]{:S(2)}, u32[]{:S(2)}) collective-permute-start(bf16[128,1344]{1,0:T(8,128)(2,1)S(1)} %copy-done.15), channel_id=1, source_target_pairs={{0,16},{4,20},{8,24},{12,28},{16,0},{20,4},{24,8},{28,12},{1,17},{... | collective-permute-start | bytes 1032200 | tf_op jit(solution)/shard_map/ppermute | solution.py:496
  165.7 11.3 %collective-permute-start.19 = (bf16[128,1344]{1,0:T(8,128)(2,1)S(1)}, bf16[128,1344]{1,0:T(8,128)(2,1)S(1)}, u32[]{:S(2)}, u32[]{:S(2)}) collective-permute-start(bf16[128,1344]{1,0:T(8,128)(2,1)S(1)} %copy-done.13), channel_id=1, source_target_pairs={{0,8},{4,12},{8,0},{12,4},{16,24},{20,28},{24,16},{28,20},{1,9},{5... | collective-permute-start | bytes 1032200 | tf_op jit(solution)/shard_map/ppermute | solution.py:496
  166.7 15.1 %collective-permute-start.17 = (bf16[2,1,512,128]{3,2,1,0:T(8,128)(2,1)S(1)}, bf16[2,1,512,128]{3,2,1,0:T(8,128)(2,1)S(1)}, u32[]{:S(2)}, u32[]{:S(2)}) collective-permute-start(bf16[2,1,512,128]{3,2,1,0:T(8,128)(2,1)S(1)} %get-tuple-element.109), channel_id=1, source_target_pairs={{8,0},{12,4},{16,8},{20,12},{24,16},{28,20},{9,1},{13,5},{17,9},{2... | collective-permute-start | bytes 786440 | tf_op jit(solution)/shard_map/ppermute | solution.py:411
  182.0 2.0 %collective-permute-start.20 = (bf16[2,2,512,128]{3,2,1,0:T(8,128)(2,1)S(1)}, bf16[2,2,512,128]{3,2,1,0:T(8,128)(2,1)S(1)}, u32[]{:S(2)}, u32[]{:S(2)}) collective-permute-start(bf16[2,2,512,128]{3,2,1,0:T(8,128)(2,1)S(1)} %get-tuple-element.120), channel_id=1, source_target_pairs={{0,4},{4,0},{8,12},{12,8},{16,20},{20,16},{24,28},{28,24},{1,5},{5... | collective-permute-start | bytes 1572872 | tf_op jit(solution)/shard_map/ppermute | solution.py:416
  (10 other events, 15.3 us)

commit v4 on v3

--- a/solution.py
+++ b/solution.py
@@ -535,7 +535,7 @@
     for g in range(all_groups[1]):
         part = backward(1, (g, 1), packet, before, attention, grads, carry, head_size)
         if g > 0:
-            part, from_low, from_high = lax.optimization_barrier((part, from_low, from_high))
+            part, from_low = lax.optimization_barrier((part, from_low))
         parts.append(part)
         from_high.append(shift(part[1], -2))
     query_high = jnp.concatenate([part[0] for part in parts], axis=1)

time: 186 us -> 188 us (1.011)
  transfers between devices with their start and end apart: 21 -> 21, of which waited for: 12 -> 13; matrix products, arithmetic and copies ran while one was open for 12% -> 12% of each run, Pallas kernels for 34% -> 34%
where the time goes in v4:
time: 188 us; the launch traced here: 187 us
  Pallas kernels  66.4 us (35%)
  waiting for transfers between devices  65.7 us (35%)
  starting transfers between devices  28.3 us (15%)
  local copies, waits for them, and re-layouts  14.6 us (8%)
  other arithmetic  10.8 us (6%)
    ppermute x2, waiting for transfers between devices, move(): return lax.ppermute(shard, ('ctx', 'head'), places)  24.8 us
    pallas_call x3, Pallas kernels, backward(): pl.pallas_call(functools.partial(backward_kernel, phase), grid=(count, ti...  23.1 us
    ppermute x4, waiting for transfers between devices, shift(): lax.ppermute(shard, 'ctx', [(i, i + by) for i in range(size) if 0 <= i +...  16.1 us
    ppermute x8, waiting for transfers between devices, exchange(): lax.ppermute(shard, 'ctx', [(i, i ^ 2 * distance) for i in range(n_ctx)])  16 us
    pallas_call x1, Pallas kernels, forward(): pl.pallas_call(forward_kernel, grid_spec=grid_spec, out_shape=[jax.ShapeD...  15 us
    pallas_call x3, Pallas kernels, add_grads(): pl.pallas_call(functools.partial(grads_kernel, number, len(others) > 0),...  13.1 us
    ppermute x8, starting transfers between devices, exchange(): lax.ppermute(shard, 'ctx', [(i, i ^ 2 * distance) for i in range(n_ctx)])  12 us
    pallas_call x3, Pallas kernels, make_terms(): pl.pallas_call(functools.partial(terms_kernel, orders, len(waiting), len(...  10.2 us
  transfers between devices with their start and end apart: 21, of which 13 were waited for; matrix products, arithmetic and copies ran while one was open for 12% of the time, Pallas kernels for 34%

profile of v4, /device:TPU:0, one launch (start us, length us, event | category | flops | bytes accessed | tf_op | source)
XLA Modules:
  0.0 187.0 jit_solution(11171176181855907458)
XLA Ops:
  6.6 1.8 pad_maximum_fusion.refs_0_
  8.4 3.0 %collective-permute-start.3 = (bf16[2,1344,512]{2,1,0:T(8,128)(2,1)}, bf16[2,1344,512]{2,1,0:T(8,128)(2,1)}, u32[]{:S(2)}, u32[]{:S(2)}) collective-permute-start(bf16[2,1344,512]{2,1,0:T(8,128)(2,1)} %pad_maximum_fusion.refs_0_), channel_id=1, source_target_pairs={{0,1},{1,2},{2,3},{3,0},{4,7},{5,4},{6,5},{7,6},{8,9},{9,10},{10,1... | collective-permute-start | bytes 8257544 | tf_op jit(solution)/shard_map/ppermute | solution.py:427
  11.3 1.7 broadcast_select_fusion.1
  14.2 3.4 %collective-permute-start.1 = (bf16[1024,512]{1,0:T(8,128)(2,1)}, bf16[1024,512]{1,0:T(8,128)(2,1)S(1)}, u32[]{:S(2)}, u32[]{:S(2)}) collective-permute-start(bf16[1024,512]{1,0:T(8,128)(2,1)} %fusion), channel_id=1, source_target_pairs={{0,8},{4,12},{8,16},{12,20},{16,24},{20,28},{1,9},{5,13},{9,17},{1... | collective-permute-start | bytes 3145736 | tf_op jit(solution)/shard_map/ppermute | solution.py:411
  17.7 8.5 %fusion.5 = (bf16[512,1344]{1,0:T(8,128)(2,1)}, bf16[512,1344]{1,0:T(8,128)(2,1)}, bf16[512,1344]{1,0:T(8,128)(2,1)S(1)}, bf16[512,1344]{1,0:T(8,128)(2,1)}) fusion(bf16[1024,5376]{1,0:T(8,128)(2,1)} %param.13, s32[]{:T(128)S(6)} %select_n.170, s32[]{:T(128)S(6)} %select_n.184, s32[]{:T(128)S(6)} %select_n.177, s32[]{:T(128)S(6)} %select_n.173, s32[]{:T(128)S(6)} %select_n.181), kind=kLoop, calls=%fused_computation.47 | loop fusion | bytes 11010068 | tf_op jit(solution)/shard_map/dynamic_slice | solution.py:480
  26.4 4.7 %out_grads.3.refs_4_ = f32[512,1024]{1,0:T(8,128)S(1)} custom-call(bf16[2,1344,512]{2,1,0:T(8,128)(2,1)} %pad_maximum_fusion.refs_0_, bf16[512,1344]{1,0:T(8,128)(2,1)S(1)} %get-tuple-element.125.refs_1_), custom_call_target="tpu_custom_call" | custom-call | flops 1 | bytes 1 | tf_op jit(solution)/shard_map/out_grads/pallas_call | solution.py:238
  32.4 8.2 %collective-permute-done.1.pk_ref.pv_ref = bf16[1024,512]{1,0:T(8,128)(2,1)S(1)} collective-permute-done((bf16[1024,512]{1,0:T(8,128)(2,1)}, bf16[1024,512]{1,0:T(8,128)(2,1)S(1)}, u32[]{:S(2)}, u32[]{:S(2)}) %collective-permute-start.1) | collective-permute-done | bytes 1048608 | tf_op jit(solution)/shard_map/ppermute | solution.py:411
  40.5 15.0 %attention_forward.1 = (f32[2,4,1280,512]{3,2,1,0:T(8,128)}, bf16[512,1024]{1,0:T(8,128)(2,1)S(1)}) custom-call(s32[1]{0:T(128)} %bitcast.5.chip_ref, bf16[1024,1024]{1,0:T(8,128)(2,1)S(1)} %pad_maximum_fusion.1.q_ref.k_ref.v_ref, bf16[1024,1024]{1,0:T(8,128)(2,1)S(1)} %pad_maximum_fusion.1.q_ref.k_ref.v_ref, ...), custom_call_target="tpu_custom_call" | custom-call | flops 1 | bytes 1 | tf_op jit(solution)/shard_map/attention_forward/pallas_call | solution.py:102
  56.6 1.7 collective-permute-done.4
  59.9 13.9 %collective-permute-done.3.refs_1_.refs_0_ = bf16[2,1344,512]{2,1,0:T(8,128)(2,1)} collective-permute-done((bf16[2,1344,512]{2,1,0:T(8,128)(2,1)}, bf16[2,1344,512]{2,1,0:T(8,128)(2,1)}, u32[]{:S(2)}, u32[]{:S(2)}) %collective-permute-start.3) | collective-permute-done | bytes 2752544 | tf_op jit(solution)/shard_map/ppermute | solution.py:427
  73.8 1.9 %collective-permute-start.5 = (bf16[2,1344,512]{2,1,0:T(8,128)(2,1)}, bf16[2,1344,512]{2,1,0:T(8,128)(2,1)S(1)}, u32[]{:S(2)}, u32[]{:S(2)}) collective-permute-start(bf16[2,1344,512]{2,1,0:T(8,128)(2,1)} %collective-permute-done.3.refs_1_.refs_0_), channel_id=1, source_target_pairs={{0,1},{5,4},{2,3},{7,6},{8,9},{13,12},{10,11},{15,14},{16,17},{21,... | collective-permute-start | bytes 8257544 | tf_op jit(solution)/shard_map/ppermute | solution.py:427
  75.7 3.4 %collective-permute-done.6.refs_2_.refs_1_ = bf16[2,1344,512]{2,1,0:T(8,128)(2,1)S(1)} collective-permute-done((bf16[2,1344,512]{2,1,0:T(8,128)(2,1)}, bf16[2,1344,512]{2,1,0:T(8,128)(2,1)S(1)}, u32[]{:S(2)}, u32[]{:S(2)}) %collective-permute-start.6) | collective-permute-done | bytes 2752544 | tf_op jit(solution)/shard_map/ppermute | solution.py:416
  79.1 7.8 %weight_terms.3 = (f32[128,1344]{1,0:T(8,128)S(1)}, f32[128,1344]{1,0:T(8,128)S(1)}, bf16[128,2688]{1,0:T(8,128)(2,1)S(1)}, f32[128,1344]{1,0:T(8,128)S(1)}, f32...) custom-call(bf16[512,1024]{1,0:T(8,128)(2,1)S(1)} %bitcast.25, ...), custom_call_target="tpu_custom_call" | custom-call | flops 1 | bytes 1 | tf_op jit(solution)/shard_map/weight_terms/pallas_call | solution.py:289
  86.9 1.6 collective-permute-start.7
  90.0 5.4 %out_grads.4.refs_3_ = f32[512,1024]{1,0:T(8,128)S(1)} custom-call(bf16[2,1344,512]{2,1,0:T(8,128)(2,1)} %collective-permute-done.3.refs_1_.refs_0_, bf16[2,1344,512]{2,1,0:T(8,128)(2,1)S(1)} %collective-permute-done.6.refs_2_.refs_1_, bf16[512,1344]{1,0:T(8,128)(2,1)S(1)} %copy-done.6, bf16[512,1344]{1,0:T(8,128)(2,1)S(1)} %copy-done.7, ...), custom_call_target="tpu_custom_call" | custom-call | flops 1 | bytes 1 | tf_op jit(solution)/shard_map/out_grads/pallas_call | solution.py:238
  95.4 10.9 %collective-permute-done.5.refs_1_.refs_0_ = bf16[2,1344,512]{2,1,0:T(8,128)(2,1)S(1)} collective-permute-done((bf16[2,1344,512]{2,1,0:T(8,128)(2,1)}, bf16[2,1344,512]{2,1,0:T(8,128)(2,1)S(1)}, u32[]{:S(2)}, u32[]{:S(2)}) %collective-permute-start.5) | collective-permute-done | bytes 2752544 | tf_op jit(solution)/shard_map/ppermute | solution.py:427
  106.3 2.1 %collective-permute-start.9 = (bf16[2,1344,512]{2,1,0:T(8,128)(2,1)S(1)}, bf16[2,1344,512]{2,1,0:T(8,128)(2,1)S(1)}, u32[]{:S(2)}, u32[]{:S(2)}) collective-permute-start(bf16[2,1344,512]{2,1,0:T(8,128)(2,1)S(1)} %collective-permute-done.5.refs_1_.refs_0_), channel_id=1, source_target_pairs={{0,4},{4,0},{8,12},{12,8},{16,20},{20,16},{24,28},{28,24},{1,5},{5... | collective-permute-start | bytes 8257544 | tf_op jit(solution)/shard_map/ppermute | solution.py:416
  109.8 3.2 %collective-permute-done.9.refs_0_.refs_2_ = bf16[2,1344,512]{2,1,0:T(8,128)(2,1)S(1)} collective-permute-done((bf16[2,1344,512]{2,1,0:T(8,128)(2,1)S(1)}, bf16[2,1344,512]{2,1,0:T(8,128)(2,1)S(1)}, u32[]{:S(2)}, u32[]{:S(2)}) %collective-permute-start.9) | collective-permute-done | bytes 2752544 | tf_op jit(solution)/shard_map/ppermute | solution.py:416
  113.0 2.1 %weight_terms.4 = (f32[128,1344]{1,0:T(8,128)S(1)}, f32[128,1344]{1,0:T(8,128)S(1)}, bf16[128,2688]{1,0:T(8,128)(2,1)S(1)}, f32[128,1344]{1,0:T(8,128)S(1)}, bf1...) custom-call(bf16[512,1024]{1,0:T(8,128)(2,1)S(1)} %bitcast.26, ...), custom_call_target="tpu_custom_call" | custom-call | flops 1 | bytes 1 | tf_op jit(solution)/shard_map/weight_terms/pallas_call | solution.py:289
  115.1 1.6 collective-permute-start.11
  118.7 7.9 %collective-permute-done.10.refs_2_ = bf16[128,2688]{1,0:T(8,128)(2,1)S(1)} collective-permute-done((bf16[128,2688]{1,0:T(8,128)(2,1)S(1)}, bf16[128,2688]{1,0:T(8,128)(2,1)S(1)}, u32[]{:S(2)}, u32[]{:S(2)}) %collective-permute-start.10) | collective-permute-done | bytes 688160 | tf_op jit(solution)/shard_map/ppermute | solution.py:496
  126.6 3.0 %out_grads.5.do_ref = bf16[512,1024]{1,0:T(8,128)(2,1)S(1)} custom-call(bf16[2,1344,512]{2,1,0:T(8,128)(2,1)S(1)} %collective-permute-done.5.refs_1_.refs_0_, bf16[512,1344]{1,0:T(8,128)(2,1)S(1)} %copy-done.5, bf16[2,1344,512]{2,1,0:T(8,128)(2,1)S(1)} %collective-permute-done.9.refs_0_.refs_2_, f32[512,1024]{1,0:T(8,128)S(1)} %out_grads.4.refs_3_), custom_call_target="tpu_custom_call" | custom-call | flops 1 | bytes 1 | tf_op jit(solution)/shard_map/out_grads/pallas_call | solution.py:238
  129.7 11.1 %attention_backward.3 = (bf16[512,512]{1,0:T(8,128)(2,1)S(1)}, bf16[2,2,512,128]{3,2,1,0:T(8,128)(2,1)}, f32[2,2,1024,128]{3,2,1,0:T(8,128)S(1)}) custom-call(bf16[1024,1024]{1,0:T(8,128)(2,1)} %copy-done, bf16[1024,1024]{1,0:T(8,128)(2,1)} %copy-done, bf16[1024,1024]{1,0:T(8,128)(2,1)} %copy-done, ...), custom_call_target="tpu_custom_call" | custom-call | flops 1 | bytes 1 | tf_op jit(solution)/shard_map/attention_backward/pallas_call | solution.py:184
  145.2 6.0 %attention_backward.5 = (bf16[512,256]{1,0:T(8,128)(2,1)S(1)}, bf16[2,1,512,128]{3,2,1,0:T(8,128)(2,1)S(1)}, f32[2,1,1024,128]{3,2,1,0:T(8,128)S(1)}) custom-call(bf16[1024,1024]{1,0:T(8,128)(2,1)S(1)} %copy-done.1, bf16[1024,1024]{1,0:T(8,128)(2,1)S(1)} %copy-done.1, bf16[1024,1024]{1,0:T(8,128)(2,1)S(1)} %copy-done.1, ...), custom_call_target="tpu_custom_call" | custom-call | flops 1 | bytes 1 | tf_op jit(solution)/shard_map/attention_backward/pallas_call | solution.py:184
  151.2 6.0 %attention_backward.4 = (bf16[512,256]{1,0:T(8,128)(2,1)S(1)}, bf16[2,1,512,128]{3,2,1,0:T(8,128)(2,1)S(1)}, f32[2,1,1024,128]{3,2,1,0:T(8,128)S(1)}) custom-call(bf16[1024,1024]{1,0:T(8,128)(2,1)S(1)} %copy-done.1, bf16[1024,1024]{1,0:T(8,128)(2,1)S(1)} %copy-done.1, bf16[1024,1024]{1,0:T(8,128)(2,1)S(1)} %copy-done.1, ...), custom_call_target="tpu_custom_call" | custom-call | flops 1 | bytes 1 | tf_op jit(solution)/shard_map/attention_backward/pallas_call | solution.py:184
  158.5 3.3 %collective-permute-start.18 = (bf16[128,1344]{1,0:T(8,128)(2,1)S(1)}, bf16[128,1344]{1,0:T(8,128)(2,1)S(1)}, u32[]{:S(2)}, u32[]{:S(2)}) collective-permute-start(bf16[128,1344]{1,0:T(8,128)(2,1)S(1)} %copy-done.15), channel_id=1, source_target_pairs={{0,16},{4,20},{8,24},{12,28},{16,0},{20,4},{24,8},{28,12},{1,17},{... | collective-permute-start | bytes 1032200 | tf_op jit(solution)/shard_map/ppermute | solution.py:496
  165.0 5.0 %collective-permute-done.18.refs_3_ = bf16[128,1344]{1,0:T(8,128)(2,1)S(1)} collective-permute-done((bf16[128,1344]{1,0:T(8,128)(2,1)S(1)}, bf16[128,1344]{1,0:T(8,128)(2,1)S(1)}, u32[]{:S(2)}, u32[]{:S(2)}) %collective-permute-start.18) | collective-permute-done | bytes 344096 | tf_op jit(solution)/shard_map/ppermute | solution.py:496
  170.1 3.0 %collective-permute-done.19.refs_7_ = bf16[128,1344]{1,0:T(8,128)(2,1)S(1)} collective-permute-done((bf16[128,1344]{1,0:T(8,128)(2,1)S(1)}, bf16[128,1344]{1,0:T(8,128)(2,1)S(1)}, u32[]{:S(2)}, u32[]{:S(2)}) %collective-permute-start.19) | collective-permute-done | bytes 344096 | tf_op jit(solution)/shard_map/ppermute | solution.py:496
  173.1 2.8 %place_terms.1 = f32[128,5376]{1,0:T(8,128)} custom-call(s32[4]{0:T(128)S(1)} %pad_add_fusion.1.at_ref, f32[128,1344]{1,0:T(8,128)S(1)} %get-tuple-element.108.refs_0_, bf16[128,1344]{1,0:T(8,128)(2,1)S(1)} %collective-permute-done.12.refs_1_, f32[128,1344]{1,0:T(8,128)S(1)} %get-tuple-element.110.refs_2_, ...), custom_call_target="tpu_custom_call" | custom-call | flops 1 | bytes 1 | tf_op jit(solution)/shard_map/place_terms/pallas_call | solution.py:394
  175.9 2.8 %collective-permute-done.16.refs_2_ = bf16[2,1,512,128]{3,2,1,0:T(8,128)(2,1)S(1)} collective-permute-done((bf16[2,1,512,128]{3,2,1,0:T(8,128)(2,1)S(1)}, bf16[2,1,512,128]{3,2,1,0:T(8,128)(2,1)S(1)}, u32[]{:S(2)}, u32[]{:S(2)}) %collective-permute-start.16) | collective-permute-done | bytes 262176 | tf_op jit(solution)/shard_map/ppermute | solution.py:411
  178.7 4.1 %collective-permute-done.17.refs_3_ = bf16[2,1,512,128]{3,2,1,0:T(8,128)(2,1)S(1)} collective-permute-done((bf16[2,1,512,128]{3,2,1,0:T(8,128)(2,1)S(1)}, bf16[2,1,512,128]{3,2,1,0:T(8,128)(2,1)S(1)}, u32[]{:S(2)}, u32[]{:S(2)}) %collective-permute-start.17) | collective-permute-done | bytes 262176 | tf_op jit(solution)/shard_map/ppermute | solution.py:411
  185.0 2.0 %place_sums.1 = (bf16[512,512]{1,0:T(8,128)(2,1)}, bf16[512,512]{1,0:T(8,128)(2,1)}, bf16[512,512]{1,0:T(8,128)(2,1)}) custom-call(s32[2]{0:T(128)S(1)} %pad_add_fusion.where_ref, s32[4]{0:T(128)S(1)} %copy-done.11, s32[4]{0:T(128)S(1)} %copy-done.10, bf16[2,2,512,128]{3,2,1,0:T(8,128)(2,1)S(1)} %get-tuple-element.117.keep_ref, ...), custom_call_target="tpu_custom_call" | custom-call | flops 1 | bytes 1 | tf_op jit(solution)/shard_map/place_sums/pallas_call | solution.py:364
  (91 shorter events, 27.3 us)
Async XLA Ops:
  0.7 2.0 %copy-start.18 = (bf16[512,512]{1,0:T(8,128)(2,1)S(1)}, bf16[512,512]{1,0:T(8,128)(2,1)}, u32[]{:S(2)}) copy-start(bf16[512,512]{1,0:T(8,128)(2,1)} %param.11) | copy-start | bytes 1572868
  0.7 2.0 %copy-start.19 = (bf16[512,512]{1,0:T(8,128)(2,1)S(1)}, bf16[512,512]{1,0:T(8,128)(2,1)}, u32[]{:S(2)}) copy-start(bf16[512,512]{1,0:T(8,128)(2,1)} %param.9) | copy-start | bytes 1572868
  0.7 4.4 %collective-permute-start.2 = (bf16[1344,512]{1,0:T(8,128)(2,1)}, bf16[1344,512]{1,0:T(8,128)(2,1)}, u32[]{:S(2)}, u32[]{:S(2)}) collective-permute-start(bf16[1344,512]{1,0:T(8,128)(2,1)} %bitcast.30), channel_id=1, source_target_pairs={{0,4},{4,0},{8,12},{12,8},{16,20},{20,16},{24,28},{28,24},{1,5},{5... | collective-permute-start | bytes 4128776 | tf_op jit(solution)/shard_map/ppermute | solution.py:416
  4.9 6.4 %collective-permute-start = (bf16[512,1024]{1,0:T(8,128)(2,1)}, bf16[512,1024]{1,0:T(8,128)(2,1)}, u32[]{:S(2)}, u32[]{:S(2)}) collective-permute-start(bf16[512,1024]{1,0:T(8,128)(2,1)} %pad_maximum_fusion.3), channel_id=1, source_target_pairs={{0,4},{4,0},{8,12},{12,8},{16,20},{20,16},{24,28},{28,24},{1,5},{5... | collective-permute-start | bytes 3145736 | tf_op jit(solution)/shard_map/ppermute | solution.py:416
  6.6 4.8 %copy-start.17 = (bf16[512,256]{1,0:T(8,128)(2,1)S(1)}, bf16[512,256]{1,0:T(8,128)(2,1)}, u32[]{:S(2)}) copy-start(bf16[512,256]{1,0:T(8,128)(2,1)} %get-tuple-element.146) | copy-start | bytes 786436
  8.4 65.4 %collective-permute-start.3 = (bf16[2,1344,512]{2,1,0:T(8,128)(2,1)}, bf16[2,1344,512]{2,1,0:T(8,128)(2,1)}, u32[]{:S(2)}, u32[]{:S(2)}) collective-permute-start(bf16[2,1344,512]{2,1,0:T(8,128)(2,1)} %pad_maximum_fusion.refs_0_), channel_id=1, source_target_pairs={{0,1},{1,2},{2,3},{3,0},{4,7},{5,4},{6,5},{7,6},{8,9},{9,10},{10,1... | collective-permute-start | bytes 8257544 | tf_op jit(solution)/shard_map/ppermute | solution.py:427
  14.2 26.4 %collective-permute-start.1 = (bf16[1024,512]{1,0:T(8,128)(2,1)}, bf16[1024,512]{1,0:T(8,128)(2,1)S(1)}, u32[]{:S(2)}, u32[]{:S(2)}) collective-permute-start(bf16[1024,512]{1,0:T(8,128)(2,1)} %fusion), channel_id=1, source_target_pairs={{0,8},{4,12},{8,16},{12,20},{16,24},{20,28},{1,9},{5,13},{9,17},{1... | collective-permute-start | bytes 3145736 | tf_op jit(solution)/shard_map/ppermute | solution.py:411
  26.4 14.2 %copy-start = (bf16[1024,1024]{1,0:T(8,128)(2,1)}, bf16[1024,1024]{1,0:T(8,128)(2,1)S(1)}, u32[]{:S(2)}) copy-start(bf16[1024,1024]{1,0:T(8,128)(2,1)S(1)} %pad_maximum_fusion.1.q_ref.k_ref.v_ref) | copy-start | bytes 6291460
  55.5 2.7 %collective-permute-start.4 = (bf16[2,128,1024]{2,1,0:T(8,128)(2,1)S(1)}, bf16[2,128,1024]{2,1,0:T(8,128)(2,1)}, u32[]{:S(2)}, u32[]{:S(2)}) collective-permute-start(bf16[2,128,1024]{2,1,0:T(8,128)(2,1)S(1)} %dynamic-slice_bitcast_fusion), channel_id=1, source_target_pairs={{0,4},{4,0},{8,12},{12,8},{16,20},{20,16},{24,28},{28,24},{1,5},{5... | collective-permute-start | bytes 1572872 | tf_op jit(solution)/shard_map/ppermute | solution.py:416
  73.8 16.2 %copy-start.4 = (f32[512,1024]{1,0:T(8,128)S(1)}, f32[512,1024]{1,0:T(8,128)}, u32[]{:S(2)}) copy-start(f32[512,1024]{1,0:T(8,128)} %copy-done.3) | copy-start | bytes 6291460
  73.8 16.2 %copy-start.6 = (bf16[512,1344]{1,0:T(8,128)(2,1)S(1)}, bf16[512,1344]{1,0:T(8,128)(2,1)}, u32[]{:S(2)}) copy-start(bf16[512,1344]{1,0:T(8,128)(2,1)} %get-tuple-element.124.refs_2_) | copy-start | bytes 4128772
  73.8 16.2 %copy-start.7 = (bf16[512,1344]{1,0:T(8,128)(2,1)S(1)}, bf16[512,1344]{1,0:T(8,128)(2,1)}, u32[]{:S(2)}) copy-start(bf16[512,1344]{1,0:T(8,128)(2,1)} %get-tuple-element.126.refs_3_) | copy-start | bytes 4128772
  73.8 5.3 %collective-permute-start.6 = (bf16[2,1344,512]{2,1,0:T(8,128)(2,1)}, bf16[2,1344,512]{2,1,0:T(8,128)(2,1)S(1)}, u32[]{:S(2)}, u32[]{:S(2)}) collective-permute-start(bf16[2,1344,512]{2,1,0:T(8,128)(2,1)} %collective-permute-done.3.refs_1_.refs_0_), channel_id=1, source_target_pairs={{0,4},{4,0},{8,12},{12,8},{16,20},{20,16},{24,28},{28,24},{1,5},{5... | collective-permute-start | bytes 8257544 | tf_op jit(solution)/shard_map/ppermute | solution.py:416
  73.8 32.4 %collective-permute-start.5 = (bf16[2,1344,512]{2,1,0:T(8,128)(2,1)}, bf16[2,1344,512]{2,1,0:T(8,128)(2,1)S(1)}, u32[]{:S(2)}, u32[]{:S(2)}) collective-permute-start(bf16[2,1344,512]{2,1,0:T(8,128)(2,1)} %collective-permute-done.3.refs_1_.refs_0_), channel_id=1, source_target_pairs={{0,1},{5,4},{2,3},{7,6},{8,9},{13,12},{10,11},{15,14},{16,17},{21,... | collective-permute-start | bytes 8257544 | tf_op jit(solution)/shard_map/ppermute | solution.py:427
  86.9 19.4 %collective-permute-start.7 = (bf16[128,2688]{1,0:T(8,128)(2,1)S(1)}, bf16[128,2688]{1,0:T(8,128)(2,1)S(1)}, u32[]{:S(2)}, u32[]{:S(2)}) collective-permute-start(bf16[128,2688]{1,0:T(8,128)(2,1)S(1)} %get-tuple-element.68), channel_id=1, source_target_pairs={{0,8},{4,12},{8,0},{12,4},{16,24},{20,28},{24,16},{28,20},{1,9},{5... | collective-permute-start | bytes 2064392 | tf_op jit(solution)/shard_map/ppermute | solution.py:496
  88.4 17.8 %collective-permute-start.8 = (bf16[128,2688]{1,0:T(8,128)(2,1)S(1)}, bf16[128,2688]{1,0:T(8,128)(2,1)S(1)}, u32[]{:S(2)}, u32[]{:S(2)}) collective-permute-start(bf16[128,2688]{1,0:T(8,128)(2,1)S(1)} %get-tuple-element.69), channel_id=1, source_target_pairs={{0,16},{4,20},{8,24},{12,28},{16,0},{20,4},{24,8},{28,12},{1,17},{... | collective-permute-start | bytes 2064392 | tf_op jit(solution)/shard_map/ppermute | solution.py:496
  106.3 6.8 %collective-permute-start.9 = (bf16[2,1344,512]{2,1,0:T(8,128)(2,1)S(1)}, bf16[2,1344,512]{2,1,0:T(8,128)(2,1)S(1)}, u32[]{:S(2)}, u32[]{:S(2)}) collective-permute-start(bf16[2,1344,512]{2,1,0:T(8,128)(2,1)S(1)} %collective-permute-done.5.refs_1_.refs_0_), channel_id=1, source_target_pairs={{0,4},{4,0},{8,12},{12,8},{16,20},{20,16},{24,28},{28,24},{1,5},{5... | collective-permute-start | bytes 8257544 | tf_op jit(solution)/shard_map/ppermute | solution.py:416
  108.3 18.3 %collective-permute-start.10 = (bf16[128,2688]{1,0:T(8,128)(2,1)S(1)}, bf16[128,2688]{1,0:T(8,128)(2,1)S(1)}, u32[]{:S(2)}, u32[]{:S(2)}) collective-permute-start(bf16[128,2688]{1,0:T(8,128)(2,1)S(1)} %get-tuple-element.78), channel_id=1, source_target_pairs={{0,8},{4,12},{8,0},{12,4},{16,24},{20,28},{24,16},{28,20},{1,9},{5... | collective-permute-start | bytes 2064392 | tf_op jit(solution)/shard_map/ppermute | solution.py:496
  113.0 13.6 %copy-start.5 = (bf16[512,1344]{1,0:T(8,128)(2,1)S(1)}, bf16[512,1344]{1,0:T(8,128)(2,1)}, u32[]{:S(2)}) copy-start(bf16[512,1344]{1,0:T(8,128)(2,1)} %get-tuple-element.123.refs_1_) | copy-start | bytes 4128772
  115.1 25.6 %collective-permute-start.11 = (bf16[128,2688]{1,0:T(8,128)(2,1)S(1)}, bf16[128,2688]{1,0:T(8,128)(2,1)S(1)}, u32[]{:S(2)}, u32[]{:S(2)}) collective-permute-start(bf16[128,2688]{1,0:T(8,128)(2,1)S(1)} %get-tuple-element.77), channel_id=1, source_target_pairs={{0,16},{4,20},{8,24},{12,28},{16,0},{20,4},{24,8},{28,12},{1,17},{... | collective-permute-start | bytes 2064392 | tf_op jit(solution)/shard_map/ppermute | solution.py:496
  116.7 24.0 %collective-permute-start.12 = (bf16[128,1344]{1,0:T(8,128)(2,1)S(1)}, bf16[128,1344]{1,0:T(8,128)(2,1)S(1)}, u32[]{:S(2)}, u32[]{:S(2)}) collective-permute-start(bf16[128,1344]{1,0:T(8,128)(2,1)S(1)} %get-tuple-element.85), channel_id=1, source_target_pairs={{0,16},{4,20},{8,24},{12,28},{16,0},{20,4},{24,8},{28,12},{1,17},{... | collective-permute-start | bytes 1032200 | tf_op jit(solution)/shard_map/ppermute | solution.py:496
  117.2 23.5 %collective-permute-start.13 = (bf16[128,1344]{1,0:T(8,128)(2,1)S(1)}, bf16[128,1344]{1,0:T(8,128)(2,1)S(1)}, u32[]{:S(2)}, u32[]{:S(2)}) collective-permute-start(bf16[128,1344]{1,0:T(8,128)(2,1)S(1)} %get-tuple-element.86), channel_id=1, source_target_pairs={{0,8},{4,12},{8,0},{12,4},{16,24},{20,28},{24,16},{28,20},{1,9},{5... | collective-permute-start | bytes 1032200 | tf_op jit(solution)/shard_map/ppermute | solution.py:496
  140.8 4.4 %copy-start.1 = (bf16[1024,1024]{1,0:T(8,128)(2,1)S(1)}, bf16[1024,1024]{1,0:T(8,128)(2,1)}, u32[]{:S(2)}) copy-start(bf16[1024,1024]{1,0:T(8,128)(2,1)} %copy-done) | copy-start | bytes 6291460
  143.6 14.7 %collective-permute-start.14 = (bf16[2,2,512,128]{3,2,1,0:T(8,128)(2,1)}, bf16[2,2,512,128]{3,2,1,0:T(8,128)(2,1)S(1)}, u32[]{:S(2)}, u32[]{:S(2)}) collective-permute-start(bf16[2,2,512,128]{3,2,1,0:T(8,128)(2,1)} %get-tuple-element.101), channel_id=1, source_target_pairs={{8,0},{12,4},{16,8},{20,12},{24,16},{28,20},{9,1},{13,5},{17,9},{2... | collective-permute-start | bytes 1572872 | tf_op jit(solution)/shard_map/ppermute | solution.py:411
  157.2 4.6 %copy-start.13 = (bf16[128,1344]{1,0:T(8,128)(2,1)S(1)}, bf16[128,1344]{1,0:T(8,128)(2,1)}, u32[]{:S(2)}) copy-start(bf16[128,1344]{1,0:T(8,128)(2,1)} %copy-done.12) | copy-start | bytes 1032196
  157.2 15.9 %copy-start.9 = (bf16[128,1344]{1,0:T(8,128)(2,1)S(1)}, bf16[128,1344]{1,0:T(8,128)(2,1)}, u32[]{:S(2)}) copy-start(bf16[128,1344]{1,0:T(8,128)(2,1)} %copy-done.8) | copy-start | bytes 1032196
  158.4 24.8 %collective-permute-start.15 = (bf16[512,512]{1,0:T(8,128)(2,1)S(1)}, bf16[512,512]{1,0:T(8,128)(2,1)S(1)}, u32[]{:S(2)}, u32[]{:S(2)}) collective-permute-start(bf16[512,512]{1,0:T(8,128)(2,1)S(1)} %broadcast_select_fusion.4), channel_id=1, source_target_pairs={{0,4},{4,0},{8,12},{12,8},{16,20},{20,16},{24,28},{28,24},{1,5},{5... | collective-permute-start | bytes 1572872 | tf_op jit(solution)/shard_map/ppermute | solution.py:416
  158.5 11.6 %collective-permute-start.18 = (bf16[128,1344]{1,0:T(8,128)(2,1)S(1)}, bf16[128,1344]{1,0:T(8,128)(2,1)S(1)}, u32[]{:S(2)}, u32[]{:S(2)}) collective-permute-start(bf16[128,1344]{1,0:T(8,128)(2,1)S(1)} %copy-done.15), channel_id=1, source_target_pairs={{0,16},{4,20},{8,24},{12,28},{16,0},{20,4},{24,8},{28,12},{1,17},{... | collective-permute-start | bytes 1032200 | tf_op jit(solution)/shard_map/ppermute | solution.py:496
  161.8 11.4 %collective-permute-start.19 = (bf16[128,1344]{1,0:T(8,128)(2,1)S(1)}, bf16[128,1344]{1,0:T(8,128)(2,1)S(1)}, u32[]{:S(2)}, u32[]{:S(2)}) collective-permute-start(bf16[128,1344]{1,0:T(8,128)(2,1)S(1)} %copy-done.13), channel_id=1, source_target_pairs={{0,8},{4,12},{8,0},{12,4},{16,24},{20,28},{24,16},{28,20},{1,9},{5... | collective-permute-start | bytes 1032200 | tf_op jit(solution)/shard_map/ppermute | solution.py:496
  162.4 16.4 %collective-permute-start.16 = (bf16[2,1,512,128]{3,2,1,0:T(8,128)(2,1)S(1)}, bf16[2,1,512,128]{3,2,1,0:T(8,128)(2,1)S(1)}, u32[]{:S(2)}, u32[]{:S(2)}) collective-permute-start(bf16[2,1,512,128]{3,2,1,0:T(8,128)(2,1)S(1)} %get-tuple-element.106), channel_id=1, source_target_pairs={{8,0},{12,4},{16,8},{20,12},{24,16},{28,20},{9,1},{13,5},{17,9},{2... | collective-permute-start | bytes 786440 | tf_op jit(solution)/shard_map/ppermute | solution.py:411
  163.7 19.1 %collective-permute-start.17 = (bf16[2,1,512,128]{3,2,1,0:T(8,128)(2,1)S(1)}, bf16[2,1,512,128]{3,2,1,0:T(8,128)(2,1)S(1)}, u32[]{:S(2)}, u32[]{:S(2)}) collective-permute-start(bf16[2,1,512,128]{3,2,1,0:T(8,128)(2,1)S(1)} %get-tuple-element.107), channel_id=1, source_target_pairs={{8,0},{12,4},{16,8},{20,12},{24,16},{28,20},{9,1},{13,5},{17,9},{2... | collective-permute-start | bytes 786440 | tf_op jit(solution)/shard_map/ppermute | solution.py:411
  183.0 2.0 %collective-permute-start.20 = (bf16[2,2,512,128]{3,2,1,0:T(8,128)(2,1)S(1)}, bf16[2,2,512,128]{3,2,1,0:T(8,128)(2,1)S(1)}, u32[]{:S(2)}, u32[]{:S(2)}) collective-permute-start(bf16[2,2,512,128]{3,2,1,0:T(8,128)(2,1)S(1)} %get-tuple-element.118), channel_id=1, source_target_pairs={{0,4},{4,0},{8,12},{12,8},{16,20},{20,16},{24,28},{28,24},{1,5},{5... | collective-permute-start | bytes 1572872 | tf_op jit(solution)/shard_map/ppermute | solution.py:416
  (10 other events, 14.5 us)
